TPU v7x, 32 devices: a whole 2x2x4 slice. The times are simulated.
32 devices in a mesh: row: 8 (over z, y), col: 4 (over x, core).
Axes of the slice: x: 2, y: 2, z: 4, core: 2. Of those that a mesh axis runs over, the one named last changes fastest.
Arguments:
- tokens: bfloat16 [2, 8192, 2048], P(None, ('row', 'col')), may hold values from -6 to 6
- cotangent: bfloat16 [2, 8192, 2048], P(None, ('row', 'col')), may hold values from -6 to 6
- segment_of: int32 [2, 8192], P(None, 'row'), may hold values from 0 to 12, as said below
- leaf_parent: int32 [2, 64], P(None, 'row'), may hold values from 0 to 3
- w_qkv: float32 [2048, 8, 384], P('row', 'col'), may hold values from -0.4375 to 0.4375
- mom_qkv: float32 [2, 2048, 8, 384], P(None, 'row', 'col'), as said below
- w_out: float32 [2048, 2048], P('col', 'row'), may hold values from -0.5 to 0.5
- mom_out: float32 [2, 2048, 2048], P(None, 'col', 'row'), as said below
- w_gu: float32 [2, 2048, 8192], P(None, 'row', 'col'), may hold values from -0.125 to 0.125
- mom_gu: float32 [2, 2, 2048, 8192], P(None, None, 'row', 'col'), as said below
- w_down: float32 [8192, 2048], P('col', 'row')
- mom_down: float32 [2, 8192, 2048], P(None, 'col', 'row'), as said below
- gains: float32 [2, 2048], replicated, may hold values from 0.25 to 3, as said below
- mom_gains: float32 [2, 2, 2048], replicated, as said below
Outputs:
- mixed: bfloat16 [2, 8192, 2048], P(None, ('row', 'col'))
- d_tokens: float32 [2, 8192, 2048], P(None, ('row', 'col'))
- grad_norm: float32 [], replicated
- new_qkv: float32 [2048, 8, 384], P('row', 'col')
- moments_qkv: float32 [2, 2048, 8, 384], P(None, 'row', 'col')
- copy_qkv: bfloat16 [2048, 8, 384], P('row', 'col')
- new_out: float32 [2048, 2048], P('col', 'row')
- moments_out: float32 [2, 2048, 2048], P(None, 'col', 'row')
- copy_out: bfloat16 [2048, 2048], P('col', 'row')
- new_gu: float32 [2, 2048, 8192], P(None, 'row', 'col')
- moments_gu: float32 [2, 2, 2048, 8192], P(None, None, 'row', 'col')
- copy_gu: bfloat16 [2, 2048, 8192], P(None, 'row', 'col')
- new_down: float32 [8192, 2048], P('col', 'row')
- moments_down: float32 [2, 8192, 2048], P(None, 'col', 'row')
- copy_down: bfloat16 [8192, 2048], P('col', 'row')
- new_gains: float32 [2, 2048], replicated
- moments_gains: float32 [2, 2, 2048], replicated
Inputs may be any that keep to these rules, and one draw needn't show every extreme that they name: `segment_of`: in each tree (1024 tokens of one micro-batch that one index of row holds) the segments stand as runs in order: the trunk (0) of 256 tokens, branches 1 to 4, leaves 4 + 1 to 12. A branch holds 32 to 96 tokens, branches 1 and 2, and 3 and 4, 128 together; a leaf 64 // 2 to 96, consecutive pairs of leaves 2 * 64 together. `gains`: positive. `mom_qkv`: the second member of the first dimension is positive. `mom_out`: the second member of the first dimension is positive. `mom_gu`: the second member of the first dimension is positive. `mom_down`: the second member of the first dimension is positive. `mom_gains`: the second member of the first dimension is positive.
All inputs are finite; a program needn't handle non-finite values.
Results may differ from a plain program's by a relative error of at most 0.025.
Values may be sent and summed in bfloat16 or wider, within the bound.
A program may use at most 272 MiB of HBM per device.

v0:
```python
import math

import jax
import jax.numpy as jnp
from jax import lax
from jax.sharding import PartitionSpec as P

D = 2048
FF = 8192
HD = 64
KVH = 8
GROUP = 4
NBRANCH = 4
NLEAF = 8
STEP = 7


norm_eps = 1e-05
residual_mult = 0.22
score_mult = 0.015625
rope_theta = 10000000.0
beta_one = 0.5
beta_two = 0.55
adam_eps = 1e-08
weight_decay = 0.1
masked_value = -1e30


def param_count():
    return D * KVH * (GROUP + 2) * HD + KVH * GROUP * HD * D + 3 * D * FF + 2 * D


def clip_bound():
    return math.sqrt(param_count())


def step_rates():
    return (
        max(D // 12, 1) ** (-0.5),
        max(D // 16, 1) ** (-0.5),
        D ** (-0.5),
        max(FF // 64, 1) ** (-0.5),
        0.3,
    )


def tree_tables(segments, parents):
    seg_count = 1 + NBRANCH + NLEAF
    seg_ids = jnp.arange(seg_count, dtype=jnp.int32)
    member = (segments[:, None] == seg_ids[None, :]).astype(jnp.int32)
    seg_lengths = jnp.sum(member, axis=0)
    seg_starts = jnp.cumsum(seg_lengths) - seg_lengths
    branch_ids = jnp.arange(NBRANCH, dtype=jnp.int32)
    parent_pick = (parents[:, None] == branch_ids[None, :]).astype(jnp.int32)
    parent_len = jnp.sum(parent_pick * seg_lengths[1 : 1 + NBRANCH][None, :], axis=1)
    trunk_len = seg_lengths[0]
    base_depth = jnp.concatenate(
        [
            jnp.zeros((1,), jnp.int32),
            trunk_len * jnp.ones((NBRANCH,), jnp.int32),
            trunk_len + parent_len,
        ]
    )
    places = jnp.arange(segments.shape[0], dtype=jnp.int32)
    depth = places + jnp.sum(member * (base_depth - seg_starts)[None, :], axis=1)
    identity = (seg_ids[:, None] == seg_ids[None, :]).astype(jnp.int32)
    rooted = jnp.broadcast_to((seg_ids[None, :] == 0).astype(jnp.int32), (seg_count, seg_count))
    leaf_links = jnp.concatenate(
        [jnp.zeros((NLEAF, 1), jnp.int32), parent_pick, jnp.zeros((NLEAF, NLEAF), jnp.int32)],
        axis=1,
    )
    leaf_links = jnp.concatenate(
        [jnp.zeros((1 + NBRANCH, seg_count), jnp.int32), leaf_links], axis=0
    )
    ancestry = jnp.minimum(identity + rooted + leaf_links, 1)
    token_path = jnp.dot(member, ancestry)
    allowed = (jnp.dot(token_path, member.T) > 0) & (depth[None, :] <= depth[:, None])
    freqs = jnp.exp(jnp.arange(HD // 2, dtype=jnp.float32) * (-2.0 * math.log(rope_theta) / HD))
    angles = depth.astype(jnp.float32)[:, None] * freqs[None, :]
    return (allowed, jnp.cos(angles), jnp.sin(angles))


def rotate(vectors, cosines, sines):
    half_width = vectors.shape[-1] // 2
    first_half = vectors[..., :half_width]
    second_half = vectors[..., half_width:]
    return jnp.concatenate(
        [first_half * cosines - second_half * sines, second_half * cosines + first_half * sines],
        axis=-1,
    )


def normalize(values, gain):
    scaling = lax.rsqrt(jnp.mean(values * values, axis=-1, keepdims=True) + norm_eps)
    return (values * scaling * gain, scaling)


def norm_back(values, scaling, gain, upstream):
    scaled = upstream * gain
    gain_grad = jnp.sum(upstream * values * scaling, axis=0)
    inner = jnp.mean(scaled * values, axis=-1, keepdims=True)
    return (scaling * scaled - values * scaling * scaling * scaling * inner, gain_grad)


def gather_forward(values):
    return lax.all_gather(values, "col", axis=0, tiled=True)


def gather_backward(values):
    return lax.all_gather(values, "col", axis=0, tiled=True)


def sum_forward(term_fn, row_count):
    return lax.psum_scatter(
        term_fn(jnp.int32(0), lax.axis_size("col") * row_count).astype(jnp.bfloat16),
        "col",
        scatter_dimension=0,
        tiled=True,
    ).astype(jnp.float32)


def sum_backward(term_fn, row_count):
    return lax.psum_scatter(
        term_fn(jnp.int32(0), lax.axis_size("col") * row_count).astype(jnp.bfloat16),
        "col",
        scatter_dimension=0,
        tiled=True,
    ).astype(jnp.float32)


def adamw(master, moments, raw_grad, factor, step_rate):
    clipped = factor * raw_grad
    first_moment = beta_one * moments[0] + (1.0 - beta_one) * clipped
    second_moment = beta_two * moments[1] + (1.0 - beta_two) * clipped * clipped
    first_hat = first_moment / (1.0 - beta_one**STEP)
    second_hat = second_moment / (1.0 - beta_two**STEP)
    updated = master - step_rate * (
        first_hat / (jnp.sqrt(second_hat) + adam_eps) + weight_decay * master
    )
    return (updated, jnp.stack([first_moment, second_moment]))


def local(
    tokens,
    cotangent,
    segment_of,
    leaf_parent,
    w_qkv,
    mom_qkv,
    w_out,
    mom_out,
    w_gu,
    mom_gu,
    w_down,
    mom_down,
    gains,
    mom_gains,
):
    low_shards = (
        w_qkv.astype(jnp.bfloat16),
        w_out.astype(jnp.bfloat16),
        w_gu.astype(jnp.bfloat16),
        w_down.astype(jnp.bfloat16),
    )

    def fetch():
        return (
            lax.all_gather(low_shards[0], "row", axis=0, tiled=True),
            lax.all_gather(low_shards[1], "row", axis=1, tiled=True),
            lax.all_gather(low_shards[2], "row", axis=1, tiled=True),
            lax.all_gather(low_shards[3], "row", axis=1, tiled=True),
        )

    outputs = []
    input_grads = []
    owned = None
    unsummed = None
    gain_partial = None
    for batch_index in range(tokens.shape[0]):
        x_local = tokens[batch_index].astype(jnp.float32)
        row_count = x_local.shape[0]
        allowed, cosines, sines = tree_tables(segment_of[batch_index], leaf_parent[batch_index])
        w_a, w_b, w_c, w_d = fetch()
        normed_a, scale_a = normalize(x_local, gains[0])
        attn_in = gather_forward(normed_a.astype(jnp.bfloat16))
        projected = jnp.einsum("td,dkf->tkf", attn_in, w_a, preferred_element_type=jnp.float32)
        tree_len = projected.shape[0]
        groups = projected.shape[1]
        queries = rotate(
            projected[:, :, : GROUP * HD].reshape(tree_len, groups, GROUP, HD),
            cosines[:, None, None, :],
            sines[:, None, None, :],
        ).astype(jnp.bfloat16)
        key_heads = rotate(
            projected[:, :, GROUP * HD : (GROUP + 1) * HD], cosines[:, None, :], sines[:, None, :]
        ).astype(jnp.bfloat16)
        values = projected[:, :, (GROUP + 1) * HD :].astype(jnp.bfloat16)
        scores = jnp.einsum(
            "tkgh,skh->kgts", queries, key_heads, preferred_element_type=jnp.float32
        )
        logits = jnp.where(allowed, score_mult * scores, masked_value)
        row_peak = jnp.max(logits, axis=-1, keepdims=True)
        exp_terms = jnp.exp(logits - row_peak)
        exp_total = jnp.sum(exp_terms, axis=-1, keepdims=True)
        log_total = row_peak + jnp.log(exp_total)
        attn_probs = exp_terms / exp_total
        mixed_heads = (
            jnp.einsum(
                "kgts,skh->tkgh",
                attn_probs.astype(jnp.bfloat16),
                values,
                preferred_element_type=jnp.float32,
            )
            .astype(jnp.bfloat16)
            .reshape(tree_len, -1)
        )

        def out_terms(first_row, row_total):
            return jnp.dot(mixed_heads, w_b, preferred_element_type=jnp.float32)

        attn_sum = sum_forward(out_terms, row_count)
        residual_mid = x_local + residual_mult * attn_sum
        normed_b, scale_b = normalize(residual_mid, gains[1])
        ffn_in = gather_forward(normed_b.astype(jnp.bfloat16))
        gate_up = jnp.einsum("td,edf->tef", ffn_in, w_c, preferred_element_type=jnp.float32)
        gate_act = jax.nn.sigmoid(gate_up[:, 0])
        silu_gate = gate_up[:, 0] * gate_act
        hidden = (silu_gate * gate_up[:, 1]).astype(jnp.bfloat16)

        def down_terms(first_row, row_total):
            return jnp.dot(hidden, w_d, preferred_element_type=jnp.float32)

        mlp_sum = sum_forward(down_terms, row_count)
        outputs.append((residual_mid + residual_mult * mlp_sum).astype(jnp.bfloat16))
        w_a, w_b, w_c, w_d = fetch()
        cot_full = gather_backward(cotangent[batch_index])
        hidden_grad = residual_mult * jnp.einsum(
            "td,fd->tf", cot_full, w_d, preferred_element_type=jnp.float32
        )
        down_grad = residual_mult * jnp.einsum(
            "tf,td->fd", hidden, cot_full, preferred_element_type=jnp.float32
        )
        gate_grad = (
            hidden_grad * gate_up[:, 1] * gate_act * (1.0 + gate_up[:, 0] * (1.0 - gate_act))
        )
        up_grad = hidden_grad * silu_gate
        gate_up_grad = jnp.stack([gate_grad, up_grad], axis=1).astype(jnp.bfloat16)
        gu_grad = jnp.einsum(
            "td,tef->edf", ffn_in, gate_up_grad, preferred_element_type=jnp.float32
        )

        def ffn_back_terms(first_row, row_total):
            return jnp.einsum("tef,edf->td", gate_up_grad, w_c, preferred_element_type=jnp.float32)

        ffn_in_grad = sum_backward(ffn_back_terms, row_count)
        mid_norm_grad, gain_b_grad = norm_back(residual_mid, scale_b, gains[1], ffn_in_grad)
        mid_grad = cotangent[batch_index].astype(jnp.float32) + mid_norm_grad
        attn_out_grad = gather_backward((residual_mult * mid_grad).astype(jnp.bfloat16))
        out_grad = jnp.einsum(
            "tf,td->fd", mixed_heads, attn_out_grad, preferred_element_type=jnp.float32
        )
        heads_grad = (
            jnp.einsum("td,fd->tf", attn_out_grad, w_b, preferred_element_type=jnp.float32)
            .astype(jnp.bfloat16)
            .reshape(tree_len, groups, GROUP, HD)
        )
        attn_probs = jnp.exp(logits - log_total)
        prob_grad = jnp.einsum(
            "tkgh,skh->kgts", heads_grad, values, preferred_element_type=jnp.float32
        )
        row_inner = jnp.sum(prob_grad * attn_probs, axis=-1, keepdims=True)
        score_grad = (score_mult * attn_probs * (prob_grad - row_inner)).astype(jnp.bfloat16)
        query_grad = jnp.einsum(
            "kgts,skh->tkgh", score_grad, key_heads, preferred_element_type=jnp.float32
        )
        key_grad = jnp.einsum(
            "kgts,tkgh->skh", score_grad, queries, preferred_element_type=jnp.float32
        )
        value_grad = jnp.einsum(
            "kgts,tkgh->skh",
            attn_probs.astype(jnp.bfloat16),
            heads_grad,
            preferred_element_type=jnp.float32,
        )
        query_grad = rotate(query_grad, cosines[:, None, None, :], -sines[:, None, None, :])
        key_grad = rotate(key_grad, cosines[:, None, :], -sines[:, None, :])
        proj_grad = jnp.concatenate(
            [query_grad.reshape(tree_len, groups, GROUP * HD), key_grad, value_grad], axis=-1
        ).astype(jnp.bfloat16)
        qkv_grad = jnp.einsum("td,tkf->dkf", attn_in, proj_grad, preferred_element_type=jnp.float32)

        def attn_back_terms(first_row, row_total):
            return jnp.einsum("tkf,dkf->td", proj_grad, w_a, preferred_element_type=jnp.float32)

        attn_in_grad = sum_backward(attn_back_terms, row_count)
        input_norm_grad, gain_a_grad = norm_back(x_local, scale_a, gains[0], attn_in_grad)
        input_grads.append(mid_grad + input_norm_grad)
        gain_step = jnp.stack([gain_a_grad, gain_b_grad])
        gain_partial = gain_step if gain_partial is None else gain_partial + gain_step
        partials = (qkv_grad, out_grad, gu_grad, down_grad)
        unsummed = (
            partials
            if unsummed is None
            else tuple((running + addend for running, addend in zip(unsummed, partials)))
        )
    owned = (
        lax.psum_scatter(
            unsummed[0].astype(jnp.bfloat16), "row", scatter_dimension=0, tiled=True
        ).astype(jnp.float32),
        lax.psum_scatter(
            unsummed[1].astype(jnp.bfloat16), "row", scatter_dimension=1, tiled=True
        ).astype(jnp.float32),
        lax.psum_scatter(
            unsummed[2].astype(jnp.bfloat16), "row", scatter_dimension=1, tiled=True
        ).astype(jnp.float32),
        lax.psum_scatter(
            unsummed[3].astype(jnp.bfloat16), "row", scatter_dimension=1, tiled=True
        ).astype(jnp.float32),
    )
    local_squares = jnp.float32(0.0)
    for grad_piece in owned:
        local_squares = local_squares + jnp.sum(grad_piece * grad_piece)
    total_squares, gain_total = lax.psum((local_squares, gain_partial), ("row", "col"))
    grad_norm = jnp.sqrt(total_squares + jnp.sum(gain_total * gain_total))
    factor = jnp.minimum(1.0, clip_bound() / (grad_norm + 1e-06))
    rates = step_rates()
    masters = (w_qkv, w_out, w_gu, w_down)
    states = (mom_qkv, mom_out, mom_gu, mom_down)
    results = []
    for index_w in range(4):
        updated, moments = adamw(
            masters[index_w], states[index_w], owned[index_w], factor, rates[index_w]
        )
        results.append((updated, moments, updated.astype(jnp.bfloat16)))
    new_gains, moments_gains = adamw(gains, mom_gains, gain_total, factor, rates[4])
    mixed = jnp.stack(outputs, axis=0)
    d_tokens = jnp.stack(input_grads, axis=0)
    return (
        mixed,
        d_tokens,
        grad_norm,
        results[0][0],
        results[0][1],
        results[0][2],
        results[1][0],
        results[1][1],
        results[1][2],
        results[2][0],
        results[2][1],
        results[2][2],
        results[3][0],
        results[3][1],
        results[3][2],
        new_gains,
        moments_gains,
    )


def solution(mesh):
    placed = (
        P(None, ("row", "col"), None),
        P(None, ("row", "col"), None),
        P(None, "row"),
        P(None, "row"),
        P("row", "col", None),
        P(None, "row", "col", None),
        P("col", "row"),
        P(None, "col", "row"),
        P(None, "row", "col"),
        P(None, None, "row", "col"),
        P("col", "row"),
        P(None, "col", "row"),
        P(),
        P(),
    )
    return jax.shard_map(
        local,
        mesh=mesh,
        in_specs=placed,
        out_specs=(
            P(None, ("row", "col"), None),
            P(None, ("row", "col"), None),
            P(),
            P("row", "col", None),
            P(None, "row", "col", None),
            P("row", "col", None),
            P("col", "row"),
            P(None, "col", "row"),
            P("col", "row"),
            P(None, "row", "col"),
            P(None, None, "row", "col"),
            P(None, "row", "col"),
            P("col", "row"),
            P(None, "col", "row"),
            P("col", "row"),
            P(),
            P(),
        ),
        check_vma=False,
    )
```

profile of v0, /device:TPU:0, one launch (start us, length us, event | category | flops | bytes accessed | tf_op | source)
XLA Modules:
  0.0 1862.2 jit_solution(6387353850068432509)
XLA Ops:
  33.6 42.9 %all-gather.17.cloned.1.call-done = bf16[2048,2,384]{0,2,1:T(8,128)(2,1)} async-done(((bf16[256,2,384]{0,2,1:T(8,128)(2,1)}), bf16[2048,2,384]{0,2,1:T(8,128)(2,1)}) %all-gather.17.cloned.1.call-update) | async-done | bytes 3145744 | tf_op jit(solution)/shard_map/all_gather | solution.py:168
  76.5 34.8 %all-gather.27.cloned.1.call-done = bf16[1024,2048]{1,0:T(8,128)(2,1)} async-done(((bf16[256,2048]{1,0:T(8,128)(2,1)}), bf16[1024,2048]{1,0:T(8,128)(2,1)}) %all-gather.27.cloned.1.call-update) | async-done | bytes 4194320 | tf_op jit(solution)/shard_map/all_gather | solution.py:106
  145.2 26.8 %fusion.98 = bf16[2,64,4,1024]{3,1,2,0:T(8,128)(2,1)S(1)} fusion(f32[2,4,1024,1024]{2,3,1,0:T(8,128)} %get-tuple-element.153, f32[2,4,1024]{2,1,0:T(4,128)S(1)} %fusion.7, f32[2,4,1024]{2,1,0:T(4,128)S(1)} %get-tuple-element.152, f32[1024,2,384]{0,2,1:T(8,128)S(1)} %fusion.41), kind=kOutput, calls=%fused_computation.179 | convolution fusion | flops 1099431936 | bytes 34930688 | tf_op jit(solution)/shard_map/kgts,skh->tkgh/dot_general | solution.py:208
  178.7 21.1 %all-gather.15.cloned.1.call-done = bf16[1024,2048]{1,0:T(8,128)(2,1)} async-done(((bf16[256,2048]{1,0:T(8,128)(2,1)}), bf16[1024,2048]{1,0:T(8,128)(2,1)}) %all-gather.15.cloned.1.call-update) | async-done | bytes 4194320 | tf_op jit(solution)/shard_map/all_gather | solution.py:106
  206.6 15.5 fusion.205
  254.9 44.6 %reduce-scatter.13.cloned.1.call-done = bf16[256,2048]{1,0:T(8,128)(2,1)} async-done(((bf16[1024,2048]{1,0:T(8,128)(2,1)}), bf16[256,2048]{1,0:T(8,128)(2,1)}) %reduce-scatter.13.cloned.1.call-update) | async-done | bytes 1048592 | tf_op jit(solution)/shard_map/reduce_scatter | solution.py:114
  314.9 24.4 %all-gather.29.cloned.1.call-done = bf16[1024,2048]{1,0:T(8,128)(2,1)} async-done(((bf16[256,2048]{1,0:T(8,128)(2,1)}), bf16[1024,2048]{1,0:T(8,128)(2,1)}) %all-gather.29.cloned.1.call-update) | async-done | bytes 4194320 | tf_op jit(solution)/shard_map/all_gather | solution.py:106
  339.3 230.4 %all-gather.23.cloned.1.call-done = bf16[2,2048,2048]{2,1,0:T(8,128)(2,1)} async-done(((bf16[2,256,2048]{2,1,0:T(8,128)(2,1)}), bf16[2,2048,2048]{2,1,0:T(8,128)(2,1)}) %all-gather.23.cloned.1.call-update) | async-done | bytes 16777232 | tf_op jit(solution)/shard_map/all_gather | solution.py:170
  569.6 23.5 %fusion.37 = f32[1024,2,2048]{2,0,1:T(8,128)} fusion(bf16[2,2048,2048]{2,1,0:T(8,128)(2,1)} %all-gather.23.cloned.1.call-done, bf16[1024,2048]{1,0:T(8,128)(2,1)} %all-gather.29.cloned.1.call-done), kind=kOutput, calls=%fused_computation.74 | convolution fusion | flops 17179869184 | bytes 37748736 | tf_op jit(solution)/shard_map/td,edf->tef/dot_general | solution.py:225
  604.5 127.9 %all-gather.25.cloned.1.call-done = bf16[2048,2048]{1,0:T(8,128)(2,1)} async-done(((bf16[2048,256]{1,0:T(8,128)(2,1)}), bf16[2048,2048]{1,0:T(8,128)(2,1)}) %all-gather.25.cloned.1.call-update) | async-done | bytes 8388624 | tf_op jit(solution)/shard_map/all_gather | solution.py:171
  732.4 22.3 %fusion.51 = (bf16[1024,1,2048]{2,0,1:T(8,128)(2,1)}, bf16[1024,1,2048]{2,0,1:T(8,128)(2,1)}, bf16[1024,2048]{1,0:T(8,128)(2,1)}) fusion(f32[1024,2,2048]{2,0,1:T(8,128)} %fusion.37, bf16[2048,2048]{1,0:T(8,128)(2,1)} %all-gather.25.cloned.1.call-done, bf16[1,1024,2048]{2,1,0:T(8,128)(2,1)} %all-gather.37.cloned.1.call-done), kind=kOutput, calls=%fused_computation.103 | convolution fusion | flops 8623489024 | bytes 41943040 | tf_op jit(solution)/shard_map/td,fd->tf/dot_general | solution.py:237
  754.7 23.9 %bitcast_convert_fusion.1 = bf16[1024,2048]{1,0:T(8,128)(2,1)} fusion(bf16[2,2048,2048]{2,1,0:T(8,128)(2,1)} %all-gather.23.cloned.1.call-done, bf16[1024,1,2048]{2,0,1:T(8,128)(2,1)} %get-tuple-element.78, bf16[1024,1,2048]{2,0,1:T(8,128)(2,1)} %get-tuple-element.77), kind=kOutput, calls=%fused_computation.39 | convolution fusion | flops 17186160640 | bytes 29360128 | tf_op jit(solution)/shard_map/tef,edf->td/dot_general | solution.py:253
  778.9 23.5 %fusion.44 = f32[1024,2,2048]{2,0,1:T(8,128)} fusion(bf16[2,2048,2048]{2,1,0:T(8,128)(2,1)} %all-gather.23.cloned.1.call-done, bf16[1024,2048]{1,0:T(8,128)(2,1)} %all-gather.21.cloned.1.call-done), kind=kOutput, calls=%fused_computation.86 | convolution fusion | flops 17179869184 | bytes 37748736 | tf_op jit(solution)/shard_map/td,edf->tef/dot_general | solution.py:225
  803.7 22.0 %fusion.50 = (bf16[1024,1,2048]{2,0,1:T(8,128)(2,1)}, bf16[1024,1,2048]{2,0,1:T(8,128)(2,1)}, bf16[1024,2048]{1,0:T(8,128)(2,1)}) fusion(f32[1024,2,2048]{2,0,1:T(8,128)} %fusion.44, bf16[2048,2048]{1,0:T(8,128)(2,1)} %all-gather.25.cloned.1.call-done, bf16[1,1024,2048]{2,1,0:T(8,128)(2,1)} %all-gather.35.cloned.1.call-done), kind=kOutput, calls=%fused_computation.102 | convolution fusion | flops 8623489024 | bytes 41943040 | tf_op jit(solution)/shard_map/td,fd->tf/dot_general | solution.py:237
  825.7 23.8 %bitcast_convert_fusion.3 = bf16[1024,2048]{1,0:T(8,128)(2,1)} fusion(bf16[2,2048,2048]{2,1,0:T(8,128)(2,1)} %all-gather.23.cloned.1.call-done, bf16[1024,1,2048]{2,0,1:T(8,128)(2,1)} %get-tuple-element.80, bf16[1024,1,2048]{2,0,1:T(8,128)(2,1)} %get-tuple-element.79), kind=kOutput, calls=%fused_computation.41 | convolution fusion | flops 17186160640 | bytes 29360128 | tf_op jit(solution)/shard_map/tef,edf->td/dot_general | solution.py:253
  863.9 34.6 %reduce-scatter.21.cloned.1.call-done = bf16[256,2048]{1,0:T(8,128)(2,1)} async-done(((bf16[1024,2048]{1,0:T(8,128)(2,1)}), bf16[256,2048]{1,0:T(8,128)(2,1)}) %reduce-scatter.21.cloned.1.call-update) | async-done | bytes 1048592 | tf_op jit(solution)/shard_map/reduce_scatter | solution.py:123
  902.7 42.7 %reduce-scatter.19.cloned.1.call-done = bf16[256,2048]{1,0:T(8,128)(2,1)} async-done(((bf16[1024,2048]{1,0:T(8,128)(2,1)}), bf16[256,2048]{1,0:T(8,128)(2,1)}) %reduce-scatter.19.cloned.1.call-update) | async-done | bytes 1048592 | tf_op jit(solution)/shard_map/reduce_scatter | solution.py:114
  952.0 15.3 fusion.32
  967.4 14.8 multiply_convert_fusion
  990.8 14.8 fusion.119
  1006.5 15.6 all-gather.31.cloned.1.call-done
  1042.4 22.4 %fusion.3 = (f32[2,4,1024]{2,1,0:T(4,128)S(1)}, f32[2,1024,1024,4]{2,1,3,0:T(8,128)}) fusion(f32[2,4,1024,1024]{2,3,1,0:T(8,128)} %get-tuple-element.151, f32[2,4,1024]{2,1,0:T(4,128)S(1)} %bitcast.437, bf16[1024,2,4,64]{0,3,2,1:T(8,128)(2,1)S(1)} %bitcast.428, f32[1024,2,384]{0,2,1:T(8,128)} %copy-done.22), kind=kOutput, calls=%fused_computation.7 | convolution fusion | flops 1098899456 | bytes 68485120 | tf_op jit(solution)/shard_map/tkgh,skh->kgts/dot_general | solution.py:268
  1064.8 29.4 %fusion.5 = bf16[2,4,1024,1024]{2,3,1,0:T(8,128)(2,1)} fusion(f32[2,1024,1024,4]{2,1,3,0:T(8,128)} %get-tuple-element.155, f32[2,4,1024,1024]{2,3,1,0:T(8,128)} %get-tuple-element.151, f32[2,4,1024]{2,1,0:T(4,128)S(1)} %get-tuple-element.154, f32[2,4,1024]{2,1,0:T(4,128)S(1)} %bitcast.438), kind=kLoop, calls=%fused_computation.9 | loop fusion | flops 41943040 | bytes 83951616 | tf_op jit(solution)/shard_map/convert_element_type | solution.py:272
  1126.8 22.7 %fusion = (f32[2,4,1024]{2,1,0:T(4,128)S(1)}, f32[2,1024,1024,4]{2,1,3,0:T(8,128)}) fusion(f32[2,4,1024,1024]{2,3,1,0:T(8,128)} %get-tuple-element.153, f32[2,4,1024]{2,1,0:T(4,128)S(1)} %bitcast.434, bf16[1024,2,4,64]{0,3,2,1:T(8,128)(2,1)S(1)} %bitcast.426, f32[1024,2,384]{0,2,1:T(8,128)} %copy-done.21), kind=kOutput, calls=%fused_computation.2 | convolution fusion | flops 1098899456 | bytes 68485120 | tf_op jit(solution)/shard_map/tkgh,skh->kgts/dot_general | solution.py:268
  1149.7 28.7 %fusion.2 = bf16[2,4,1024,1024]{2,3,1,0:T(8,128)(2,1)} fusion(f32[2,1024,1024,4]{2,1,3,0:T(8,128)} %get-tuple-element.157, f32[2,4,1024,1024]{2,3,1,0:T(8,128)} %get-tuple-element.153, f32[2,4,1024]{2,1,0:T(4,128)S(1)} %get-tuple-element.156, f32[2,4,1024]{2,1,0:T(4,128)S(1)} %bitcast.435), kind=kLoop, calls=%fused_computation.4 | loop fusion | flops 41943040 | bytes 83951616 | tf_op jit(solution)/shard_map/convert_element_type | solution.py:272
  1244.5 25.8 %fusion.22 = f32[2,2048,2048]{2,1,0:T(8,128)} fusion(bf16[1024,1,2048]{2,0,1:T(8,128)(2,1)} %get-tuple-element.80, bf16[1024,1,2048]{2,0,1:T(8,128)(2,1)} %get-tuple-element.79, bf16[1024,2048]{1,0:T(8,128)(2,1)} %all-gather.21.cloned.1.call-done), kind=kOutput, calls=%fused_computation.55 | convolution fusion | flops 17184063488 | bytes 46137344 | tf_op jit(solution)/shard_map/td,tef->edf/dot_general | solution.py:248
  1270.3 27.9 %fusion.14 = bf16[2,2048,2048]{1,2,0:T(8,128)(2,1)} fusion(f32[2,2048,2048]{2,1,0:T(8,128)} %fusion.22, bf16[1024,1,2048]{2,0,1:T(8,128)(2,1)} %get-tuple-element.78, bf16[1024,1,2048]{2,0,1:T(8,128)(2,1)} %get-tuple-element.77, bf16[1024,2048]{1,0:T(8,128)(2,1)} %all-gather.29.cloned.1.call-done), kind=kOutput, calls=%fused_computation.25 | convolution fusion | flops 17200840704 | bytes 62914560 | tf_op jit(solution)/shard_map/td,tef->edf/dot_general | solution.py:248
  1333.3 37.1 %reduce-scatter.23.cloned.1.call-done = bf16[256,2048]{1,0:T(8,128)(2,1)} async-done(((bf16[1024,2048]{1,0:T(8,128)(2,1)}), bf16[256,2048]{1,0:T(8,128)(2,1)}) %reduce-scatter.23.cloned.1.call-update) | async-done | bytes 1048592 | tf_op jit(solution)/shard_map/reduce_scatter | solution.py:123
  1370.4 47.2 %reduce-scatter.27.cloned.1.call-done = bf16[256,2048]{1,0:T(8,128)(2,1)} async-done(((bf16[1024,2048]{1,0:T(8,128)(2,1)}), bf16[256,2048]{1,0:T(8,128)(2,1)}) %reduce-scatter.27.cloned.1.call-update) | async-done | bytes 1048592 | tf_op jit(solution)/shard_map/reduce_scatter | solution.py:123
  1424.1 40.6 %reduce-scatter.15.cloned.1.call-done = bf16[256,2048]{1,0:T(8,128)(2,1)} async-done(((bf16[1024,2048]{1,0:T(8,128)(2,1)}), bf16[256,2048]{1,0:T(8,128)(2,1)}) %reduce-scatter.15.cloned.1.call-update) | async-done | bytes 1048592 | tf_op jit(solution)/shard_map/reduce_scatter | solution.py:114
  1471.7 279.9 %reduce-scatter.33.cloned.1.call-done = bf16[2,256,2048]{1,2,0:T(8,128)(2,1)} async-done(((bf16[2,2048,2048]{1,2,0:T(8,128)(2,1)}), bf16[2,256,2048]{1,2,0:T(8,128)(2,1)}) %reduce-scatter.33.cloned.1.call-update) | async-done | bytes 2097168 | tf_op jit(solution)/shard_map/reduce_scatter | solution.py:313
  1759.1 39.4 %all-reduce.2 = (f32[]{:T(128)}, f32[2,2048]{1,0:T(2,128)S(1)}) all-reduce(f32[]{:T(128)S(6)} %add.348, f32[2,2048]{1,0:T(2,128)S(1)} %maximum_add_fusion), channel_id=1, replica_groups=mesh['row'=8,'col'=4] {'row','col'}, use_global_device_ids=true, to_apply=%region_38.39 | all-reduce | flops 4097 | bytes 32776 | tf_op jit(solution)/shard_map/psum | solution.py:323
  (382 shorter events, 394.9 us)
Async XLA Ops:
  7.2 69.3 %all-gather.17.cloned.1.call-start = ((), (), s32[]{:S(2)}) async-start(), calls=%async_computation.13 | async-start | bytes 3538944 | tf_op jit(solution)/shard_map/all_gather | solution.py:168
  9.4 101.9 %all-gather.27.cloned.1.call-start = ((), (), s32[]{:S(2)}) async-start(), calls=%async_computation.20 | async-start | bytes 5242880 | tf_op jit(solution)/shard_map/all_gather | solution.py:106
  14.9 157.2 %all-gather.19.cloned.1.call-start = ((), (), s32[]{:S(2)}) async-start(), calls=%async_computation.14 | async-start | bytes 2359296 | tf_op jit(solution)/shard_map/all_gather | solution.py:169
  15.7 184.0 %all-gather.15.cloned.1.call-start = ((), (), s32[]{:S(2)}) async-start(), calls=%async_computation.12 | async-start | bytes 5242880 | tf_op jit(solution)/shard_map/all_gather | solution.py:106
  16.3 238.6 %reduce-scatter.17.cloned.1.call-start = ((), (), s32[]{:S(2)}) async-start(), calls=%async_computation.21 | async-start | bytes 5242880 | tf_op jit(solution)/shard_map/reduce_scatter | solution.py:114
  33.6 172.7 %copy-start.19 = (f32[1024,32]{0,1:T(8,128)}, f32[1024,32]{0,1:T(8,128)S(1)}, u32[]{:S(2)}) copy-start(f32[1024,32]{0,1:T(8,128)S(1)} %get-tuple-element.135) | copy-start | bytes 393220
  178.6 120.9 %reduce-scatter.13.cloned.1.call-start = ((), (), s32[]{:S(2)}) async-start(), calls=%async_computation.15 | async-start | bytes 5242880 | tf_op jit(solution)/shard_map/reduce_scatter | solution.py:114
  254.8 84.5 %all-gather.29.cloned.1.call-start = ((), (), s32[]{:S(2)}) async-start(), calls=%async_computation.22 | async-start | bytes 5242880 | tf_op jit(solution)/shard_map/all_gather | solution.py:106
  304.6 265.0 %all-gather.23.cloned.1.call-start = ((), (), s32[]{:S(2)}) async-start(), calls=%async_computation.17 | async-start | bytes 18874368 | tf_op jit(solution)/shard_map/all_gather | solution.py:170
  308.7 295.8 %all-gather.37.cloned.1.call-start = ((), (), s32[]{:S(2)}) async-start(), calls=%async_computation.35 | async-start | bytes 5242880 | tf_op jit(solution)/shard_map/all_gather | solution.py:110
  310.2 422.2 %all-gather.25.cloned.1.call-start = ((), (), s32[]{:S(2)}) async-start(), calls=%async_computation.18 | async-start | bytes 9437184 | tf_op jit(solution)/shard_map/all_gather | solution.py:171
  313.1 465.7 %all-gather.21.cloned.1.call-start = ((), (), s32[]{:S(2)}) async-start(), calls=%async_computation.16 | async-start | bytes 5242880 | tf_op jit(solution)/shard_map/all_gather | solution.py:106
  313.9 489.9 %all-gather.35.cloned.1.call-start = ((), (), s32[]{:S(2)}) async-start(), calls=%async_computation.34 | async-start | bytes 5242880 | tf_op jit(solution)/shard_map/all_gather | solution.py:110
  314.5 549.4 %reduce-scatter.25.cloned.1.call-start = ((), (), s32[]{:S(2)}) async-start(), calls=%async_computation.27 | async-start | bytes 5242880 | tf_op jit(solution)/shard_map/reduce_scatter | solution.py:123
  778.6 119.9 %reduce-scatter.21.cloned.1.call-start = ((), (), s32[]{:S(2)}) async-start(), calls=%async_computation.24 | async-start | bytes 5242880 | tf_op jit(solution)/shard_map/reduce_scatter | solution.py:123
  849.5 95.8 %reduce-scatter.19.cloned.1.call-start = ((), (), s32[]{:S(2)}) async-start(), calls=%async_computation.23 | async-start | bytes 5242880 | tf_op jit(solution)/shard_map/reduce_scatter | solution.py:114
  863.8 121.7 %all-gather.33.cloned.1.call-start = ((), (), s32[]{:S(2)}) async-start(), calls=%async_computation.28 | async-start | bytes 5242880 | tf_op jit(solution)/shard_map/all_gather | solution.py:110
  950.9 71.2 %all-gather.31.cloned.1.call-start = ((), (), s32[]{:S(2)}) async-start(), calls=%async_computation.25 | async-start | bytes 5242880 | tf_op jit(solution)/shard_map/all_gather | solution.py:110
  951.5 374.6 %reduce-scatter.35.cloned.1.call-start = ((), (), s32[]{:S(2)}) async-start(), calls=%async_computation.33 | async-start | bytes 9437184 | tf_op jit(solution)/shard_map/reduce_scatter | solution.py:316
  982.2 346.3 %reduce-scatter.31.cloned.1.call-start = ((), (), s32[]{:S(2)}) async-start(), calls=%async_computation.31 | async-start | bytes 2359296 | tf_op jit(solution)/shard_map/reduce_scatter | solution.py:310
  1149.6 180.5 %reduce-scatter.29.cloned.1.call-start = ((), (), s32[]{:S(2)}) async-start(), calls=%async_computation.30 | async-start | bytes 3538944 | tf_op jit(solution)/shard_map/reduce_scatter | solution.py:307
  1214.4 156.0 %reduce-scatter.23.cloned.1.call-start = ((), (), s32[]{:S(2)}) async-start(), calls=%async_computation.26 | async-start | bytes 5242880 | tf_op jit(solution)/shard_map/reduce_scatter | solution.py:123
  1222.0 195.7 %reduce-scatter.27.cloned.1.call-start = ((), (), s32[]{:S(2)}) async-start(), calls=%async_computation.29 | async-start | bytes 5242880 | tf_op jit(solution)/shard_map/reduce_scatter | solution.py:123
  1230.4 234.4 %reduce-scatter.15.cloned.1.call-start = ((), (), s32[]{:S(2)}) async-start(), calls=%async_computation.19 | async-start | bytes 5242880 | tf_op jit(solution)/shard_map/reduce_scatter | solution.py:114
  1244.5 507.1 %reduce-scatter.33.cloned.1.call-start = ((), (), s32[]{:S(2)}) async-start(), calls=%async_computation.32 | async-start | bytes 18874368 | tf_op jit(solution)/shard_map/reduce_scatter | solution.py:313
  1322.8 98.1 %copy-start.70 = (f32[2048]{0:T(1024)S(1)}, f32[2048]{0:T(1024)}, u32[]{:S(2)}) copy-start(f32[2048]{0:T(1024)} %get-tuple-element.53) | copy-start | bytes 24580
  1322.8 98.1 %copy-start.71 = (f32[2048]{0:T(1024)S(1)}, f32[2048]{0:T(1024)}, u32[]{:S(2)}) copy-start(f32[2048]{0:T(1024)} %get-tuple-element.62) | copy-start | bytes 24580
  1322.8 98.2 %copy-start.6 = (bf16[256,2048]{1,0:T(8,128)(2,1)S(1)}, bf16[256,2048]{1,0:T(8,128)(2,1)}, u32[]{:S(2)}) copy-start(bf16[256,2048]{1,0:T(8,128)(2,1)} %reduce-scatter.17.cloned.1.call-done) | copy-start | bytes 3145732
  1322.8 98.2 %copy-start.58 = (f32[1,2048]{1,0:T(1,128)S(1)}, f32[1,2048]{1,0:T(1,128)}, u32[]{:S(2)}) copy-start(f32[1,2048]{1,0:T(1,128)} %get-tuple-element.129) | copy-start | bytes 24580
  1322.8 98.2 %copy-start.78 = (f32[256]{0:T(256)S(1)}, f32[256]{0:T(256)}, u32[]{:S(2)}) copy-start(f32[256]{0:T(256)} %copy-done.76) | copy-start | bytes 3076
  1322.8 98.2 %copy-start.86 = (f32[256]{0:T(256)S(1)}, f32[256]{0:T(256)}, u32[]{:S(2)}) copy-start(f32[256]{0:T(256)} %copy-done.85) | copy-start | bytes 3076
  1469.4 286.9 %copy-start.16 = (bf16[1,256,2048]{2,1,0:T(8,128)(2,1)S(1)}, bf16[1,256,2048]{2,1,0:T(8,128)(2,1)}, u32[]{:S(2)}) copy-start(bf16[1,256,2048]{2,1,0:T(8,128)(2,1)} %get-tuple-element.97) | copy-start | bytes 3145732
  (89 other events, 1826.1 us)
Sparse Core Ops, SparseCore 0:
  10.7 65.7 all-gather.16
  78.6 32.6 all-gather.26
  113.9 51.0 all-gather.18
  167.0 32.6 all-gather.14
  202.7 44.4 reduce-scatter.16
  254.9 44.5 reduce-scatter.12
  304.7 34.4 all-gather.28
  342.0 227.5 all-gather.22
  571.8 32.6 all-gather.36
  606.9 125.3 all-gather.24
  734.5 32.6 all-gather.20
  769.2 34.4 all-gather.34
  806.3 44.4 reduce-scatter.24
  853.9 44.5 reduce-scatter.20
  900.8 44.4 reduce-scatter.18
  951.0 34.4 all-gather.32
  987.6 34.4 all-gather.30
  1026.6 149.3 reduce-scatter.34
  1180.1 67.3 reduce-scatter.30
  1250.9 73.2 reduce-scatter.28
  1326.7 43.6 reduce-scatter.22
  1373.1 44.5 reduce-scatter.26
  1420.2 44.5 reduce-scatter.14
  1468.9 282.6 reduce-scatter.32
where the time goes:
time: 1870 us; the launch traced here: 1860 us
  waiting for transfers between devices  1040 us (56%)
  matrix products  513 us (27%)
  other arithmetic  171 us (9%)
  local copies, waits for them, and re-layouts  73.1 us (4%)
  blocking collectives  39.4 us (2%)
  between operations  21.2 us (1%)
    reduce_scatter x1, waiting for transfers between devices, local(): lax.psum_scatter(unsummed[2].astype(jnp.bfloat16), 'row', scatter_dimensi...  280 us
    all_gather x1, waiting for transfers between devices, fetch(): lax.all_gather(low_shards[2], 'row', axis=1, tiled=True)  230 us
    reduce_scatter x4, waiting for transfers between devices, sum_forward(): lax.psum_scatter(term_fn(jnp.int32(0), lax.axis_size('col') * row_count)....  128 us
    all_gather x1, waiting for transfers between devices, fetch(): lax.all_gather(low_shards[3], 'row', axis=1, tiled=True)  128 us
    reduce_scatter x4, waiting for transfers between devices, sum_backward(): lax.psum_scatter(term_fn(jnp.int32(0), lax.axis_size('col') * row_count)....  119 us
    all_gather x4, waiting for transfers between devices, gather_forward(): return lax.all_gather(values, 'col', axis=0, tiled=True)  80.3 us
    convert_element_type x2, other arithmetic, local(): (score_mult * attn_probs * (prob_grad - row_inner)).astype(jnp.bfloat16)  58 us
    dot_general x2, matrix products, local(): jnp.einsum('td,tef->edf', ffn_in, gate_up_grad, preferred_element_type=jn...  53.6 us
  transfers between devices with their start and end apart: 24, of which 17 were waited for; matrix products, arithmetic and copies ran while one was open for 37% of the time, Pallas kernels for 0%

commit v1 on v0

--- a/solution.py
+++ b/solution.py
@@ -1,8 +1,11 @@
+import functools
 import math
 
 import jax
 import jax.numpy as jnp
 from jax import lax
+from jax.experimental import pallas as pl
+from jax.experimental.pallas import tpu as pltpu
 from jax.sharding import PartitionSpec as P
 
 D = 2048
@@ -356,6 +359,714 @@
     )
 
 
+def position_tables(segments, parents):
+    seg_ids = jnp.arange(1 + NBRANCH + NLEAF, dtype=jnp.int32)
+    member = (segments[:, None] == seg_ids[None, :]).astype(jnp.int32)
+    seg_lengths = jnp.sum(member, axis=0)
+    seg_starts = jnp.cumsum(seg_lengths) - seg_lengths
+    parent_of = jnp.concatenate([jnp.full((1 + NBRANCH,), -1, jnp.int32), 1 + parents])
+    branch_ids = jnp.arange(NBRANCH, dtype=jnp.int32)
+    parent_pick = (parents[:, None] == branch_ids[None, :]).astype(jnp.int32)
+    parent_len = jnp.sum(parent_pick * seg_lengths[1 : 1 + NBRANCH][None, :], axis=1)
+    base_depth = jnp.concatenate(
+        [
+            jnp.zeros((1,), jnp.int32),
+            seg_lengths[0] * jnp.ones((NBRANCH,), jnp.int32),
+            seg_lengths[0] + parent_len,
+        ]
+    )
+    places = jnp.arange(segments.shape[0], dtype=jnp.int32)
+    depth = places + jnp.sum(member * (base_depth - seg_starts)[None, :], axis=1)
+    parent = jnp.sum(member * parent_of[None, :], axis=1)
+    freqs = jnp.exp(jnp.arange(HD // 2, dtype=jnp.float32) * (-2.0 * math.log(rope_theta) / HD))
+    angles = depth.astype(jnp.float32)[:, None] * freqs[None, :]
+    cosines, sines = jnp.cos(angles), jnp.sin(angles)
+    return (
+        jnp.concatenate([cosines] * 4, axis=1),
+        jnp.concatenate([-sines, sines] * 2, axis=1),
+        jnp.broadcast_to(segments[:, None].astype(jnp.float32), (segments.shape[0], 128)),
+        jnp.broadcast_to(parent[:, None].astype(jnp.float32), (segments.shape[0], 128)),
+        jnp.broadcast_to(segments[None, :].astype(jnp.float32), (8, segments.shape[0])),
+    )
+
+def dot_nn(a, b):
+    return lax.dot_general(a, b, (((1,), (0,)), ((), ())), preferred_element_type=jnp.float32)
+
+
+def dot_nt(a, b):
+    return lax.dot_general(a, b, (((1,), (1,)), ((), ())), preferred_element_type=jnp.float32)
+
+
+def dot_tn(a, b):
+    return lax.dot_general(a, b, (((0,), (0,)), ((), ())), preferred_element_type=jnp.float32)
+
+
+MICRO = 2
+TREE = 1024
+OWN = 256
+WIDE = 2048
+NX, NC, NZ, NY = 2, 2, 4, 2
+SEG = 128
+MESH = pl.DeviceIdType.MESH
+HBM = pl.BlockSpec(memory_space=pl.ANY)
+
+
+class Place:
+    def __init__(self):
+        row, col = lax.axis_index("row"), lax.axis_index("col")
+        self.row, self.col = row, col
+        self.z, self.y = row // NY, row % NY
+        self.x, self.c = col // NC, col % NC
+        self.own = col
+        self.row_z = [lax.rem(row + NY * off, NZ * NY) for off in range(NZ)]
+        self.row_y = self.z * NY + (1 - self.y)
+        self.row_yz = [lax.rem(self.z + off, NZ) * NY + (1 - self.y) for off in range(NZ)]
+        self.col_x = (1 - self.x) * NC + self.c
+        self.col_c = self.x * NC + (1 - self.c)
+        self.col_xc = (1 - self.x) * NC + (1 - self.c)
+        self.at_z = [None] + [(self.row_z[off], col) for off in range(1, NZ)]
+        self.at_y = (self.row_y, col)
+        self.at_x = (row, self.col_x)
+        self.at_c = (row, self.col_c)
+
+    def greet(self):
+        barrier = pltpu.get_barrier_semaphore()
+        partners = self.at_z[1:] + [self.at_y, self.at_x, self.at_c]
+        for partner in partners:
+            pl.semaphore_signal(barrier, inc=1, device_id=partner, device_id_type=MESH)
+        pl.semaphore_wait(barrier, len(partners))
+
+
+class Copies:
+    def __init__(self):
+        self.open_sends = []
+
+    def send(self, src, dst, send_sem, recv_sem, device):
+        copy = pltpu.make_async_remote_copy(
+            src_ref=src, dst_ref=dst, send_sem=send_sem, recv_sem=recv_sem,
+            device_id=device, device_id_type=MESH,
+        )
+        copy.start()
+        self.open_sends.append(copy)
+        return copy
+
+    def arrive(self, dst, send_sem, recv_sem, device):
+        pltpu.make_async_remote_copy(
+            src_ref=dst, dst_ref=dst, send_sem=send_sem, recv_sem=recv_sem,
+            device_id=device, device_id_type=MESH,
+        ).wait_recv()
+
+    def local(self, src, dst, sem):
+        copy = pltpu.make_async_copy(src, dst, sem)
+        copy.start()
+        return copy
+
+    def close(self):
+        for copy in self.open_sends:
+            copy.wait_send()
+        self.open_sends = []
+
+
+def rows_of(index, size):
+    return pl.ds(pl.multiple_of(index * size, size), size)
+
+
+class WeightGather:
+    def __init__(self, place, copies, own, full, view, send, recv, keep):
+        self.place, self.copies, self.own, self.full, self.view = place, copies, own, full, view
+        self.send, self.recv, self.keep = send, recv, keep
+
+    def start(self):
+        p = self.place
+        here = self.view(self.full, p.row)
+        self.kept = self.copies.local(self.own, here, self.keep)
+        for off in (1, 3, 2):
+            self.copies.send(self.own, here, self.send.at[off - 1], self.recv.at[p.row], p.at_z[off])
+        self.copies.send(self.own, here, self.send.at[3], self.recv.at[p.row], p.at_y)
+
+    def relay(self):
+        p = self.place
+        for off in (1, 3, 2):
+            block = self.view(self.full, p.row_z[off])
+            self.copies.arrive(block, self.send.at[3 + off], self.recv.at[p.row_z[off]], p.at_y)
+            self.copies.send(block, block, self.send.at[3 + off], self.recv.at[p.row_z[off]], p.at_y)
+
+    def finish(self):
+        p = self.place
+        for off in range(NZ):
+            block = self.view(self.full, p.row_yz[off])
+            self.copies.arrive(block, self.send.at[3], self.recv.at[p.row_yz[off]], p.at_y)
+        self.kept.wait()
+
+
+class TokenGather:
+    def __init__(self, place, copies, full, base, send, recv):
+        self.place, self.copies, self.full, self.base = place, copies, full, base
+        self.send, self.recv = send, recv
+
+    def block(self, index):
+        return self.full.at[pl.ds(pl.multiple_of(self.base + index * OWN, OWN), OWN), :]
+
+    def start(self, own, keep):
+        p = self.place
+        here = self.block(p.own)
+        self.kept = self.copies.local(own, here, keep)
+        self.copies.send(own, here, self.send.at[0], self.recv.at[p.own], p.at_x)
+        self.copies.send(own, here, self.send.at[1], self.recv.at[p.own], p.at_c)
+
+    def relay(self):
+        p = self.place
+        block = self.block(p.col_x)
+        self.copies.arrive(block, self.send.at[2], self.recv.at[p.col_x], p.at_c)
+        self.copies.send(block, block, self.send.at[2], self.recv.at[p.col_x], p.at_c)
+
+    def finish(self):
+        p = self.place
+        for index in (p.col_c, p.col_xc):
+            self.copies.arrive(self.block(index), self.send.at[2], self.recv.at[index], p.at_c)
+        self.kept.wait()
+
+
+class TokenSum:
+    def __init__(self, place, copies, partial, from_core, from_x, send, recv):
+        self.place, self.copies, self.partial = place, copies, partial
+        self.from_core, self.from_x, self.send, self.recv = from_core, from_x, send, recv
+
+    def start(self):
+        p = self.place
+        self.sent = []
+        for there in range(NX):
+            self.sent.append(
+                self.copies.send(
+                    self.partial.at[there * NC + (1 - p.c)], self.from_core.at[there],
+                    self.send.at[there], self.recv.at[there], p.at_c,
+                )
+            )
+
+    def middle(self):
+        p = self.place
+        for there in range(NX):
+            self.copies.arrive(self.from_core.at[there], self.send.at[there], self.recv.at[there], p.at_c)
+        away = 1 - p.x
+
+        @pl.loop(0, OWN // 32)
+        def _(i):
+            rows = rows_of(i, 32)
+            self.partial[p.col_x, rows, :] = (
+                self.partial[p.col_x, rows, :].astype(jnp.float32)
+                + self.from_core[away, rows, :].astype(jnp.float32)
+            ).astype(jnp.bfloat16)
+
+        self.copies.send(self.partial.at[p.col_x], self.from_x, self.send.at[2], self.recv.at[2], p.at_x)
+
+    def arrive(self):
+        p = self.place
+        self.copies.arrive(self.from_x, self.send.at[2], self.recv.at[2], p.at_x)
+
+    def rows(self, rows):
+        p = self.place
+        return (
+            self.partial[p.own, rows, :].astype(jnp.float32)
+            + self.from_core[p.x, rows, :].astype(jnp.float32)
+            + self.from_x[rows, :].astype(jnp.float32)
+        )
+
+
+def swap_halves(tile):
+    lane = lax.broadcasted_iota(jnp.int32, tile.shape, 1)
+    return jnp.where(lane % HD < HD // 2, pltpu.roll(tile, 128 - HD // 2, 1), pltpu.roll(tile, HD // 2, 1))
+
+
+def key_value_tiles(kv):
+    wide = kv.astype(jnp.float32)
+    lane = lax.broadcasted_iota(jnp.int32, wide.shape, 1)
+    key_low = jnp.where(lane < HD, wide, 0.0)
+    value_high = jnp.where(lane < HD, 0.0, wide)
+    key_high = pltpu.roll(key_low, HD, 1)
+    value_low = pltpu.roll(value_high, HD, 1)
+    low = jnp.bfloat16
+    return (key_low.astype(low), key_high.astype(low)), (value_low.astype(low), value_high.astype(low))
+
+
+def masked_parts(run, seg_col, parent_col, seg_row):
+    rows = slice(run * SEG, (run + 1) * SEG)
+
+    def causal():
+        shape = (SEG, 2 * SEG)
+        return lax.broadcasted_iota(jnp.int32, shape, 1) <= lax.broadcasted_iota(jnp.int32, shape, 0) + run * SEG
+
+    def of_parent():
+        return seg_row[0:1, 2 * SEG : 4 * SEG] == parent_col[rows, 0:1]
+
+    def of_run():
+        shape = (SEG, SEG)
+        order = lax.broadcasted_iota(jnp.int32, shape, 1) <= lax.broadcasted_iota(jnp.int32, shape, 0)
+        return order & (seg_row[0:1, rows] == seg_col[rows, 0:1])
+
+    if run < 2:
+        return [(slice(0, 2 * SEG), causal())]
+    parts = [(slice(0, 2 * SEG), None)]
+    if run >= 4:
+        parts.append((slice(2 * SEG, 4 * SEG), of_parent()))
+    parts.append((rows, of_run()))
+    return parts
+
+
+def score_parts(pairs, keys, parts):
+    scores = []
+    for span, mask in parts:
+        score = dot_nt(pairs, keys[span])
+        if mask is not None:
+            both = jnp.concatenate([mask, mask], axis=0)
+            score = jnp.where(both, score, masked_value)
+        scores.append(score)
+    return scores
+
+
+def softmax_parts(scores):
+    peak = None
+    for score in scores:
+        top = jnp.max(score, axis=-1, keepdims=True)
+        peak = top if peak is None else jnp.maximum(peak, top)
+    exps = [jnp.exp((score - peak) * score_mult) for score in scores]
+    total = None
+    for term in exps:
+        part = jnp.sum(term, axis=-1, keepdims=True)
+        total = part if total is None else total + part
+    return exps, 1.0 / total
+
+
+def attend(qkv_ref, seg_col_ref, parent_col_ref, seg_row_ref, heads_ref):
+    seg_row = seg_row_ref[...]
+    keys, values = key_value_tiles(qkv_ref[:, 2 * SEG : 3 * SEG])
+    for run in range(TREE // SEG):
+        rows = slice(run * SEG, (run + 1) * SEG)
+        pairs = jnp.concatenate([qkv_ref[rows, 0:128], qkv_ref[rows, 128:256]], axis=0)
+        parts = masked_parts(run, seg_col_ref, parent_col_ref, seg_row)
+        mixed = None
+        for half in range(2):
+            exps, inverse = softmax_parts(score_parts(pairs, keys[half], parts))
+            for (span, _), term in zip(parts, exps):
+                got = dot_nn((term * inverse).astype(jnp.bfloat16), values[half][span])
+                mixed = got if mixed is None else mixed + got
+        low = mixed.astype(jnp.bfloat16)
+        heads_ref[rows, 0:128] = low[0:SEG]
+        heads_ref[rows, 128:256] = low[SEG:]
+
+
+def forward_kernel(
+    near, tokens, cot, own_qkv, own_out, own_gu, own_down, gain, cosines, sines,
+    seg_col, parent_col, seg_row,
+    w_qkv, w_out, w_gu, w_down, attn_in, cot_full, ffn_in, qkv, heads, resid, gate, up, hidden, down_grad,
+    partial, from_core, from_x, resid_buf, normed_buf, tokens_buf, gain_buf,
+    w_send, w_recv, w_keep, t_send, t_recv, t_keep, s_send, s_recv, l_sem,
+):
+    place = Place()
+    copies = Copies()
+    place.greet()
+
+    def row_block(full, r):
+        return full.at[rows_of(r, OWN), :]
+
+    def col_block(full, r):
+        return full.at[:, rows_of(r, OWN)]
+
+    def weight(index, own, full, view):
+        return WeightGather(
+            place, copies, own, full, view, w_send.at[index], w_recv.at[index], w_keep.at[index]
+        )
+
+    g_qkv = weight(0, own_qkv, w_qkv, row_block)
+    g_out = weight(1, own_out, w_out, col_block)
+    g_gate = weight(2, own_gu.at[0], w_gu.at[0], row_block)
+    g_up = weight(3, own_gu.at[1], w_gu.at[1], row_block)
+    g_down = weight(4, own_down, w_down, col_block)
+
+    def token_gather(index, full, m):
+        return TokenGather(place, copies, full, m * TREE, t_send.at[index], t_recv.at[index])
+
+    a_in = [token_gather(m, attn_in, m) for m in range(MICRO)]
+    a_cot = [token_gather(2 + m, cot_full, m) for m in range(MICRO)]
+    a_ffn = [token_gather(4 + m, ffn_in, m) for m in range(MICRO)]
+    sums = [
+        TokenSum(place, copies, partial.at[m], from_core.at[m], from_x.at[m], s_send.at[m], s_recv.at[m])
+        for m in range(MICRO)
+    ]
+
+    def project(m):
+        def body(a_ref, w_ref, cos_ref, sin_ref, out_ref):
+            got = dot_nn(a_ref[...], w_ref[...])
+            cos, sin = cos_ref[...], sin_ref[...]
+            lane = lax.broadcasted_iota(jnp.int32, cos.shape, 1)
+            cos_key = jnp.where(lane < HD, cos, 1.0)
+            sin_key = jnp.where(lane < HD, sin, 0.0)
+            for tile in range(got.shape[1] // 128):
+                part = got[:, tile * 128 : (tile + 1) * 128]
+                is_key = tile % 3 == 2
+                turned = part * (cos_key if is_key else cos) + swap_halves(part) * (sin_key if is_key else sin)
+                out_ref[:, tile * 128 : (tile + 1) * 128] = turned.astype(jnp.bfloat16)
+
+        steps = TREE // OWN
+        rows = pl.BlockSpec((OWN, D), lambda i: (m * steps + i, 0))
+        table = pl.BlockSpec((OWN, 128), lambda i: (m * steps + i, 0))
+        out = pl.BlockSpec((OWN, 768), lambda i: (m * steps + i, 0))
+        whole = pl.BlockSpec((D, 768), lambda i: (0, 0))
+        pltpu.emit_pipeline(body, grid=(steps,), in_specs=[rows, whole, table, table], out_specs=[out])(
+            attn_in, w_qkv, cosines, sines, qkv
+        )
+
+    def attention(m):
+        tree = pl.BlockSpec((TREE, 128), lambda g: (m, 0))
+        pltpu.emit_pipeline(
+            attend,
+            grid=(2,),
+            in_specs=[
+                pl.BlockSpec((TREE, 384), lambda g: (m, g)),
+                tree,
+                tree,
+                pl.BlockSpec((8, TREE), lambda g: (m, 0)),
+            ],
+            out_specs=[pl.BlockSpec((TREE, 256), lambda g: (m, g))],
+        )(qkv, seg_col, parent_col, seg_row, heads)
+
+    def out_project(m):
+        def body_at(step, a_ref, w_ref):
+            partial[m, step.index[0]] = dot_nn(a_ref[...], w_ref[...]).astype(jnp.bfloat16)
+
+        steps = TREE // OWN
+        pltpu.emit_pipeline(
+            body_at,
+            grid=(steps,),
+            in_specs=[
+                pl.BlockSpec((OWN, 512), lambda i: (m * steps + i, 0)),
+                pl.BlockSpec((512, D), lambda i: (0, 0)),
+            ],
+            out_specs=[],
+            _explicit_indices=True,
+        )(heads, w_out)
+
+    def middle_norm(m):
+        sums[m].arrive()
+        load = copies.local(tokens.at[m], tokens_buf, l_sem.at[0])
+        load_gain = copies.local(gain, gain_buf, l_sem.at[1])
+        load.wait()
+        load_gain.wait()
+
+        @pl.loop(0, OWN // 32)
+        def _(i):
+            rows = rows_of(i, 32)
+            value = tokens_buf[rows, :].astype(jnp.float32) + residual_mult * sums[m].rows(rows)
+            resid_buf[m, rows, :] = value
+            scale = lax.rsqrt(jnp.mean(value * value, axis=-1, keepdims=True) + norm_eps)
+            normed_buf[m, rows, :] = (value * scale * gain_buf[1:2, :]).astype(jnp.bfloat16)
+
+        a_ffn[m].start(normed_buf.at[m], t_keep.at[4 + m])
+        return copies.local(resid_buf.at[m], resid.at[m], l_sem.at[2 + m])
+
+    def gate_up(m):
+        def body(a_ref, g_ref, u_ref, gate_ref, up_ref, hidden_ref):
+            for part in range(TREE // OWN):
+                rows = slice(part * OWN, (part + 1) * OWN)
+                value = a_ref[rows, :]
+                g = dot_nn(value, g_ref[0])
+                u = dot_nn(value, u_ref[0])
+                gate_ref[rows, :] = g.astype(jnp.bfloat16)
+                up_ref[rows, :] = u.astype(jnp.bfloat16)
+                hidden_ref[rows, :] = (g * jax.nn.sigmoid(g) * u).astype(jnp.bfloat16)
+
+        cols = pl.BlockSpec((TREE, 256), lambda j: (m, j))
+        pltpu.emit_pipeline(
+            body,
+            grid=(WIDE // 256,),
+            in_specs=[
+                pl.BlockSpec((TREE, D), lambda j: (m, 0)),
+                pl.BlockSpec((1, D, 256), lambda j: (0, 0, j)),
+                pl.BlockSpec((1, D, 256), lambda j: (1, 0, j)),
+            ],
+            out_specs=[cols, cols, cols],
+        )(ffn_in, w_gu, w_gu, gate, up, hidden)
+
+    def grad_down():
+        def body(h_ref, c_ref, out_ref):
+            out_ref[...] = (residual_mult * dot_tn(h_ref[...], c_ref[...])).astype(jnp.bfloat16)
+
+        pltpu.emit_pipeline(
+            body,
+            grid=(WIDE // 256,),
+            in_specs=[
+                pl.BlockSpec((MICRO * TREE, 256), lambda i: (0, i)),
+                pl.BlockSpec((MICRO * TREE, D), lambda i: (0, 0)),
+            ],
+            out_specs=[pl.BlockSpec((256, D), lambda i: (i, 0))],
+        )(hidden, cot_full, down_grad)
+
+    g_qkv.start()
+    for m in range(MICRO):
+        a_in[m].start(near.at[m], t_keep.at[m])
+    g_out.start()
+    g_gate.start()
+    for m in range(MICRO):
+        a_cot[m].start(cot.at[m], t_keep.at[2 + m])
+    a_in[0].relay()
+    a_in[1].relay()
+    g_qkv.relay()
+    g_out.relay()
+    g_up.start()
+    a_in[0].finish()
+    g_qkv.finish()
+    project(0)
+    a_in[1].finish()
+    project(1)
+    a_cot[0].relay()
+    a_cot[1].relay()
+    attention(0)
+    g_out.finish()
+    out_project(0)
+    sums[0].start()
+    attention(1)
+    sums[0].middle()
+    out_project(1)
+    sums[1].start()
+    g_gate.relay()
+    g_down.start()
+    stored = [middle_norm(0)]
+    sums[1].middle()
+    a_ffn[0].relay()
+    stored.append(middle_norm(1))
+    a_ffn[1].relay()
+    g_up.relay()
+    a_cot[0].finish()
+    a_cot[1].finish()
+    a_ffn[0].finish()
+    g_gate.finish()
+    g_up.finish()
+    gate_up(0)
+    a_ffn[1].finish()
+    gate_up(1)
+    g_down.relay()
+    grad_down()
+    g_down.finish()
+    for copy in stored:
+        copy.wait()
+    copies.close()
+
+
+def forward(near, tokens, cot, low_qkv, low_out, low_gu, low_down, gains, cosines, sines, seg_col, parent_col, seg_row):
+    low = jnp.bfloat16
+    shape = jax.ShapeDtypeStruct
+    all_tokens = MICRO * TREE
+    outs = [
+        shape((D, 768), low), shape((512, D), low), shape((2, D, WIDE), low), shape((WIDE, D), low),
+        shape((all_tokens, D), low), shape((all_tokens, D), low), shape((all_tokens, D), low),
+        shape((all_tokens, 768), low), shape((all_tokens, 512), low), shape((MICRO, OWN, D), jnp.float32),
+        shape((all_tokens, WIDE), low), shape((all_tokens, WIDE), low), shape((all_tokens, WIDE), low),
+        shape((WIDE, D), low),
+    ]
+    dma = pltpu.SemaphoreType.DMA
+    return pl.pallas_call(
+        forward_kernel,
+        out_shape=outs,
+        in_specs=[HBM] * 13,
+        out_specs=[HBM] * len(outs),
+        scratch_shapes=[
+            pltpu.VMEM((MICRO, NX * NC, OWN, D), low),
+            pltpu.VMEM((MICRO, NX, OWN, D), low),
+            pltpu.VMEM((MICRO, OWN, D), low),
+            pltpu.VMEM((MICRO, OWN, D), jnp.float32),
+            pltpu.VMEM((MICRO, OWN, D), low),
+            pltpu.VMEM((OWN, D), low),
+            pltpu.VMEM((2, D), jnp.float32),
+            dma((5, 7)), dma((5, NZ * NY)), dma((5,)),
+            dma((6, 3)), dma((6, NX * NC)), dma((6,)),
+            dma((MICRO, 3)), dma((MICRO, 3)), dma((4,)),
+        ],
+        compiler_params=pltpu.CompilerParams(
+            collective_id=0, has_side_effects=True, vmem_limit_bytes=60 * 1024 * 1024
+        ),
+        cost_estimate=pl.CostEstimate(flops=90 * 10**9, bytes_accessed=2 * 10**8, transcendentals=10**7),
+        name="forward",
+    )(near, tokens, cot, low_qkv, low_out, low_gu, low_down, gains, cosines, sines, seg_col, parent_col, seg_row)
+
+
+def fast_local(
+    tokens,
+    cotangent,
+    segment_of,
+    leaf_parent,
+    w_qkv,
+    mom_qkv,
+    w_out,
+    mom_out,
+    w_gu,
+    mom_gu,
+    w_down,
+    mom_down,
+    gains,
+    mom_gains,
+):
+    low = jnp.bfloat16
+    tables = [position_tables(segment_of[m], leaf_parent[m]) for m in range(MICRO)]
+    cos_all, sin_all, seg_col, parent_col, seg_row = (
+        jnp.concatenate([table[i] for table in tables], axis=0) for i in range(5)
+    )
+    wide = tokens.astype(jnp.float32)
+    near, scales = normalize(wide, gains[0])
+    (w_a, w_b, w_c, w_d, attn_all, cot_all, ffn_all, qkv_all, heads_all, resid_all, gate_all, up_all, hidden_all, down_all) = forward(
+        near.astype(low), tokens, cotangent,
+        w_qkv.astype(low).reshape(OWN, 768), w_out.astype(low), w_gu.astype(low), w_down.astype(low),
+        gains, cos_all, sin_all, seg_col, parent_col, seg_row,
+    )
+    w_a = w_a.reshape(D, 2, 384)
+    groups = 2
+    tree_len = TREE
+    row_count = OWN
+    outputs = []
+    input_grads = []
+    unsummed = None
+    gain_partial = None
+    for batch_index in range(MICRO):
+        span = slice(batch_index * TREE, (batch_index + 1) * TREE)
+        allowed, cosines, sines = tree_tables(segment_of[batch_index], leaf_parent[batch_index])
+        x_local = wide[batch_index]
+        scale_a = scales[batch_index]
+        attn_in, cot_full, ffn_in, hidden, mixed_heads = attn_all[span], cot_all[span], ffn_all[span], hidden_all[span], heads_all[span]
+        gate_up = jnp.stack([gate_all[span], up_all[span]], axis=1).astype(jnp.float32)
+        gate_act = jax.nn.sigmoid(gate_up[:, 0])
+        silu_gate = gate_up[:, 0] * gate_act
+        residual_mid = resid_all[batch_index]
+        normed_b, scale_b = normalize(residual_mid, gains[1])
+        packed = qkv_all[span].reshape(tree_len, groups, 384)
+        queries = packed[:, :, :256].reshape(tree_len, groups, GROUP, HD)
+        key_heads, values = packed[:, :, 256:320], packed[:, :, 320:]
+        scores = jnp.einsum("tkgh,skh->kgts", queries, key_heads, preferred_element_type=jnp.float32)
+        logits = jnp.where(allowed, score_mult * scores, masked_value)
+        row_peak = jnp.max(logits, axis=-1, keepdims=True)
+        log_total = row_peak + jnp.log(jnp.sum(jnp.exp(logits - row_peak), axis=-1, keepdims=True))
+
+        def down_terms(first_row, row_total):
+            return jnp.dot(hidden, w_d, preferred_element_type=jnp.float32)
+
+        mlp_sum = sum_forward(down_terms, row_count)
+        outputs.append((residual_mid + residual_mult * mlp_sum).astype(jnp.bfloat16))
+        hidden_grad = residual_mult * jnp.einsum(
+            "td,fd->tf", cot_full, w_d, preferred_element_type=jnp.float32
+        )
+        gate_grad = (
+            hidden_grad * gate_up[:, 1] * gate_act * (1.0 + gate_up[:, 0] * (1.0 - gate_act))
+        )
+        up_grad = hidden_grad * silu_gate
+        gate_up_grad = jnp.stack([gate_grad, up_grad], axis=1).astype(jnp.bfloat16)
+        gu_grad = jnp.einsum(
+            "td,tef->edf", ffn_in, gate_up_grad, preferred_element_type=jnp.float32
+        )
+
+        def ffn_back_terms(first_row, row_total):
+            return jnp.einsum("tef,edf->td", gate_up_grad, w_c, preferred_element_type=jnp.float32)
+
+        ffn_in_grad = sum_backward(ffn_back_terms, row_count)
+        mid_norm_grad, gain_b_grad = norm_back(residual_mid, scale_b, gains[1], ffn_in_grad)
+        mid_grad = cotangent[batch_index].astype(jnp.float32) + mid_norm_grad
+        attn_out_grad = gather_backward((residual_mult * mid_grad).astype(jnp.bfloat16))
+        out_grad = jnp.einsum(
+            "tf,td->fd", mixed_heads, attn_out_grad, preferred_element_type=jnp.float32
+        )
+        heads_grad = (
+            jnp.einsum("td,fd->tf", attn_out_grad, w_b, preferred_element_type=jnp.float32)
+            .astype(jnp.bfloat16)
+            .reshape(tree_len, groups, GROUP, HD)
+        )
+        attn_probs = jnp.exp(logits - log_total)
+        prob_grad = jnp.einsum(
+            "tkgh,skh->kgts", heads_grad, values, preferred_element_type=jnp.float32
+        )
+        row_inner = jnp.sum(prob_grad * attn_probs, axis=-1, keepdims=True)
+        score_grad = (score_mult * attn_probs * (prob_grad - row_inner)).astype(jnp.bfloat16)
+        query_grad = jnp.einsum(
+            "kgts,skh->tkgh", score_grad, key_heads, preferred_element_type=jnp.float32
+        )
+        key_grad = jnp.einsum(
+            "kgts,tkgh->skh", score_grad, queries, preferred_element_type=jnp.float32
+        )
+        value_grad = jnp.einsum(
+            "kgts,tkgh->skh",
+            attn_probs.astype(jnp.bfloat16),
+            heads_grad,
+            preferred_element_type=jnp.float32,
+        )
+        query_grad = rotate(query_grad, cosines[:, None, None, :], -sines[:, None, None, :])
+        key_grad = rotate(key_grad, cosines[:, None, :], -sines[:, None, :])
+        proj_grad = jnp.concatenate(
+            [query_grad.reshape(tree_len, groups, GROUP * HD), key_grad, value_grad], axis=-1
+        ).astype(jnp.bfloat16)
+        qkv_grad = jnp.einsum("td,tkf->dkf", attn_in, proj_grad, preferred_element_type=jnp.float32)
+
+        def attn_back_terms(first_row, row_total):
+            return jnp.einsum("tkf,dkf->td", proj_grad, w_a, preferred_element_type=jnp.float32)
+
+        attn_in_grad = sum_backward(attn_back_terms, row_count)
+        input_norm_grad, gain_a_grad = norm_back(x_local, scale_a, gains[0], attn_in_grad)
+        input_grads.append(mid_grad + input_norm_grad)
+        gain_step = jnp.stack([gain_a_grad, gain_b_grad])
+        gain_partial = gain_step if gain_partial is None else gain_partial + gain_step
+        partials = (qkv_grad, out_grad, gu_grad)
+        unsummed = (
+            partials
+            if unsummed is None
+            else tuple((running + addend for running, addend in zip(unsummed, partials)))
+        )
+    owned = (
+        lax.psum_scatter(
+            unsummed[0].astype(jnp.bfloat16), "row", scatter_dimension=0, tiled=True
+        ).astype(jnp.float32),
+        lax.psum_scatter(
+            unsummed[1].astype(jnp.bfloat16), "row", scatter_dimension=1, tiled=True
+        ).astype(jnp.float32),
+        lax.psum_scatter(
+            unsummed[2].astype(jnp.bfloat16), "row", scatter_dimension=1, tiled=True
+        ).astype(jnp.float32),
+        lax.psum_scatter(
+            down_all, "row", scatter_dimension=1, tiled=True
+        ).astype(jnp.float32),
+    )
+    local_squares = jnp.float32(0.0)
+    for grad_piece in owned:
+        local_squares = local_squares + jnp.sum(grad_piece * grad_piece)
+    total_squares, gain_total = lax.psum((local_squares, gain_partial), ("row", "col"))
+    grad_norm = jnp.sqrt(total_squares + jnp.sum(gain_total * gain_total))
+    factor = jnp.minimum(1.0, clip_bound() / (grad_norm + 1e-06))
+    rates = step_rates()
+    masters = (w_qkv, w_out, w_gu, w_down)
+    states = (mom_qkv, mom_out, mom_gu, mom_down)
+    results = []
+    for index_w in range(4):
+        updated, moments = adamw(
+            masters[index_w], states[index_w], owned[index_w], factor, rates[index_w]
+        )
+        results.append((updated, moments, updated.astype(jnp.bfloat16)))
+    new_gains, moments_gains = adamw(gains, mom_gains, gain_total, factor, rates[4])
+    mixed = jnp.stack(outputs, axis=0)
+    d_tokens = jnp.stack(input_grads, axis=0)
+    return (
+        mixed,
+        d_tokens,
+        grad_norm,
+        results[0][0],
+        results[0][1],
+        results[0][2],
+        results[1][0],
+        results[1][1],
+        results[1][2],
+        results[2][0],
+        results[2][1],
+        results[2][2],
+        results[3][0],
+        results[3][1],
+        results[3][2],
+        new_gains,
+        moments_gains,
+    )
+
+
 def solution(mesh):
     placed = (
         P(None, ("row", "col"), None),
@@ -373,8 +1084,10 @@
         P(),
         P(),
     )
+    sizes = dict(mesh.shape)
+    fits = sizes == {"row": NZ * NY, "col": NX * NC}
     return jax.shard_map(
-        local,
+        fast_local if fits else local,
         mesh=mesh,
         in_specs=placed,
         out_specs=(

time: 1870 us -> 1650 us (0.88)
  waiting for transfers between devices: 1040 us -> 441 us
  Pallas kernels: 0 us -> 451 us
  matrix products: 513 us -> 369 us
  local copies, waits for them, and re-layouts: 73.1 us -> 115 us
  other arithmetic: 171 us -> 202 us
    all_gather x8 -> x0, waiting for transfers between devices: 481 us -> none  [the longest x1 230 us: fetch(): lax.all_gather(low_shards[2], 'row', axis=1, tiled=True)]
    pallas_call x0 -> x1, Pallas kernels: none -> 451 us  [forward(): pl.pallas_call(forward_kernel, out_shape=outs, in_specs=[HBM] * 13, out_s...]
    dot_general x30 -> x20, matrix products: 414 us -> 271 us  [the longest x2 54.8 us: fast_local(): jnp.einsum('td,tef->edf', ffn_in, gate_up_grad, preferred_element_type=jn...]
    reduce_scatter x4 -> x2, waiting for transfers between devices: 128 us -> 85.4 us  [sum_forward(): lax.psum_scatter(term_fn(jnp.int32(0), lax.axis_size('col') * row_count)....]
    reduce_scatter x4, waiting for transfers between devices: 119 us -> 78.1 us  [sum_backward(): lax.psum_scatter(term_fn(jnp.int32(0), lax.axis_size('col') * row_count)....]
    all_gather x4 -> x2, waiting for transfers between devices: 31.4 us -> 0.02 us  [gather_backward(): return lax.all_gather(values, 'col', axis=0, tiled=True)]
    convert_element_type x13 -> x19, other arithmetic: 86.7 us -> 105 us  [the longest x2 57.3 us: fast_local(): (score_mult * attn_probs * (prob_grad - row_inner)).astype(jnp.bfloat16)]
    unnamed x204 -> x182, local copies, waits for them, and re-layouts: 44.8 us -> 53.2 us
  transfers between devices with their start and end apart: 24 -> 12, of which waited for: 17 -> 5; matrix products, arithmetic and copies ran while one was open for 37% -> 32% of each run, Pallas kernels for 0% -> 0%
where the time goes in v1:
time: 1650 us; the launch traced here: 1640 us
  Pallas kernels  451 us (27%)
  waiting for transfers between devices  441 us (27%)
  matrix products  369 us (22%)
  other arithmetic  202 us (12%)
  local copies, waits for them, and re-layouts  115 us (7%)
  blocking collectives  39.8 us (2%)
  between operations  21.8 us (1%)
    pallas_call x1, Pallas kernels, forward(): pl.pallas_call(forward_kernel, out_shape=outs, in_specs=[HBM] * 13, out_s...  451 us
    reduce_scatter x1, waiting for transfers between devices, fast_local(): lax.psum_scatter(unsummed[2].astype(jnp.bfloat16), 'row', scatter_dimensi...  276 us
    reduce_scatter x2, waiting for transfers between devices, sum_forward(): lax.psum_scatter(term_fn(jnp.int32(0), lax.axis_size('col') * row_count)....  85.4 us
    reduce_scatter x4, waiting for transfers between devices, sum_backward(): lax.psum_scatter(term_fn(jnp.int32(0), lax.axis_size('col') * row_count)....  78.1 us
    convert_element_type x2, other arithmetic, fast_local(): (score_mult * attn_probs * (prob_grad - row_inner)).astype(jnp.bfloat16)  57.3 us
    dot_general x2, matrix products, fast_local(): jnp.einsum('td,tef->edf', ffn_in, gate_up_grad, preferred_element_type=jn...  54.8 us
    unnamed x182, local copies, waits for them, and re-layouts  53.2 us
    dot_general x2, matrix products, ffn_back_terms(): jnp.einsum('tef,edf->td', gate_up_grad, w_c, preferred_element_type=jnp.f...  47.7 us
  transfers between devices with their start and end apart: 12, of which 5 were waited for; matrix products, arithmetic and copies ran while one was open for 32% of the time, Pallas kernels for 0%

profile of v1, /device:TPU:0, one launch (start us, length us, event | category | flops | bytes accessed | tf_op | source)
XLA Modules:
  0.0 1639.1 jit_solution(18320019652877239858)
XLA Ops:
  38.5 450.8 %forward.1 = (bf16[2048,768]{1,0:T(8,128)(2,1)}, bf16[512,2048]{1,0:T(8,128)(2,1)}, bf16[2,2048,2048]{2,1,0:T(8,128)(2,1)}, bf16[2048,2048]{1,0:T(8,128)(2,1)}, ...) custom-call(bf16[2,256,2048]{2,1,0:T(8,128)(2,1)} %multiply_convert_, ...), custom_call_target="tpu_custom_call" | custom-call | flops 89999998976 | bytes 200000000 | tf_op jit(solution)/shard_map/forward/pallas_call | solution.py:866
  500.5 9.0 maximum_convert_fusion.1
  509.5 20.7 %fusion.50 = (bf16[1024,1,2048]{2,0,1:T(8,128)(2,1)}, bf16[1024,1,2048]{2,0,1:T(8,128)(2,1)}) fusion(f32[1024,2,2048]{2,0,1:T(8,128)} %maximum_convert_fusion.1, bf16[2048,2048]{1,0:T(8,128)(2,1)} %get-tuple-element.33, bf16[2048,2048]{1,0:T(8,128)(2,1)} %get-tuple-element.34), kind=kOutput, calls=%fused_computation.93 | convolution fusion | flops 8619294720 | bytes 37748736 | tf_op jit(solution)/shard_map/td,fd->tf/dot_general | solution.py:951
  530.2 23.9 %bitcast_convert_fusion.1 = bf16[1024,2048]{1,0:T(8,128)(2,1)} fusion(bf16[2,2048,2048]{2,1,0:T(8,128)(2,1)} %get-tuple-element.37, bf16[1024,1,2048]{2,0,1:T(8,128)(2,1)} %get-tuple-element.125, bf16[1024,1,2048]{2,0,1:T(8,128)(2,1)} %get-tuple-element.124), kind=kOutput, calls=%fused_computation.42 | convolution fusion | flops 17186160640 | bytes 29360128 | tf_op jit(solution)/shard_map/tef,edf->td/dot_general | solution.py:964
  554.2 12.0 maximum_convert_fusion
  566.1 21.3 %fusion.49 = (bf16[1024,1,2048]{2,0,1:T(8,128)(2,1)}, bf16[1024,1,2048]{2,0,1:T(8,128)(2,1)}) fusion(f32[1024,2,2048]{2,0,1:T(8,128)} %maximum_convert_fusion, bf16[2048,2048]{1,0:T(8,128)(2,1)} %get-tuple-element.33, bf16[2048,2048]{1,0:T(8,128)(2,1)} %get-tuple-element.34), kind=kOutput, calls=%fused_computation.92 | convolution fusion | flops 8619294720 | bytes 37748736 | tf_op jit(solution)/shard_map/td,fd->tf/dot_general | solution.py:951
  587.4 23.9 %bitcast_convert_fusion.3 = bf16[1024,2048]{1,0:T(8,128)(2,1)} fusion(bf16[2,2048,2048]{2,1,0:T(8,128)(2,1)} %get-tuple-element.37, bf16[1024,1,2048]{2,0,1:T(8,128)(2,1)} %get-tuple-element.127, bf16[1024,1,2048]{2,0,1:T(8,128)(2,1)} %get-tuple-element.126), kind=kOutput, calls=%fused_computation.44 | convolution fusion | flops 17186160640 | bytes 29360128 | tf_op jit(solution)/shard_map/tef,edf->td/dot_general | solution.py:964
  614.2 44.0 %reduce-scatter.15.cloned.1.call-done = bf16[256,2048]{1,0:T(8,128)(2,1)} async-done(((bf16[1024,2048]{1,0:T(8,128)(2,1)}), bf16[256,2048]{1,0:T(8,128)(2,1)}) %reduce-scatter.15.cloned.1.call-update) | async-done | bytes 1048592 | tf_op jit(solution)/shard_map/reduce_scatter | solution.py:126
  710.4 15.2 fusion.212
  725.6 13.4 exponential_reduce_fusion
  739.1 13.8 fusion.211
  753.0 13.3 exponential_reduce_fusion.1
  771.6 14.5 fusion.122
  787.0 21.8 %fusion = (f32[2,4,1024]{2,1,0:T(4,128)S(1)}, f32[2,1024,1024,4]{2,1,3,0:T(8,128)}) fusion(f32[2,4,1024,1024]{2,3,1,0:T(8,128)} %get-tuple-element.202, f32[2,4,1024]{2,1,0:T(4,128)S(1)} %bitcast.441, bf16[1024,2,4,64]{0,3,2,1:T(8,128)(2,1)S(1)} %bitcast.430, bf16[1024,2,64]{0,2,1:T(8,128)(2,1)S(1)} %copy-done.42), kind=kOutput, calls=%fused_computation.2 | convolution fusion | flops 1098899456 | bytes 68485120 | tf_op jit(solution)/shard_map/tkgh,skh->kgts/dot_general | solution.py:979
  808.9 28.2 %fusion.2 = bf16[2,4,1024,1024]{2,3,1,0:T(8,128)(2,1)} fusion(f32[2,1024,1024,4]{2,1,3,0:T(8,128)} %get-tuple-element.204, f32[2,4,1024,1024]{2,3,1,0:T(8,128)} %get-tuple-element.202, f32[2,4,1024]{2,1,0:T(4,128)S(1)} %get-tuple-element.203, f32[2,4,1024]{2,1,0:T(4,128)S(1)} %bitcast.442), kind=kLoop, calls=%fused_computation.4 | loop fusion | flops 41943040 | bytes 83951616 | tf_op jit(solution)/shard_map/convert_element_type | solution.py:983
  847.8 11.0 convolution_bitcast_fusion.2
  866.1 13.7 fusion.119
  889.2 21.6 %fusion.3 = (f32[2,4,1024]{2,1,0:T(4,128)S(1)}, f32[2,1024,1024,4]{2,1,3,0:T(8,128)}) fusion(f32[2,4,1024,1024]{2,3,1,0:T(8,128)} %get-tuple-element.198, f32[2,4,1024]{2,1,0:T(4,128)S(1)} %bitcast.438, bf16[1024,2,4,64]{0,3,2,1:T(8,128)(2,1)S(1)} %bitcast.428, bf16[1024,2,64]{0,2,1:T(8,128)(2,1)S(1)} %copy-done.41), kind=kOutput, calls=%fused_computation.8 | convolution fusion | flops 1098899456 | bytes 68485120 | tf_op jit(solution)/shard_map/tkgh,skh->kgts/dot_general | solution.py:979
  910.9 29.0 %fusion.5 = bf16[2,4,1024,1024]{2,3,1,0:T(8,128)(2,1)} fusion(f32[2,1024,1024,4]{2,1,3,0:T(8,128)} %get-tuple-element.200, f32[2,4,1024,1024]{2,3,1,0:T(8,128)} %get-tuple-element.198, f32[2,4,1024]{2,1,0:T(4,128)S(1)} %get-tuple-element.199, f32[2,4,1024]{2,1,0:T(4,128)S(1)} %bitcast.439), kind=kLoop, calls=%fused_computation.10 | loop fusion | flops 41943040 | bytes 83951616 | tf_op jit(solution)/shard_map/convert_element_type | solution.py:983
  939.9 9.0 convolution_bitcast_fusion.1
  950.7 11.1 convolution_bitcast_fusion.3
  995.1 13.9 fusion.51
  1009.0 13.9 fusion.54
  1023.1 25.8 %fusion.24 = f32[2,2048,2048]{2,1,0:T(8,128)} fusion(bf16[1024,1,2048]{2,0,1:T(8,128)(2,1)} %get-tuple-element.127, bf16[1024,1,2048]{2,0,1:T(8,128)(2,1)} %get-tuple-element.126, bf16[2048,2048]{1,0:T(8,128)(2,1)} %get-tuple-element.43), kind=kOutput, calls=%fused_computation.52 | convolution fusion | flops 17184063488 | bytes 46137344 | tf_op jit(solution)/shard_map/td,tef->edf/dot_general | solution.py:959
  1048.9 29.0 %fusion.12 = bf16[2,2048,2048]{1,2,0:T(8,128)(2,1)} fusion(f32[2,2048,2048]{2,1,0:T(8,128)} %fusion.24, bf16[1024,1,2048]{2,0,1:T(8,128)(2,1)} %get-tuple-element.125, bf16[1024,1,2048]{2,0,1:T(8,128)(2,1)} %get-tuple-element.124, bf16[2048,2048]{1,0:T(8,128)(2,1)} %get-tuple-element.43), kind=kOutput, calls=%fused_computation.21 | convolution fusion | flops 17200840704 | bytes 62914560 | tf_op jit(solution)/shard_map/td,tef->edf/dot_general | solution.py:959
  1115.8 34.1 %reduce-scatter.17.cloned.1.call-done = bf16[256,2048]{1,0:T(8,128)(2,1)} async-done(((bf16[1024,2048]{1,0:T(8,128)(2,1)}), bf16[256,2048]{1,0:T(8,128)(2,1)}) %reduce-scatter.17.cloned.1.call-update) | async-done | bytes 1048592 | tf_op jit(solution)/shard_map/reduce_scatter | solution.py:126
  1158.5 38.5 %reduce-scatter.11.cloned.1.call-done = bf16[256,2048]{1,0:T(8,128)(2,1)} async-done(((bf16[1024,2048]{1,0:T(8,128)(2,1)}), bf16[256,2048]{1,0:T(8,128)(2,1)}) %reduce-scatter.11.cloned.1.call-update) | async-done | bytes 1048592 | tf_op jit(solution)/shard_map/reduce_scatter | solution.py:117
  1197.0 46.9 %reduce-scatter.13.cloned.1.call-done = bf16[256,2048]{1,0:T(8,128)(2,1)} async-done(((bf16[1024,2048]{1,0:T(8,128)(2,1)}), bf16[256,2048]{1,0:T(8,128)(2,1)}) %reduce-scatter.13.cloned.1.call-update) | async-done | bytes 1048592 | tf_op jit(solution)/shard_map/reduce_scatter | solution.py:117
  1252.1 275.8 %reduce-scatter.27.cloned.1.call-done = bf16[2,256,2048]{1,2,0:T(8,128)(2,1)} async-done(((bf16[2,2048,2048]{1,2,0:T(8,128)(2,1)}), bf16[2,256,2048]{1,2,0:T(8,128)(2,1)}) %reduce-scatter.27.cloned.1.call-update) | async-done | bytes 2097168 | tf_op jit(solution)/shard_map/reduce_scatter | solution.py:1024
  1535.4 39.8 %all-reduce.4 = (f32[]{:T(128)}, f32[2,2048]{1,0:T(2,128)S(1)}) all-reduce(f32[]{:T(128)S(6)} %add.334, f32[2,2048]{1,0:T(2,128)S(1)} %maximum_add_fusion), channel_id=1, replica_groups=mesh['row'=8,'col'=4] {'row','col'}, use_global_device_ids=true, to_apply=%region_37.38 | all-reduce | flops 4097 | bytes 32776 | tf_op jit(solution)/shard_map/psum | solution.py:1034
  1577.2 10.6 fusion.201
  1611.1 8.8 copy.185
  (344 shorter events, 259.0 us)
Async XLA Ops:
  8.0 606.1 %reduce-scatter.19.cloned.1.call-start = ((), (), s32[]{:S(2)}) async-start(), calls=%async_computation.15 | async-start | bytes 5242880 | tf_op jit(solution)/shard_map/reduce_scatter | solution.py:126
  554.1 104.1 %reduce-scatter.15.cloned.1.call-start = ((), (), s32[]{:S(2)}) async-start(), calls=%async_computation.12 | async-start | bytes 5242880 | tf_op jit(solution)/shard_map/reduce_scatter | solution.py:126
  611.3 46.9 %copy-start.58 = (f32[1,2048]{1,0:T(1,128)S(1)}, f32[1,2048]{1,0:T(1,128)}, u32[]{:S(2)}) copy-start(f32[1,2048]{1,0:T(1,128)} %get-tuple-element.170) | copy-start | bytes 24580
  611.3 155.0 %all-gather.5.cloned.1.call-start = ((), (), s32[]{:S(2)}) async-start(), calls=%async_computation.16 | async-start | bytes 5242880 | tf_op jit(solution)/shard_map/all_gather | solution.py:113
  611.3 51.7 %copy-start.13 = (bf16[2,256,2048]{2,1,0:T(8,128)(2,1)S(1)}, bf16[2,256,2048]{2,1,0:T(8,128)(2,1)}, u32[]{:S(2)}) copy-start(bf16[2,256,2048]{2,1,0:T(8,128)(2,1)} %cot.1) | copy-start | bytes 6291460
  614.1 51.9 %copy-start.70 = (f32[256]{0:T(256)}, f32[256]{0:T(256)S(1)}, u32[]{:S(2)}) copy-start(f32[256]{0:T(256)S(1)} %add_rsqrt_fusion.2) | copy-start | bytes 3076
  614.1 51.9 %copy-start.72 = (f32[256]{0:T(256)}, f32[256]{0:T(256)S(1)}, u32[]{:S(2)}) copy-start(f32[256]{0:T(256)S(1)} %add_rsqrt_fusion.1) | copy-start | bytes 3076
  614.1 48.9 %copy-start.7 = (bf16[256,2048]{1,0:T(8,128)(2,1)S(1)}, bf16[256,2048]{1,0:T(8,128)(2,1)}, u32[]{:S(2)}) copy-start(bf16[256,2048]{1,0:T(8,128)(2,1)} %reduce-scatter.19.cloned.1.call-done) | copy-start | bytes 3145732
  666.1 194.8 %all-gather.3.cloned.1.call-start = ((), (), s32[]{:S(2)}) async-start(), calls=%async_computation.13 | async-start | bytes 5242880 | tf_op jit(solution)/shard_map/all_gather | solution.py:113
  666.6 441.7 %reduce-scatter.29.cloned.1.call-start = ((), (), s32[]{:S(2)}) async-start(), calls=%async_computation.21 | async-start | bytes 9437184 | tf_op jit(solution)/shard_map/reduce_scatter | solution.py:1027
  667.2 443.6 %reduce-scatter.25.cloned.1.call-start = ((), (), s32[]{:S(2)}) async-start(), calls=%async_computation.19 | async-start | bytes 2359296 | tf_op jit(solution)/shard_map/reduce_scatter | solution.py:1021
  703.5 35.6 %copy-start.5 = (bf16[1024,2,256]{0,2,1:T(8,128)(2,1)}, bf16[1024,2,256]{0,2,1:T(8,128)(2,1)S(1)}, u32[]{:S(2)}) copy-start(bf16[1024,2,256]{0,2,1:T(8,128)(2,1)S(1)} %copy.138) | copy-start | bytes 3145732
  910.8 201.7 %reduce-scatter.23.cloned.1.call-start = ((), (), s32[]{:S(2)}) async-start(), calls=%async_computation.18 | async-start | bytes 3538944 | tf_op jit(solution)/shard_map/reduce_scatter | solution.py:1018
  910.9 29.1 %copy-start.40 = (bf16[1024,2,64]{0,2,1:T(8,128)(2,1)S(1)}, bf16[1024,2,64]{0,2,1:T(8,128)(2,1)}, u32[]{:S(2)}) copy-start(bf16[1024,2,64]{0,2,1:T(8,128)(2,1)} %copy.207) | copy-start | bytes 786436
  978.8 137.0 %reduce-scatter.21.cloned.1.call-start = ((), (), s32[]{:S(2)}) async-start(), calls=%async_computation.17 | async-start | bytes 5242880 | tf_op jit(solution)/shard_map/reduce_scatter | solution.py:126
  986.4 163.4 %reduce-scatter.17.cloned.1.call-start = ((), (), s32[]{:S(2)}) async-start(), calls=%async_computation.14 | async-start | bytes 5242880 | tf_op jit(solution)/shard_map/reduce_scatter | solution.py:126
  995.0 202.0 %reduce-scatter.11.cloned.1.call-start = ((), (), s32[]{:S(2)}) async-start(), calls=%async_computation.10 | async-start | bytes 5242880 | tf_op jit(solution)/shard_map/reduce_scatter | solution.py:117
  1009.0 234.9 %reduce-scatter.13.cloned.1.call-start = ((), (), s32[]{:S(2)}) async-start(), calls=%async_computation.11 | async-start | bytes 5242880 | tf_op jit(solution)/shard_map/reduce_scatter | solution.py:117
  1023.0 504.9 %reduce-scatter.27.cloned.1.call-start = ((), (), s32[]{:S(2)}) async-start(), calls=%async_computation.20 | async-start | bytes 18874368 | tf_op jit(solution)/shard_map/reduce_scatter | solution.py:1024
  1106.6 43.3 %copy-start.57 = (f32[1,2048]{1,0:T(1,128)S(1)}, f32[1,2048]{1,0:T(1,128)}, u32[]{:S(2)}) copy-start(f32[1,2048]{1,0:T(1,128)} %copy-done.56) | copy-start | bytes 24580
  1108.3 45.9 %copy-start.65 = (f32[2048]{0:T(1024)S(1)}, f32[2048]{0:T(1024)}, u32[]{:S(2)}) copy-start(f32[2048]{0:T(1024)} %get-tuple-element.102) | copy-start | bytes 24580
  1108.3 45.9 %copy-start.66 = (f32[2048]{0:T(1024)S(1)}, f32[2048]{0:T(1024)}, u32[]{:S(2)}) copy-start(f32[2048]{0:T(1024)} %get-tuple-element.105) | copy-start | bytes 24580
  1108.3 45.9 %copy-start.8 = (bf16[256,2048]{1,0:T(8,128)(2,1)S(1)}, bf16[256,2048]{1,0:T(8,128)(2,1)}, u32[]{:S(2)}) copy-start(bf16[256,2048]{1,0:T(8,128)(2,1)} %reduce-scatter.19.cloned.1.call-done) | copy-start | bytes 3145732
  1108.3 45.9 %copy-start.59 = (f32[1,2048]{1,0:T(1,128)S(1)}, f32[1,2048]{1,0:T(1,128)}, u32[]{:S(2)}) copy-start(f32[1,2048]{1,0:T(1,128)} %get-tuple-element.170) | copy-start | bytes 24580
  1108.3 45.9 %copy-start.73 = (f32[256]{0:T(256)S(1)}, f32[256]{0:T(256)}, u32[]{:S(2)}) copy-start(f32[256]{0:T(256)} %copy-done.72) | copy-start | bytes 3076
  1108.3 45.9 %copy-start.77 = (f32[256]{0:T(256)S(1)}, f32[256]{0:T(256)}, u32[]{:S(2)}) copy-start(f32[256]{0:T(256)} %copy-done.76) | copy-start | bytes 3076
  1154.3 89.6 %copy-start.10 = (bf16[256,2048]{1,0:T(8,128)(2,1)S(1)}, bf16[256,2048]{1,0:T(8,128)(2,1)}, u32[]{:S(2)}) copy-start(bf16[256,2048]{1,0:T(8,128)(2,1)} %reduce-scatter.15.cloned.1.call-done) | copy-start | bytes 3145732
  1154.3 89.6 %copy-start.26 = (bf16[256,2048]{1,0:T(8,128)(2,1)S(1)}, bf16[256,2048]{1,0:T(8,128)(2,1)}, u32[]{:S(2)}) copy-start(bf16[256,2048]{1,0:T(8,128)(2,1)} %reduce-scatter.17.cloned.1.call-done) | copy-start | bytes 3145732
  1154.3 89.6 %copy-start.71 = (f32[256]{0:T(256)S(1)}, f32[256]{0:T(256)}, u32[]{:S(2)}) copy-start(f32[256]{0:T(256)} %copy-done.70) | copy-start | bytes 3076
  1154.3 89.6 %copy-start.75 = (f32[256]{0:T(256)S(1)}, f32[256]{0:T(256)}, u32[]{:S(2)}) copy-start(f32[256]{0:T(256)} %copy-done.74) | copy-start | bytes 3076
  1249.8 282.8 %copy-start.28 = (bf16[1,256,2048]{2,1,0:T(8,128)(2,1)S(1)}, bf16[1,256,2048]{2,1,0:T(8,128)(2,1)}, u32[]{:S(2)}) copy-start(bf16[1,256,2048]{2,1,0:T(8,128)(2,1)} %get-tuple-element.143) | copy-start | bytes 3145732
  1527.9 49.3 %copy-start.16 = (bf16[2,256,2048]{1,2,0:T(8,128)(2,1)S(1)}, bf16[2,256,2048]{1,2,0:T(8,128)(2,1)}, u32[]{:S(2)}) copy-start(bf16[2,256,2048]{1,2,0:T(8,128)(2,1)} %reduce-scatter.27.cloned.1.call-done) | copy-start | bytes 6291460
  (66 other events, 413.8 us)
Sparse Core Ops, SparseCore 0:
  554.2 46.6 reduce-scatter.18
  611.4 46.7 reduce-scatter.14
  666.2 34.4 all-gather.4
  702.8 34.5 all-gather.2
Sparse Core Ops, SparseCore 1:
  670.7 147.3 reduce-scatter.28
  910.9 68.4 reduce-scatter.24
  983.3 72.7 reduce-scatter.22
  1058.7 43.4 reduce-scatter.20
  1105.4 44.4 reduce-scatter.16
  1152.6 44.4 reduce-scatter.10
  1199.4 44.4 reduce-scatter.12
  1248.0 279.8 reduce-scatter.26

commit v2 on v1

--- a/solution.py
+++ b/solution.py
@@ -557,7 +557,9 @@
                 + self.from_core[away, rows, :].astype(jnp.float32)
             ).astype(jnp.bfloat16)
 
-        self.copies.send(self.partial.at[p.col_x], self.from_x, self.send.at[2], self.recv.at[2], p.at_x)
+        self.passed = self.copies.send(
+            self.partial.at[p.col_x], self.from_x, self.send.at[2], self.recv.at[2], p.at_x
+        )
 
     def arrive(self):
         p = self.place
@@ -575,17 +577,6 @@
 def swap_halves(tile):
     lane = lax.broadcasted_iota(jnp.int32, tile.shape, 1)
     return jnp.where(lane % HD < HD // 2, pltpu.roll(tile, 128 - HD // 2, 1), pltpu.roll(tile, HD // 2, 1))
-
-
-def key_value_tiles(kv):
-    wide = kv.astype(jnp.float32)
-    lane = lax.broadcasted_iota(jnp.int32, wide.shape, 1)
-    key_low = jnp.where(lane < HD, wide, 0.0)
-    value_high = jnp.where(lane < HD, 0.0, wide)
-    key_high = pltpu.roll(key_low, HD, 1)
-    value_low = pltpu.roll(value_high, HD, 1)
-    low = jnp.bfloat16
-    return (key_low.astype(low), key_high.astype(low)), (value_low.astype(low), value_high.astype(low))
 
 
 def masked_parts(run, seg_col, parent_col, seg_row):
@@ -610,17 +601,6 @@
         parts.append((slice(2 * SEG, 4 * SEG), of_parent()))
     parts.append((rows, of_run()))
     return parts
-
-
-def score_parts(pairs, keys, parts):
-    scores = []
-    for span, mask in parts:
-        score = dot_nt(pairs, keys[span])
-        if mask is not None:
-            both = jnp.concatenate([mask, mask], axis=0)
-            score = jnp.where(both, score, masked_value)
-        scores.append(score)
-    return scores
 
 
 def softmax_parts(scores):
@@ -636,22 +616,92 @@
     return exps, 1.0 / total
 
 
+def stacked_pairs(tile_ref, rows):
+    both = jnp.concatenate([tile_ref[rows, 0:128], tile_ref[rows, 128:256]], axis=0)
+    lane = lax.broadcasted_iota(jnp.int32, both.shape, 1)
+    zero = jnp.zeros_like(both)
+    return jnp.concatenate([jnp.where(lane < HD, both, zero), jnp.where(lane < HD, zero, both)], axis=0)
+
+
+def unstack_pairs(wide):
+    half = wide.shape[0] // 2
+    lane = lax.broadcasted_iota(jnp.int32, (half, 128), 1)
+    return jnp.where(lane < HD, wide[:half], wide[half:])
+
+
+def twice(kv):
+    wide = kv.astype(jnp.float32)
+    lane = lax.broadcasted_iota(jnp.int32, wide.shape, 1)
+    other = pltpu.roll(wide, HD, 1)
+    key = jnp.where(lane < HD, wide, other)
+    value = jnp.where(lane < HD, other, wide)
+    return key.astype(jnp.bfloat16), value.astype(jnp.bfloat16)
+
+
+def score_parts(queries, keys, parts):
+    scores = []
+    for span, mask in parts:
+        score = dot_nt(queries, keys[span])
+        if mask is not None:
+            score = jnp.where(jnp.concatenate([mask] * 4, axis=0), score, masked_value)
+        scores.append(score)
+    return scores
+
+
 def attend(qkv_ref, seg_col_ref, parent_col_ref, seg_row_ref, heads_ref):
     seg_row = seg_row_ref[...]
-    keys, values = key_value_tiles(qkv_ref[:, 2 * SEG : 3 * SEG])
+    keys, values = twice(qkv_ref[:, 256:384])
     for run in range(TREE // SEG):
         rows = slice(run * SEG, (run + 1) * SEG)
-        pairs = jnp.concatenate([qkv_ref[rows, 0:128], qkv_ref[rows, 128:256]], axis=0)
         parts = masked_parts(run, seg_col_ref, parent_col_ref, seg_row)
+        exps, inverse = softmax_parts(score_parts(stacked_pairs(qkv_ref, rows), keys, parts))
         mixed = None
-        for half in range(2):
-            exps, inverse = softmax_parts(score_parts(pairs, keys[half], parts))
-            for (span, _), term in zip(parts, exps):
-                got = dot_nn((term * inverse).astype(jnp.bfloat16), values[half][span])
-                mixed = got if mixed is None else mixed + got
-        low = mixed.astype(jnp.bfloat16)
+        for (span, _), term in zip(parts, exps):
+            got = dot_nn((term * inverse).astype(jnp.bfloat16), values[span])
+            mixed = got if mixed is None else mixed + got
+        low = unstack_pairs(mixed).astype(jnp.bfloat16)
         heads_ref[rows, 0:128] = low[0:SEG]
         heads_ref[rows, 128:256] = low[SEG:]
+
+
+def attend_back(
+    key_sum, value_sum, qkv_ref, grad_ref, cos_ref, sin_ref, seg_col_ref, parent_col_ref, seg_row_ref, out_ref
+):
+    seg_row = seg_row_ref[...]
+    keys, values = twice(qkv_ref[:, 256:384])
+    key_sum[...] = jnp.zeros_like(key_sum)
+    value_sum[...] = jnp.zeros_like(value_sum)
+    for run in range(TREE // SEG):
+        rows = slice(run * SEG, (run + 1) * SEG)
+        parts = masked_parts(run, seg_col_ref, parent_col_ref, seg_row)
+        queries = stacked_pairs(qkv_ref, rows)
+        upstream = stacked_pairs(grad_ref, rows)
+        exps, inverse = softmax_parts(score_parts(queries, keys, parts))
+        probs = [term * inverse for term in exps]
+        prob_grads = [dot_nt(upstream, values[span]) for span, _ in parts]
+        inner = None
+        for prob, prob_grad in zip(probs, prob_grads):
+            term = jnp.sum(prob * prob_grad, axis=-1, keepdims=True)
+            inner = term if inner is None else inner + term
+        query_grad = None
+        for (span, _), prob, prob_grad in zip(parts, probs, prob_grads):
+            score_grad = (score_mult * prob * (prob_grad - inner)).astype(jnp.bfloat16)
+            term = dot_nn(score_grad, keys[span])
+            query_grad = term if query_grad is None else query_grad + term
+            key_sum[span, :] += dot_tn(score_grad, queries)
+            value_sum[span, :] += dot_tn(prob.astype(jnp.bfloat16), upstream)
+        pair_grad = unstack_pairs(query_grad)
+        cos, sin = cos_ref[rows, :], sin_ref[rows, :]
+        for tile in range(2):
+            part = pair_grad[tile * SEG : (tile + 1) * SEG]
+            out_ref[rows, tile * 128 : (tile + 1) * 128] = (part * cos - swap_halves(part) * sin).astype(jnp.bfloat16)
+    key_grad = key_sum[...]
+    key_grad = key_grad + pltpu.roll(key_grad, HD, 1)
+    value_grad = value_sum[...]
+    value_grad = value_grad + pltpu.roll(value_grad, HD, 1)
+    turned = key_grad * cos_ref[...] - swap_halves(key_grad) * sin_ref[...]
+    lane = lax.broadcasted_iota(jnp.int32, turned.shape, 1)
+    out_ref[:, 256:384] = jnp.where(lane < HD, turned, value_grad).astype(jnp.bfloat16)
 
 
 def forward_kernel(
@@ -888,6 +938,412 @@
     )(near, tokens, cot, low_qkv, low_out, low_gu, low_down, gains, cosines, sines, seg_col, parent_col, seg_row)
 
 
+class GradSum:
+    ORDER = (2, 1, 3)
+
+    def __init__(self, place, copies, full, view, from_y, summed, from_z, owned, squares, sems):
+        self.place, self.copies, self.full, self.view = place, copies, full, view
+        self.from_y, self.summed, self.from_z, self.owned = from_y, summed, from_z, owned
+        self.squares = squares
+        self.y_send, self.y_recv, self.z_send, self.z_recv = sems
+        rows, cols = owned.shape
+        step = max(16, min(rows, (256 * 1024) // cols))
+        self.grid = rows // step
+        self.spec = pl.BlockSpec((step, cols), lambda i: (i, 0))
+
+    def start(self):
+        p = self.place
+        for off in self.ORDER + (0,):
+            self.copies.send(
+                self.view(self.full, p.row_yz[off]), self.from_y.at[off], self.y_send.at[off], self.y_recv.at[off], p.at_y
+            )
+
+    def got_y(self, off):
+        self.copies.arrive(self.from_y.at[off], self.y_send.at[off], self.y_recv.at[off], self.place.at_y)
+
+    def middle(self, off):
+        p = self.place
+        self.got_y(off)
+
+        def body(a_ref, b_ref, out_ref):
+            out_ref[...] = (a_ref[...].astype(jnp.float32) + b_ref[...].astype(jnp.float32)).astype(jnp.bfloat16)
+
+        mine = self.view(self.full, p.row_z[off])
+        pltpu.emit_pipeline(body, grid=(self.grid,), in_specs=[self.spec] * 2, out_specs=[self.spec])(
+            mine, self.from_y.at[off], self.summed.at[off - 1]
+        )
+        self.copies.send(
+            self.summed.at[off - 1], self.from_z.at[off - 1], self.z_send.at[off - 1], self.z_recv.at[off - 1], p.at_z[off]
+        )
+
+    def end(self):
+        p = self.place
+        self.got_y(0)
+        for off in (1, 3, 2):
+            self.copies.arrive(self.from_z.at[off - 1], self.z_send.at[off - 1], self.z_recv.at[off - 1], p.at_z[off])
+
+        def body(a_ref, b_ref, c_ref, d_ref, e_ref, out_ref):
+            total = a_ref[...].astype(jnp.float32)
+            for ref in (b_ref, c_ref, d_ref, e_ref):
+                total = total + ref[...].astype(jnp.float32)
+            out_ref[...] = total
+            cols = total.shape[1]
+            self.squares[0:1, 0:cols] += jnp.sum(total * total, axis=0, keepdims=True)
+
+        mine = self.view(self.full, p.row)
+        pltpu.emit_pipeline(body, grid=(self.grid,), in_specs=[self.spec] * 5, out_specs=[self.spec])(
+            mine, self.from_y.at[0], self.from_z.at[0], self.from_z.at[1], self.from_z.at[2], self.owned
+        )
+
+
+def backward_kernel(
+    w_qkv, w_out, w_gu, w_down, attn_in, cot_full, ffn_in, qkv, heads, resid, gate, up, hidden, down_grad,
+    tokens, cot, gain, cosines, sines, seg_col, parent_col, seg_row,
+    mixed, d_tokens, own_qkv, own_out, own_gate, own_up, own_down, gain_out, square_out,
+    gate_grad, up_grad, out_back, heads_grad, proj_grad, gu_grad, out_grad, qkv_grad,
+    y_qkv, y_out, y_gate, y_up, y_down, s_qkv, s_out, s_gate, s_up, s_down, z_qkv, z_out, z_gate, z_up, z_down,
+    partial, from_core, from_x, mid, wide_buf, low_buf, near_buf, gain_buf, gain_sum, squares, key_sum, value_sum,
+    r_ysend, r_yrecv, r_zsend, r_zrecv, t_send, t_recv, t_keep, u_send, u_recv, l_sem,
+):
+    place = Place()
+    copies = Copies()
+    place.greet()
+
+    def row_block(full, r):
+        return full.at[rows_of(r, OWN), :]
+
+    def col_block(full, r):
+        return full.at[:, rows_of(r, OWN)]
+
+    def grad_sum(index, full, view, *refs):
+        sems = (r_ysend.at[index], r_yrecv.at[index], r_zsend.at[index], r_zrecv.at[index])
+        return GradSum(place, copies, full, view, *refs, squares, sems)
+
+    r_qkv = grad_sum(0, qkv_grad, row_block, y_qkv, s_qkv, z_qkv, own_qkv)
+    r_out = grad_sum(1, out_grad, col_block, y_out, s_out, z_out, own_out)
+    r_gate = grad_sum(2, gu_grad.at[0], row_block, y_gate, s_gate, z_gate, own_gate)
+    r_up = grad_sum(3, gu_grad.at[1], row_block, y_up, s_up, z_up, own_up)
+    r_down = grad_sum(4, down_grad, col_block, y_down, s_down, z_down, own_down)
+    a_back = [
+        TokenGather(place, copies, out_back, m * TREE, t_send.at[m], t_recv.at[m]) for m in range(MICRO)
+    ]
+
+    def token_sum(turn, m):
+        lands = 1 if turn == 1 else 0
+        return TokenSum(
+            place, copies, partial.at[m], from_core.at[lands, m], from_x.at[lands, m], u_send.at[turn, m], u_recv.at[turn, m]
+        )
+
+    ffn_sum = [token_sum(0, m) for m in range(MICRO)]
+    mlp_sum = [token_sum(1, m) for m in range(MICRO)]
+    attn_sum = [token_sum(2, m) for m in range(MICRO)]
+
+    def grad_hidden(m):
+        def body(c_ref, w_ref, gate_ref, up_ref, gate_out, up_out):
+            for part in range(TREE // OWN):
+                rows = slice(part * OWN, (part + 1) * OWN)
+                back = residual_mult * dot_nt(c_ref[rows, :], w_ref[...])
+                g = gate_ref[rows, :].astype(jnp.float32)
+                u = up_ref[rows, :].astype(jnp.float32)
+                act = jax.nn.sigmoid(g)
+                gate_out[rows, :] = (back * u * act * (1.0 + g * (1.0 - act))).astype(jnp.bfloat16)
+                up_out[rows, :] = (back * g * act).astype(jnp.bfloat16)
+
+        cols = pl.BlockSpec((TREE, 256), lambda j: (m, j))
+        pltpu.emit_pipeline(
+            body,
+            grid=(WIDE // 256,),
+            in_specs=[
+                pl.BlockSpec((TREE, D), lambda j: (m, 0)),
+                pl.BlockSpec((256, D), lambda j: (j, 0)),
+                cols,
+                cols,
+            ],
+            out_specs=[cols, cols],
+        )(cot_full, w_down, gate, up, gate_grad, up_grad)
+
+    def grad_weight(near_all, far_all, out, near_cols, far_cols):
+        def body(a_ref, b_ref, out_ref):
+            out_ref[...] = dot_tn(a_ref[...], b_ref[...]).astype(jnp.bfloat16)
+
+        step = min(256, near_cols)
+        pltpu.emit_pipeline(
+            body,
+            grid=(near_cols // step,),
+            in_specs=[
+                pl.BlockSpec((MICRO * TREE, step), lambda i: (0, i)),
+                pl.BlockSpec((MICRO * TREE, far_cols), lambda i: (0, 0)),
+            ],
+            out_specs=[pl.BlockSpec((step, far_cols), lambda i: (i, 0))],
+        )(near_all, far_all, out)
+
+    def back_ffn(m):
+        def body(step, g_ref, u_ref, wg_ref, wu_ref):
+            for part in range(TREE // OWN):
+                rows = slice(part * OWN, (part + 1) * OWN)
+                value = dot_nt(g_ref[rows, :], wg_ref[0]) + dot_nt(u_ref[rows, :], wu_ref[0])
+                partial[m, part, :, pl.ds(pl.multiple_of(step.index[0] * 256, 256), 256)] = value.astype(jnp.bfloat16)
+
+        tree = pl.BlockSpec((TREE, WIDE), lambda j: (m, 0))
+        pltpu.emit_pipeline(
+            body,
+            grid=(D // 256,),
+            in_specs=[
+                tree,
+                tree,
+                pl.BlockSpec((1, 256, WIDE), lambda j: (0, j, 0)),
+                pl.BlockSpec((1, 256, WIDE), lambda j: (1, j, 0)),
+            ],
+            out_specs=[],
+            _explicit_indices=True,
+        )(gate_grad, up_grad, w_gu, w_gu)
+
+    def down(m):
+        def body(step, h_ref, w_ref):
+            for part in range(TREE // OWN):
+                rows = slice(part * OWN, (part + 1) * OWN)
+                value = dot_nn(h_ref[rows, :], w_ref[...])
+                partial[m, part, :, pl.ds(pl.multiple_of(step.index[0] * 256, 256), 256)] = value.astype(jnp.bfloat16)
+
+        pltpu.emit_pipeline(
+            body,
+            grid=(D // 256,),
+            in_specs=[
+                pl.BlockSpec((TREE, WIDE), lambda j: (m, 0)),
+                pl.BlockSpec((WIDE, 256), lambda j: (0, j)),
+            ],
+            out_specs=[],
+            _explicit_indices=True,
+        )(hidden, w_down)
+
+    def back_heads(m):
+        def body(a_ref, w_ref, out_ref):
+            out_ref[...] = dot_nt(a_ref[...], w_ref[...]).astype(jnp.bfloat16)
+
+        steps = TREE // OWN
+        pltpu.emit_pipeline(
+            body,
+            grid=(steps,),
+            in_specs=[
+                pl.BlockSpec((OWN, D), lambda i: (m * steps + i, 0)),
+                pl.BlockSpec((512, D), lambda i: (0, 0)),
+            ],
+            out_specs=[pl.BlockSpec((OWN, 512), lambda i: (m * steps + i, 0))],
+        )(out_back, w_out, heads_grad)
+
+    def back_attention(m):
+        tree = pl.BlockSpec((TREE, 128), lambda g: (m, 0))
+        group = pl.BlockSpec((TREE, 384), lambda g: (m, g))
+        pltpu.emit_pipeline(
+            functools.partial(attend_back, key_sum, value_sum),
+            grid=(2,),
+            in_specs=[
+                group,
+                pl.BlockSpec((TREE, 256), lambda g: (m, g)),
+                tree,
+                tree,
+                tree,
+                tree,
+                pl.BlockSpec((8, TREE), lambda g: (m, 0)),
+            ],
+            out_specs=[group],
+        )(qkv, heads_grad, cosines, sines, seg_col, parent_col, seg_row, proj_grad)
+
+    def back_project(m):
+        def body(step, a_ref, w_ref):
+            partial[m, step.index[0]] = dot_nt(a_ref[...], w_ref[...]).astype(jnp.bfloat16)
+
+        steps = TREE // OWN
+        pltpu.emit_pipeline(
+            body,
+            grid=(steps,),
+            in_specs=[
+                pl.BlockSpec((OWN, 768), lambda i: (m * steps + i, 0)),
+                pl.BlockSpec((D, 768), lambda i: (0, 0)),
+            ],
+            out_specs=[],
+            _explicit_indices=True,
+        )(proj_grad, w_qkv)
+
+    def norm_back_rows(value, upstream, which):
+        row_gain = gain_buf[which : which + 1, :]
+        scale = lax.rsqrt(jnp.mean(value * value, axis=-1, keepdims=True) + norm_eps)
+        scaled = upstream * row_gain
+        inner = jnp.mean(scaled * value, axis=-1, keepdims=True)
+        gain_sum[which : which + 1, :] += jnp.sum(upstream * value * scale, axis=0, keepdims=True)
+        return scale * scaled - value * (scale * scale * scale * inner)
+
+    def middle_back(m):
+        ffn_sum[m].arrive()
+        load = copies.local(resid.at[m], wide_buf, l_sem.at[0])
+        load_low = copies.local(cot.at[m], low_buf, l_sem.at[1])
+        load.wait()
+        load_low.wait()
+
+        @pl.loop(0, OWN // 16)
+        def _(i):
+            rows = rows_of(i, 16)
+            back = norm_back_rows(wide_buf[rows, :], ffn_sum[m].rows(rows), 1)
+            value = low_buf[rows, :].astype(jnp.float32) + back
+            mid[m, rows, :] = value
+            near_buf[m, rows, :] = (residual_mult * value).astype(jnp.bfloat16)
+
+        a_back[m].start(near_buf.at[m], t_keep.at[m])
+
+    def finish_mixed(m):
+        mlp_sum[m].arrive()
+        load = copies.local(resid.at[m], wide_buf, l_sem.at[0])
+        load.wait()
+
+        @pl.loop(0, OWN // 16)
+        def _(i):
+            rows = rows_of(i, 16)
+            low_buf[rows, :] = (wide_buf[rows, :] + residual_mult * mlp_sum[m].rows(rows)).astype(jnp.bfloat16)
+
+        copies.local(low_buf, mixed.at[m], l_sem.at[1]).wait()
+
+    def finish_tokens(m):
+        attn_sum[m].arrive()
+        copies.local(tokens.at[m], low_buf, l_sem.at[1]).wait()
+
+        @pl.loop(0, OWN // 16)
+        def _(i):
+            rows = rows_of(i, 16)
+            back = norm_back_rows(low_buf[rows, :].astype(jnp.float32), attn_sum[m].rows(rows), 0)
+            mid[m, rows, :] = mid[m, rows, :] + back
+
+        return copies.local(mid.at[m], d_tokens.at[m], l_sem.at[2 + m])
+
+    def sent(part):
+        done = part.sent + [part.passed]
+        for copy in done:
+            copy.wait_send()
+        copies.open_sends = [copy for copy in copies.open_sends if not any(copy is gone for gone in done)]
+
+    r_down.start()
+    load_gain = copies.local(gain, gain_buf, l_sem.at[0])
+    gain_sum[...] = jnp.zeros_like(gain_sum)
+    squares[...] = jnp.zeros_like(squares)
+    load_gain.wait()
+    grad_hidden(0)
+    grad_hidden(1)
+    back_ffn(0)
+    ffn_sum[0].start()
+    r_down.middle(2)
+    back_ffn(1)
+    ffn_sum[1].start()
+    ffn_sum[0].middle()
+    r_down.middle(1)
+    grad_weight(ffn_in, gate_grad, gu_grad.at[0], D, WIDE)
+    r_gate.start()
+    ffn_sum[1].middle()
+    r_down.middle(3)
+    middle_back(0)
+    middle_back(1)
+    sent(ffn_sum[0])
+    down(0)
+    mlp_sum[0].start()
+    r_gate.middle(2)
+    a_back[0].relay()
+    a_back[1].relay()
+    sent(ffn_sum[1])
+    down(1)
+    mlp_sum[1].start()
+    mlp_sum[0].middle()
+    r_gate.middle(1)
+    grad_weight(ffn_in, up_grad, gu_grad.at[1], D, WIDE)
+    r_up.start()
+    mlp_sum[1].middle()
+    r_gate.middle(3)
+    a_back[0].finish()
+    back_heads(0)
+    back_attention(0)
+    finish_mixed(0)
+    sent(mlp_sum[0])
+    back_project(0)
+    attn_sum[0].start()
+    r_up.middle(2)
+    a_back[1].finish()
+    back_heads(1)
+    back_attention(1)
+    finish_mixed(1)
+    sent(mlp_sum[1])
+    back_project(1)
+    attn_sum[1].start()
+    attn_sum[0].middle()
+    grad_weight(attn_in, proj_grad, qkv_grad, D, 768)
+    r_qkv.start()
+    grad_weight(heads, out_back, out_grad, 512, D)
+    r_out.start()
+    r_up.middle(1)
+    attn_sum[1].middle()
+    r_up.middle(3)
+    r_down.end()
+    stores = [finish_tokens(0)]
+    for off in GradSum.ORDER:
+        r_qkv.middle(off)
+    stores.append(finish_tokens(1))
+    for off in GradSum.ORDER:
+        r_out.middle(off)
+    stores.append(copies.local(gain_sum, gain_out, l_sem.at[0]))
+    r_gate.end()
+    r_up.end()
+    r_qkv.end()
+    r_out.end()
+    stores.append(copies.local(squares, square_out, l_sem.at[1]))
+    for copy in stores:
+        copy.wait()
+    copies.close()
+
+
+def backward(saved, tokens, cot, gains, tables):
+    low = jnp.bfloat16
+    wide = jnp.float32
+    shape = jax.ShapeDtypeStruct
+    all_tokens = MICRO * TREE
+    blocks = [(OWN, 768), (512, OWN), (OWN, WIDE), (OWN, WIDE), (WIDE, OWN)]
+    outs = [shape((MICRO, OWN, D), low), shape((MICRO, OWN, D), wide)]
+    outs += [shape(block, wide) for block in blocks]
+    outs += [shape((8, D), wide), shape((8, D), wide)]
+    outs += [
+        shape((all_tokens, WIDE), low), shape((all_tokens, WIDE), low), shape((all_tokens, D), low),
+        shape((all_tokens, 512), low), shape((all_tokens, 768), low),
+        shape((2, D, WIDE), low), shape((512, D), low), shape((D, 768), low),
+    ]
+    outs += [shape((NZ,) + block, low) for block in blocks]
+    outs += [shape((NZ - 1,) + block, low) for block in blocks]
+    outs += [shape((NZ - 1,) + block, low) for block in blocks]
+    dma = pltpu.SemaphoreType.DMA
+    return pl.pallas_call(
+        backward_kernel,
+        out_shape=outs,
+        in_specs=[HBM] * 22,
+        out_specs=[HBM] * len(outs),
+        scratch_shapes=[
+            pltpu.VMEM((MICRO, NX * NC, OWN, D), low),
+            pltpu.VMEM((2, MICRO, NX, OWN, D), low),
+            pltpu.VMEM((2, MICRO, OWN, D), low),
+            pltpu.VMEM((MICRO, OWN, D), wide),
+            pltpu.VMEM((OWN, D), wide),
+            pltpu.VMEM((OWN, D), low),
+            pltpu.VMEM((MICRO, OWN, D), low),
+            pltpu.VMEM((2, D), wide),
+            pltpu.VMEM((8, D), wide),
+            pltpu.VMEM((8, D), wide),
+            pltpu.VMEM((TREE, 128), wide),
+            pltpu.VMEM((TREE, 128), wide),
+            dma((5, NZ)), dma((5, NZ)), dma((5, NZ)), dma((5, NZ)),
+            dma((MICRO, 3)), dma((MICRO, NX * NC)), dma((MICRO,)),
+            dma((3, MICRO, 3)), dma((3, MICRO, 3)), dma((4,)),
+        ],
+        compiler_params=pltpu.CompilerParams(
+            collective_id=1, has_side_effects=True, vmem_limit_bytes=63 * 1024 * 1024
+        ),
+        cost_estimate=pl.CostEstimate(flops=140 * 10**9, bytes_accessed=5 * 10**8, transcendentals=10**7),
+        name="backward",
+    )(*saved, tokens, cot, gains, *tables)
+
+
 def fast_local(
     tokens,
     cotangent,
@@ -906,131 +1362,19 @@
 ):
     low = jnp.bfloat16
     tables = [position_tables(segment_of[m], leaf_parent[m]) for m in range(MICRO)]
-    cos_all, sin_all, seg_col, parent_col, seg_row = (
-        jnp.concatenate([table[i] for table in tables], axis=0) for i in range(5)
-    )
-    wide = tokens.astype(jnp.float32)
-    near, scales = normalize(wide, gains[0])
-    (w_a, w_b, w_c, w_d, attn_all, cot_all, ffn_all, qkv_all, heads_all, resid_all, gate_all, up_all, hidden_all, down_all) = forward(
+    tables = [jnp.concatenate([table[i] for table in tables], axis=0) for i in range(5)]
+    near, _ = normalize(tokens.astype(jnp.float32), gains[0])
+    saved = forward(
         near.astype(low), tokens, cotangent,
         w_qkv.astype(low).reshape(OWN, 768), w_out.astype(low), w_gu.astype(low), w_down.astype(low),
-        gains, cos_all, sin_all, seg_col, parent_col, seg_row,
+        gains, *tables,
     )
-    w_a = w_a.reshape(D, 2, 384)
-    groups = 2
-    tree_len = TREE
-    row_count = OWN
-    outputs = []
-    input_grads = []
-    unsummed = None
-    gain_partial = None
-    for batch_index in range(MICRO):
-        span = slice(batch_index * TREE, (batch_index + 1) * TREE)
-        allowed, cosines, sines = tree_tables(segment_of[batch_index], leaf_parent[batch_index])
-        x_local = wide[batch_index]
-        scale_a = scales[batch_index]
-        attn_in, cot_full, ffn_in, hidden, mixed_heads = attn_all[span], cot_all[span], ffn_all[span], hidden_all[span], heads_all[span]
-        gate_up = jnp.stack([gate_all[span], up_all[span]], axis=1).astype(jnp.float32)
-        gate_act = jax.nn.sigmoid(gate_up[:, 0])
-        silu_gate = gate_up[:, 0] * gate_act
-        residual_mid = resid_all[batch_index]
-        normed_b, scale_b = normalize(residual_mid, gains[1])
-        packed = qkv_all[span].reshape(tree_len, groups, 384)
-        queries = packed[:, :, :256].reshape(tree_len, groups, GROUP, HD)
-        key_heads, values = packed[:, :, 256:320], packed[:, :, 320:]
-        scores = jnp.einsum("tkgh,skh->kgts", queries, key_heads, preferred_element_type=jnp.float32)
-        logits = jnp.where(allowed, score_mult * scores, masked_value)
-        row_peak = jnp.max(logits, axis=-1, keepdims=True)
-        log_total = row_peak + jnp.log(jnp.sum(jnp.exp(logits - row_peak), axis=-1, keepdims=True))
-
-        def down_terms(first_row, row_total):
-            return jnp.dot(hidden, w_d, preferred_element_type=jnp.float32)
-
-        mlp_sum = sum_forward(down_terms, row_count)
-        outputs.append((residual_mid + residual_mult * mlp_sum).astype(jnp.bfloat16))
-        hidden_grad = residual_mult * jnp.einsum(
-            "td,fd->tf", cot_full, w_d, preferred_element_type=jnp.float32
-        )
-        gate_grad = (
-            hidden_grad * gate_up[:, 1] * gate_act * (1.0 + gate_up[:, 0] * (1.0 - gate_act))
-        )
-        up_grad = hidden_grad * silu_gate
-        gate_up_grad = jnp.stack([gate_grad, up_grad], axis=1).astype(jnp.bfloat16)
-        gu_grad = jnp.einsum(
-            "td,tef->edf", ffn_in, gate_up_grad, preferred_element_type=jnp.float32
-        )
-
-        def ffn_back_terms(first_row, row_total):
-            return jnp.einsum("tef,edf->td", gate_up_grad, w_c, preferred_element_type=jnp.float32)
-
-        ffn_in_grad = sum_backward(ffn_back_terms, row_count)
-        mid_norm_grad, gain_b_grad = norm_back(residual_mid, scale_b, gains[1], ffn_in_grad)
-        mid_grad = cotangent[batch_index].astype(jnp.float32) + mid_norm_grad
-        attn_out_grad = gather_backward((residual_mult * mid_grad).astype(jnp.bfloat16))
-        out_grad = jnp.einsum(
-            "tf,td->fd", mixed_heads, attn_out_grad, preferred_element_type=jnp.float32
-        )
-        heads_grad = (
-            jnp.einsum("td,fd->tf", attn_out_grad, w_b, preferred_element_type=jnp.float32)
-            .astype(jnp.bfloat16)
-            .reshape(tree_len, groups, GROUP, HD)
-        )
-        attn_probs = jnp.exp(logits - log_total)
-        prob_grad = jnp.einsum(
-            "tkgh,skh->kgts", heads_grad, values, preferred_element_type=jnp.float32
-        )
-        row_inner = jnp.sum(prob_grad * attn_probs, axis=-1, keepdims=True)
-        score_grad = (score_mult * attn_probs * (prob_grad - row_inner)).astype(jnp.bfloat16)
-        query_grad = jnp.einsum(
-            "kgts,skh->tkgh", score_grad, key_heads, preferred_element_type=jnp.float32
-        )
-        key_grad = jnp.einsum(
-            "kgts,tkgh->skh", score_grad, queries, preferred_element_type=jnp.float32
-        )
-        value_grad = jnp.einsum(
-            "kgts,tkgh->skh",
-            attn_probs.astype(jnp.bfloat16),
-            heads_grad,
-            preferred_element_type=jnp.float32,
-        )
-        query_grad = rotate(query_grad, cosines[:, None, None, :], -sines[:, None, None, :])
-        key_grad = rotate(key_grad, cosines[:, None, :], -sines[:, None, :])
-        proj_grad = jnp.concatenate(
-            [query_grad.reshape(tree_len, groups, GROUP * HD), key_grad, value_grad], axis=-1
-        ).astype(jnp.bfloat16)
-        qkv_grad = jnp.einsum("td,tkf->dkf", attn_in, proj_grad, preferred_element_type=jnp.float32)
-
-        def attn_back_terms(first_row, row_total):
-            return jnp.einsum("tkf,dkf->td", proj_grad, w_a, preferred_element_type=jnp.float32)
-
-        attn_in_grad = sum_backward(attn_back_terms, row_count)
-        input_norm_grad, gain_a_grad = norm_back(x_local, scale_a, gains[0], attn_in_grad)
-        input_grads.append(mid_grad + input_norm_grad)
-        gain_step = jnp.stack([gain_a_grad, gain_b_grad])
-        gain_partial = gain_step if gain_partial is None else gain_partial + gain_step
-        partials = (qkv_grad, out_grad, gu_grad)
-        unsummed = (
-            partials
-            if unsummed is None
-            else tuple((running + addend for running, addend in zip(unsummed, partials)))
-        )
-    owned = (
-        lax.psum_scatter(
-            unsummed[0].astype(jnp.bfloat16), "row", scatter_dimension=0, tiled=True
-        ).astype(jnp.float32),
-        lax.psum_scatter(
-            unsummed[1].astype(jnp.bfloat16), "row", scatter_dimension=1, tiled=True
-        ).astype(jnp.float32),
-        lax.psum_scatter(
-            unsummed[2].astype(jnp.bfloat16), "row", scatter_dimension=1, tiled=True
-        ).astype(jnp.float32),
-        lax.psum_scatter(
-            down_all, "row", scatter_dimension=1, tiled=True
-        ).astype(jnp.float32),
-    )
-    local_squares = jnp.float32(0.0)
-    for grad_piece in owned:
-        local_squares = local_squares + jnp.sum(grad_piece * grad_piece)
+    mixed, d_tokens, g_qkv, g_out, g_gate, g_up, g_down, gain_rows, squares = backward(
+        saved, tokens, cotangent, gains, tables
+    )[:9]
+    owned = (g_qkv.reshape(w_qkv.shape), g_out, jnp.stack([g_gate, g_up]), g_down)
+    local_squares = jnp.sum(squares[0])
+    gain_partial = gain_rows[:2]
     total_squares, gain_total = lax.psum((local_squares, gain_partial), ("row", "col"))
     grad_norm = jnp.sqrt(total_squares + jnp.sum(gain_total * gain_total))
     factor = jnp.minimum(1.0, clip_bound() / (grad_norm + 1e-06))
@@ -1044,8 +1388,6 @@
         )
         results.append((updated, moments, updated.astype(jnp.bfloat16)))
     new_gains, moments_gains = adamw(gains, mom_gains, gain_total, factor, rates[4])
-    mixed = jnp.stack(outputs, axis=0)
-    d_tokens = jnp.stack(input_grads, axis=0)
     return (
         mixed,
         d_tokens,

time: 1650 us -> 1020 us (0.62)
  Pallas kernels: 451 us -> 897 us
  waiting for transfers between devices: 441 us -> 0 us
  matrix products: 369 us -> 0 us
  other arithmetic: 202 us -> 51.1 us
  local copies, waits for them, and re-layouts: 115 us -> 15.7 us
  between operations: 21.8 us -> 3.91 us
    pallas_call x0 -> x1, Pallas kernels: none -> 446 us  [backward(): pl.pallas_call(backward_kernel, out_shape=outs, in_specs=[HBM] * 22, out_...]
    reduce_scatter x10 -> x0, waiting for transfers between devices: 439 us -> none  [the longest x1 276 us: fast_local(): lax.psum_scatter(unsummed[2].astype(jnp.bfloat16), 'row', scatter_dimensi...]
    dot_general x28 -> x0, matrix products: 369 us -> none  [the longest x2 54.8 us: fast_local(): jnp.einsum('td,tef->edf', ffn_in, gate_up_grad, preferred_element_type=jn...]
    convert_element_type x8 -> x2, other arithmetic: 83.7 us -> 0.01 us  [position_tables(): angles = depth.astype(jnp.float32)[:, None] * freqs[None, :]]
    unnamed x182 -> x45, local copies, waits for them, and re-layouts: 53.2 us -> 8.53 us
    reduce_sum x8 -> x1, other arithmetic: 45.3 us -> 1.61 us  [fast_local(): local_squares = jnp.sum(squares[0])]
    slice x13 -> x3, local copies, waits for them, and re-layouts: 22.5 us -> 0.85 us  [the longest x1 0.84 us: fast_local(): gain_partial = gain_rows[:2]]
  transfers between devices with their start and end apart: 12 -> 0, of which waited for: 5 -> 0; matrix products, arithmetic and copies ran while one was open for 32% -> 0% of each run, Pallas kernels for 0% -> 0%
where the time goes in v2:
time: 1020 us; the launch traced here: 1010 us
  Pallas kernels  897 us (88%)
  other arithmetic  51.1 us (5%)
  blocking collectives  45 us (4%)
  local copies, waits for them, and re-layouts  15.7 us (2%)
    pallas_call x1, Pallas kernels, forward(): pl.pallas_call(forward_kernel, out_shape=outs, in_specs=[HBM] * 13, out_s...  451 us
    pallas_call x1, Pallas kernels, backward(): pl.pallas_call(backward_kernel, out_shape=outs, in_specs=[HBM] * 22, out_...  446 us
    psum x1, blocking collectives, fast_local(): lax.psum((local_squares, gain_partial), ('row', 'col'))  45 us

profile of v2, /device:TPU:0, one launch (start us, length us, event | category | flops | bytes accessed | tf_op | source)
XLA Modules:
  0.0 1012.7 jit_solution(9979341304082784831)
XLA Ops:
  2.4 2.1 fusion
  7.5 1.8 convert_element_type.93.own_out
  9.2 1.4 convert_element_type.92
  11.4 1.3 broadcast.150.parent_col
  12.8 1.3 broadcast.149.seg_col
  14.1 1.1 convert_element_type.95.own_down
  15.1 1.9 fusion.2.near
  17.0 1.6 convert_element_type.94.own_gu
  18.6 3.7 fusion.20
  22.4 1.9 maximum_maximum_fusion.1.sines
  24.2 1.8 maximum_maximum_fusion.cosines
  26.1 451.0 %forward.1 = (bf16[2048,768]{1,0:T(8,128)(2,1)}, bf16[512,2048]{1,0:T(8,128)(2,1)}, bf16[2,2048,2048]{2,1,0:T(8,128)(2,1)}, bf16[2048,2048]{1,0:T(8,128)(2,1)}, ...) custom-call(bf16[2,256,2048]{2,1,0:T(8,128)(2,1)} %fusion.2.near, ...), custom_call_target="tpu_custom_call" | custom-call | flops 89999998976 | bytes 200000000 | tf_op jit(solution)/shard_map/forward/pallas_call | solution.py:916
  477.1 445.9 %backward.1 = (bf16[2,256,2048]{2,1,0:T(8,128)(2,1)}, f32[2,256,2048]{2,1,0:T(8,128)}, f32[256,768]{1,0:T(8,128)}, f32[512,256]{1,0:T(8,128)}, f32[256,2048]{1,0...) custom-call(bf16[2048,768]{1,0:T(8,128)(2,1)} %get-tuple-element.40., ...), custom_call_target="tpu_custom_call" | custom-call | flops 140000002048 | bytes 500000000 | tf_op jit(solution)/shard_map/backward/pallas_call | solution.py:1317
  923.0 1.6 slice_reduce_fusion
  925.5 45.0 %all-reduce.2 = (f32[]{:T(128)}, f32[2,2048]{1,0:T(2,128)S(1)}) all-reduce(f32[]{:T(128)} %slice_reduce_fusion, f32[2,2048]{1,0:T(2,128)S(1)} %slice.75), channel_id=1, replica_groups=mesh['row'=8,'col'=4] {'row','col'}, use_global_device_ids=true, to_apply=%region_12.13 | all-reduce | flops 4097 | bytes 32776 | tf_op jit(solution)/shard_map/psum | solution.py:1378
  972.5 1.2 broadcast_multiply_fusion
  975.1 1.3 mul.433
  976.3 1.3 mul.421
  977.6 4.2 fusion.32
  981.8 1.1 add_multiply_fusion.1
  983.0 1.9 pad_maximum_fusion.2
  984.8 1.3 multiply_bitcast_fusion.1
  986.1 1.0 pad_maximum_fusion.3
  987.3 3.3 multiply_bitcast_fusion
  990.6 2.4 pad_maximum_fusion.1
  993.0 1.3 copy-done.1
  995.5 4.7 fusion.30
  1000.3 1.8 add_multiply_fusion
  1002.1 4.0 pad_maximum_fusion
  1006.1 1.3 copy.36
  1007.5 1.6 copy-done.9
  1009.1 2.0 copy.37
  (81 shorter events, 9.7 us)
Async XLA Ops:
  0.7 13.4 %copy-start.4 = (f32[2048,256]{1,0:T(8,128)S(1)}, f32[2048,256]{1,0:T(8,128)}, u32[]{:S(2)}) copy-start(f32[2048,256]{1,0:T(8,128)} %param.24) | copy-start | bytes 6291460
  5.3 9.8 slice-start.2
  6.2 8.9 copy-start.6
  12.8 4.3 copy-start
  477.1 496.7 %copy-start.17 = (f32[2,2048]{1,0:T(2,128)S(1)}, f32[2,2048]{1,0:T(2,128)}, u32[]{:S(2)}) copy-start(f32[2,2048]{1,0:T(2,128)} %gain.3) | copy-start | bytes 49156
  477.1 496.7 %copy-start.18 = (f32[2,2,2048]{2,1,0:T(2,128)S(1)}, f32[2,2,2048]{2,1,0:T(2,128)}, u32[]{:S(2)}) copy-start(f32[2,2,2048]{2,1,0:T(2,128)} %param.27) | copy-start | bytes 98308
  923.0 54.6 %copy-start.7 = (f32[2,256,2,384]{3,2,1,0:T(2,128)S(1)}, f32[2,256,2,384]{3,2,1,0:T(2,128)}, u32[]{:S(2)}) copy-start(f32[2,256,2,384]{3,2,1,0:T(2,128)} %param.19) | copy-start | bytes 4718596
  923.0 54.6 %copy-start.10 = (f32[256,2,384]{2,1,0:T(2,128)S(1)}, f32[256,2,384]{2,1,0:T(2,128)}, u32[]{:S(2)}) copy-start(f32[256,2,384]{2,1,0:T(2,128)} %param.18) | copy-start | bytes 2359300
  977.6 4.2 copy-start.11
  981.8 3.0 copy-start.13
  981.8 3.0 copy-start.15
  981.8 3.0 copy-start.16
  982.9 4.2 copy-start.5
  982.9 4.2 copy-start.8
  982.9 4.3 copy-start.12
  986.1 6.8 slice-start
  987.3 5.7 slice-start.1
  990.6 3.7 copy-start.1
  990.6 4.4 copy-start.2
  990.6 5.0 copy-start.3
  1002.1 4.0 copy-start.14
  1006.1 2.9 copy-start.9

commit v3 on v2

--- a/solution.py
+++ b/solution.py
@@ -425,6 +425,8 @@
         self.col_c = self.x * NC + (1 - self.c)
         self.col_xc = (1 - self.x) * NC + (1 - self.c)
         self.at_z = [None] + [(self.row_z[off], col) for off in range(1, NZ)]
+        self.at_up = (lax.rem(row + NY, NZ * NY), col)
+        self.at_down = (lax.rem(row + (NZ - 1) * NY, NZ * NY), col)
         self.at_y = (self.row_y, col)
         self.at_x = (row, self.col_x)
         self.at_c = (row, self.col_c)
@@ -441,30 +443,43 @@
     def __init__(self):
         self.open_sends = []
 
-    def send(self, src, dst, send_sem, recv_sem, device):
+    def send(self, src, dst, send_sem, recv_sem, device, when=True):
         copy = pltpu.make_async_remote_copy(
             src_ref=src, dst_ref=dst, send_sem=send_sem, recv_sem=recv_sem,
             device_id=device, device_id_type=MESH,
         )
-        copy.start()
-        self.open_sends.append(copy)
+        if when is True:
+            copy.start()
+        else:
+            pl.when(when)(copy.start)
+        self.open_sends.append((copy, when))
         return copy
 
-    def arrive(self, dst, send_sem, recv_sem, device):
-        pltpu.make_async_remote_copy(
+    def arrive(self, dst, send_sem, recv_sem, device, when=True):
+        copy = pltpu.make_async_remote_copy(
             src_ref=dst, dst_ref=dst, send_sem=send_sem, recv_sem=recv_sem,
             device_id=device, device_id_type=MESH,
-        ).wait_recv()
+        )
+        if when is True:
+            copy.wait_recv()
+        else:
+            pl.when(when)(copy.wait_recv)
 
     def local(self, src, dst, sem):
         copy = pltpu.make_async_copy(src, dst, sem)
         copy.start()
         return copy
 
-    def close(self):
-        for copy in self.open_sends:
-            copy.wait_send()
-        self.open_sends = []
+    def close(self, some=None):
+        left = []
+        for copy, when in self.open_sends:
+            if some is not None and not any(copy is one for one in some):
+                left.append((copy, when))
+            elif when is True:
+                copy.wait_send()
+            else:
+                pl.when(when)(copy.wait_send)
+        self.open_sends = left
 
 
 def rows_of(index, size):
@@ -472,31 +487,65 @@
 
 
 class WeightGather:
-    def __init__(self, place, copies, own, full, view, send, recv, keep):
+    def __init__(self, place, copies, own, full, view, send, recv, keep, over_y_first):
         self.place, self.copies, self.own, self.full, self.view = place, copies, own, full, view
         self.send, self.recv, self.keep = send, recv, keep
-
-    def start(self):
+        self.sides = (place.y, 1 - place.y) if over_y_first else (place.y,)
+        self.over_y_first = over_y_first
+
+    def block(self, r):
+        return self.view(self.full, r)
+
+    def pass_on(self, src, r, up, down, over_y):
         p = self.place
-        here = self.view(self.full, p.row)
-        self.kept = self.copies.local(self.own, here, self.keep)
-        for off in (1, 3, 2):
-            self.copies.send(self.own, here, self.send.at[off - 1], self.recv.at[p.row], p.at_z[off])
-        self.copies.send(self.own, here, self.send.at[3], self.recv.at[p.row], p.at_y)
-
-    def relay(self):
+        here = self.block(r)
+        if up is not None:
+            self.copies.send(src, here, self.send.at[0, r], self.recv.at[r], p.at_up, up)
+        if down is not None:
+            self.copies.send(src, here, self.send.at[1, r], self.recv.at[r], p.at_down, down)
+        if over_y is not None:
+            self.copies.send(src, here, self.send.at[2, r], self.recv.at[r], p.at_y, over_y)
+
+    def start_y(self):
         p = self.place
-        for off in (1, 3, 2):
-            block = self.view(self.full, p.row_z[off])
-            self.copies.arrive(block, self.send.at[3 + off], self.recv.at[p.row_z[off]], p.at_y)
-            self.copies.send(block, block, self.send.at[3 + off], self.recv.at[p.row_z[off]], p.at_y)
+        self.kept = self.copies.local(self.own, self.block(p.row), self.keep)
+        self.pass_on(self.own, p.row, None, None, True)
+
+    def start_z(self):
+        p = self.place
+        self.pass_on(self.own, p.row, p.z < NZ - 1, p.z > 0, None)
+
+    def arrive(self, r, when=True):
+        self.copies.arrive(self.block(r), self.send.at[2, r], self.recv.at[r], self.place.at_y, when)
+
+    def relay_y(self):
+        p = self.place
+        self.arrive(p.row_y)
+        self.pass_on(self.block(p.row_y), p.row_y, p.z < NZ - 1, p.z > 0, None)
+
+    def relay(self, k):
+        p = self.place
+        for there, upward in ((p.z - k, True), (p.z + k, False)):
+            came = there >= 0 if upward else there < NZ
+            safe = lax.rem(there + NZ, NZ)
+            for side in self.sides:
+                r = safe * NY + side
+                self.arrive(r, came)
+                on = jnp.logical_and(came, p.z < NZ - 1) if upward else jnp.logical_and(came, p.z > 0)
+                self.pass_on(
+                    self.block(r), r, on if upward else None, None if upward else on, None if self.over_y_first else came
+                )
 
     def finish(self):
-        p = self.place
-        for off in range(NZ):
-            block = self.view(self.full, p.row_yz[off])
-            self.copies.arrive(block, self.send.at[3], self.recv.at[p.row_yz[off]], p.at_y)
+        if not self.over_y_first:
+            for off in range(NZ):
+                self.arrive(self.place.row_yz[off])
+        if self.kept is not None:
+            self.keep_own()
+
+    def keep_own(self):
         self.kept.wait()
+        self.kept = None
 
 
 class TokenGather:
@@ -528,8 +577,8 @@
 
 
 class TokenSum:
-    def __init__(self, place, copies, partial, from_core, from_x, send, recv):
-        self.place, self.copies, self.partial = place, copies, partial
+    def __init__(self, place, copies, blocks, away, mine, from_core, from_x, send, recv):
+        self.place, self.copies, self.blocks, self.away, self.mine = place, copies, blocks, away, mine
         self.from_core, self.from_x, self.send, self.recv = from_core, from_x, send, recv
 
     def start(self):
@@ -538,7 +587,7 @@
         for there in range(NX):
             self.sent.append(
                 self.copies.send(
-                    self.partial.at[there * NC + (1 - p.c)], self.from_core.at[there],
+                    self.blocks(there * NC + (1 - p.c)), self.from_core.at[there],
                     self.send.at[there], self.recv.at[there], p.at_c,
                 )
             )
@@ -547,19 +596,16 @@
         p = self.place
         for there in range(NX):
             self.copies.arrive(self.from_core.at[there], self.send.at[there], self.recv.at[there], p.at_c)
-        away = 1 - p.x
+        other = 1 - p.x
 
         @pl.loop(0, OWN // 32)
         def _(i):
             rows = rows_of(i, 32)
-            self.partial[p.col_x, rows, :] = (
-                self.partial[p.col_x, rows, :].astype(jnp.float32)
-                + self.from_core[away, rows, :].astype(jnp.float32)
+            self.away[rows, :] = (
+                self.away[rows, :].astype(jnp.float32) + self.from_core[other, rows, :].astype(jnp.float32)
             ).astype(jnp.bfloat16)
 
-        self.passed = self.copies.send(
-            self.partial.at[p.col_x], self.from_x, self.send.at[2], self.recv.at[2], p.at_x
-        )
+        self.sent.append(self.copies.send(self.away, self.from_x, self.send.at[2], self.recv.at[2], p.at_x))
 
     def arrive(self):
         p = self.place
@@ -568,7 +614,7 @@
     def rows(self, rows):
         p = self.place
         return (
-            self.partial[p.own, rows, :].astype(jnp.float32)
+            self.mine[rows, :].astype(jnp.float32)
             + self.from_core[p.x, rows, :].astype(jnp.float32)
             + self.from_x[rows, :].astype(jnp.float32)
         )
@@ -608,12 +654,13 @@
     for score in scores:
         top = jnp.max(score, axis=-1, keepdims=True)
         peak = top if peak is None else jnp.maximum(peak, top)
-    exps = [jnp.exp((score - peak) * score_mult) for score in scores]
+    peak = peak * score_mult
+    exps = [jnp.exp(score * score_mult - peak) for score in scores]
     total = None
     for term in exps:
         part = jnp.sum(term, axis=-1, keepdims=True)
         total = part if total is None else total + part
-    return exps, 1.0 / total
+    return exps, total, peak + jnp.log(total)
 
 
 def stacked_pairs(tile_ref, rows):
@@ -648,25 +695,30 @@
     return scores
 
 
-def attend(qkv_ref, seg_col_ref, parent_col_ref, seg_row_ref, heads_ref):
+def attend(qkv_ref, seg_col_ref, parent_col_ref, seg_row_ref, heads_ref, log_ref):
     seg_row = seg_row_ref[...]
     keys, values = twice(qkv_ref[:, 256:384])
     for run in range(TREE // SEG):
         rows = slice(run * SEG, (run + 1) * SEG)
         parts = masked_parts(run, seg_col_ref, parent_col_ref, seg_row)
-        exps, inverse = softmax_parts(score_parts(stacked_pairs(qkv_ref, rows), keys, parts))
+        exps, total, log_total = softmax_parts(score_parts(stacked_pairs(qkv_ref, rows), keys, parts))
         mixed = None
         for (span, _), term in zip(parts, exps):
-            got = dot_nn((term * inverse).astype(jnp.bfloat16), values[span])
+            got = dot_nn(term.astype(jnp.bfloat16), values[span])
             mixed = got if mixed is None else mixed + got
-        low = unstack_pairs(mixed).astype(jnp.bfloat16)
+        low = unstack_pairs(mixed * (1.0 / total)).astype(jnp.bfloat16)
         heads_ref[rows, 0:128] = low[0:SEG]
         heads_ref[rows, 128:256] = low[SEG:]
+        log_ref[run * 4 * SEG : (run + 1) * 4 * SEG, :] = jnp.broadcast_to(log_total, (4 * SEG, 128))
 
 
 def attend_back(
-    key_sum, value_sum, qkv_ref, grad_ref, cos_ref, sin_ref, seg_col_ref, parent_col_ref, seg_row_ref, out_ref
+    key_sum, value_sum, grad_buf, back_ref, w_ref, heads_ref, log_ref, qkv_ref, cos_ref, sin_ref, seg_col_ref,
+    parent_col_ref, seg_row_ref, out_ref,
 ):
+    for part in range(TREE // OWN):
+        rows = slice(part * OWN, (part + 1) * OWN)
+        grad_buf[rows, :] = dot_nt(back_ref[rows, :], w_ref[...]).astype(jnp.bfloat16)
     seg_row = seg_row_ref[...]
     keys, values = twice(qkv_ref[:, 256:384])
     key_sum[...] = jnp.zeros_like(key_sum)
@@ -675,27 +727,25 @@
         rows = slice(run * SEG, (run + 1) * SEG)
         parts = masked_parts(run, seg_col_ref, parent_col_ref, seg_row)
         queries = stacked_pairs(qkv_ref, rows)
-        upstream = stacked_pairs(grad_ref, rows)
-        exps, inverse = softmax_parts(score_parts(queries, keys, parts))
-        probs = [term * inverse for term in exps]
-        prob_grads = [dot_nt(upstream, values[span]) for span, _ in parts]
-        inner = None
-        for prob, prob_grad in zip(probs, prob_grads):
-            term = jnp.sum(prob * prob_grad, axis=-1, keepdims=True)
-            inner = term if inner is None else inner + term
+        upstream = stacked_pairs(grad_buf, rows)
+        mixed = stacked_pairs(heads_ref, rows)
+        inner = jnp.sum(upstream.astype(jnp.float32) * mixed.astype(jnp.float32), axis=-1, keepdims=True)
+        log_total = log_ref[run * 4 * SEG : (run + 1) * 4 * SEG, 0:1]
         query_grad = None
-        for (span, _), prob, prob_grad in zip(parts, probs, prob_grads):
-            score_grad = (score_mult * prob * (prob_grad - inner)).astype(jnp.bfloat16)
+        for (span, _), score in zip(parts, score_parts(queries, keys, parts)):
+            prob = jnp.exp(score * score_mult - log_total)
+            prob_grad = dot_nt(upstream, values[span])
+            score_grad = (prob * (prob_grad - inner)).astype(jnp.bfloat16)
             term = dot_nn(score_grad, keys[span])
             query_grad = term if query_grad is None else query_grad + term
             key_sum[span, :] += dot_tn(score_grad, queries)
             value_sum[span, :] += dot_tn(prob.astype(jnp.bfloat16), upstream)
-        pair_grad = unstack_pairs(query_grad)
+        pair_grad = unstack_pairs(query_grad) * score_mult
         cos, sin = cos_ref[rows, :], sin_ref[rows, :]
         for tile in range(2):
             part = pair_grad[tile * SEG : (tile + 1) * SEG]
             out_ref[rows, tile * 128 : (tile + 1) * 128] = (part * cos - swap_halves(part) * sin).astype(jnp.bfloat16)
-    key_grad = key_sum[...]
+    key_grad = key_sum[...] * score_mult
     key_grad = key_grad + pltpu.roll(key_grad, HD, 1)
     value_grad = value_sum[...]
     value_grad = value_grad + pltpu.roll(value_grad, HD, 1)
@@ -705,14 +755,21 @@
 
 
 def forward_kernel(
-    near, tokens, cot, own_qkv, own_out, own_gu, own_down, gain, cosines, sines,
-    seg_col, parent_col, seg_row,
-    w_qkv, w_out, w_gu, w_down, attn_in, cot_full, ffn_in, qkv, heads, resid, gate, up, hidden, down_grad,
-    partial, from_core, from_x, resid_buf, normed_buf, tokens_buf, gain_buf,
+    tokens, cot, own_qkv, own_out, own_gu, own_down, gain, cosines, sines, seg_col, parent_col, seg_row,
+    w_qkv, w_out, w_gu, w_down, attn_in, cot_full, ffn_in, qkv, heads, log_sums, resid, gate, up, hidden, down_grad,
+    down_out,
+    partial, from_core, from_x, normed_buf, tokens_buf, cot_buf, near_buf, gain_buf,
+    wide_qkv, wide_out, wide_gu, wide_down, low_qkv, low_out, low_gu, low_down,
     w_send, w_recv, w_keep, t_send, t_recv, t_keep, s_send, s_recv, l_sem,
 ):
+    resid_buf = wide_gu
     place = Place()
     copies = Copies()
+    pairs = (
+        (own_qkv, wide_qkv), (tokens, tokens_buf), (gain, gain_buf), (own_out, wide_out),
+        (own_gu, wide_gu), (cot, cot_buf), (own_down, wide_down),
+    )
+    loads = [copies.local(src, dst, l_sem.at[i]) for i, (src, dst) in enumerate(pairs)]
     place.greet()
 
     def row_block(full, r):
@@ -721,16 +778,16 @@
     def col_block(full, r):
         return full.at[:, rows_of(r, OWN)]
 
-    def weight(index, own, full, view):
+    def weight(index, own, full, view, over_y_first):
         return WeightGather(
-            place, copies, own, full, view, w_send.at[index], w_recv.at[index], w_keep.at[index]
-        )
-
-    g_qkv = weight(0, own_qkv, w_qkv, row_block)
-    g_out = weight(1, own_out, w_out, col_block)
-    g_gate = weight(2, own_gu.at[0], w_gu.at[0], row_block)
-    g_up = weight(3, own_gu.at[1], w_gu.at[1], row_block)
-    g_down = weight(4, own_down, w_down, col_block)
+            place, copies, own, full, view, w_send.at[index], w_recv.at[index], w_keep.at[index], over_y_first
+        )
+
+    g_qkv = weight(0, low_qkv, w_qkv, row_block, True)
+    g_out = weight(1, low_out, w_out, col_block, True)
+    g_gate = weight(2, low_gu.at[0], w_gu.at[0], row_block, False)
+    g_up = weight(3, low_gu.at[1], w_gu.at[1], row_block, False)
+    g_down = weight(4, low_down, w_down, col_block, False)
 
     def token_gather(index, full, m):
         return TokenGather(place, copies, full, m * TREE, t_send.at[index], t_recv.at[index])
@@ -739,7 +796,10 @@
     a_cot = [token_gather(2 + m, cot_full, m) for m in range(MICRO)]
     a_ffn = [token_gather(4 + m, ffn_in, m) for m in range(MICRO)]
     sums = [
-        TokenSum(place, copies, partial.at[m], from_core.at[m], from_x.at[m], s_send.at[m], s_recv.at[m])
+        TokenSum(
+            place, copies, functools.partial(lambda m, i: partial.at[m, i], m), partial.at[m, place.col_x],
+            partial.at[m, place.own], from_core.at[m], from_x.at[m], s_send.at[m], s_recv.at[m],
+        )
         for m in range(MICRO)
     ]
 
@@ -776,8 +836,11 @@
                 tree,
                 pl.BlockSpec((8, TREE), lambda g: (m, 0)),
             ],
-            out_specs=[pl.BlockSpec((TREE, 256), lambda g: (m, g))],
-        )(qkv, seg_col, parent_col, seg_row, heads)
+            out_specs=[
+                pl.BlockSpec((TREE, 256), lambda g: (m, g)),
+                pl.BlockSpec((4 * TREE, 128), lambda g: (m * 2 + g, 0)),
+            ],
+        )(qkv, seg_col, parent_col, seg_row, heads, log_sums)
 
     def out_project(m):
         def body_at(step, a_ref, w_ref):
@@ -795,23 +858,37 @@
             _explicit_indices=True,
         )(heads, w_out)
 
-    def middle_norm(m):
-        sums[m].arrive()
-        load = copies.local(tokens.at[m], tokens_buf, l_sem.at[0])
-        load_gain = copies.local(gain, gain_buf, l_sem.at[1])
-        load.wait()
-        load_gain.wait()
-
+    def lower(wide, low):
+        step = 64
+
+        @pl.loop(0, wide.shape[0] // step)
+        def _(i):
+            rows = rows_of(i, step)
+            low[rows, :] = wide[rows, :].astype(jnp.bfloat16)
+
+    def first_norm(m):
         @pl.loop(0, OWN // 32)
         def _(i):
             rows = rows_of(i, 32)
-            value = tokens_buf[rows, :].astype(jnp.float32) + residual_mult * sums[m].rows(rows)
+            value = tokens_buf[m, rows, :].astype(jnp.float32)
+            scale = lax.rsqrt(jnp.mean(value * value, axis=-1, keepdims=True) + norm_eps)
+            near_buf[m, rows, :] = (value * scale * gain_buf[0:1, :]).astype(jnp.bfloat16)
+
+        a_in[m].start(near_buf.at[m], t_keep.at[m])
+
+    def middle_norm(m):
+        sums[m].arrive()
+
+        @pl.loop(0, OWN // 32)
+        def _(i):
+            rows = rows_of(i, 32)
+            value = tokens_buf[m, rows, :].astype(jnp.float32) + residual_mult * sums[m].rows(rows)
             resid_buf[m, rows, :] = value
             scale = lax.rsqrt(jnp.mean(value * value, axis=-1, keepdims=True) + norm_eps)
             normed_buf[m, rows, :] = (value * scale * gain_buf[1:2, :]).astype(jnp.bfloat16)
 
         a_ffn[m].start(normed_buf.at[m], t_keep.at[4 + m])
-        return copies.local(resid_buf.at[m], resid.at[m], l_sem.at[2 + m])
+        return copies.local(resid_buf.at[m], resid.at[m], l_sem.at[m])
 
     def gate_up(m):
         def body(a_ref, g_ref, u_ref, gate_ref, up_ref, hidden_ref):
@@ -820,9 +897,11 @@
                 value = a_ref[rows, :]
                 g = dot_nn(value, g_ref[0])
                 u = dot_nn(value, u_ref[0])
-                gate_ref[rows, :] = g.astype(jnp.bfloat16)
-                up_ref[rows, :] = u.astype(jnp.bfloat16)
-                hidden_ref[rows, :] = (g * jax.nn.sigmoid(g) * u).astype(jnp.bfloat16)
+                act = jax.nn.sigmoid(g)
+                silu = g * act
+                gate_ref[rows, :] = (u * act * (1.0 + g * (1.0 - act))).astype(jnp.bfloat16)
+                up_ref[rows, :] = silu.astype(jnp.bfloat16)
+                hidden_ref[rows, :] = (silu * u).astype(jnp.bfloat16)
 
         cols = pl.BlockSpec((TREE, 256), lambda j: (m, j))
         pltpu.emit_pipeline(
@@ -850,100 +929,161 @@
             out_specs=[pl.BlockSpec((256, D), lambda i: (i, 0))],
         )(hidden, cot_full, down_grad)
 
-    g_qkv.start()
+    def down(m, near):
+        def body(h_ref, w_ref, out_ref):
+            for part in range(TREE // OWN):
+                rows = slice(part * OWN, (part + 1) * OWN)
+                out_ref[rows, :] = dot_nn(h_ref[rows, :], w_ref[...]).astype(jnp.bfloat16)
+
+        side = place.y if near else 1 - place.y
+        pltpu.emit_pipeline(
+            body,
+            grid=(NZ,),
+            in_specs=[
+                pl.BlockSpec((TREE, WIDE), lambda j: (m, 0)),
+                pl.BlockSpec((WIDE, OWN), lambda j: (0, j * NY + side)),
+            ],
+            out_specs=[pl.BlockSpec((TREE, OWN), lambda j: (m, j * NY + side))],
+        )(hidden, w_down, down_out)
+
+    g_qkv_load, tokens_load, gain_load, out_load, gu_load, cot_load, down_load = loads
+    g_qkv_load.wait()
+    lower(wide_qkv, low_qkv)
+    g_qkv.start_y()
+    g_qkv.start_z()
+    out_load.wait()
+    lower(wide_out, low_out)
+    g_out.start_y()
+    g_out.start_z()
+    tokens_load.wait()
+    gain_load.wait()
     for m in range(MICRO):
-        a_in[m].start(near.at[m], t_keep.at[m])
-    g_out.start()
-    g_gate.start()
+        first_norm(m)
+    gu_load.wait()
+    lower(wide_gu.at[0], low_gu.at[0])
+    g_gate.start_y()
+    g_qkv.relay_y()
+    g_out.relay_y()
+    lower(wide_gu.at[1], low_gu.at[1])
+    g_up.start_y()
+    cot_load.wait()
     for m in range(MICRO):
-        a_cot[m].start(cot.at[m], t_keep.at[2 + m])
+        a_cot[m].start(cot_buf.at[m], t_keep.at[2 + m])
+    down_load.wait()
+    lower(wide_down, low_down)
+    g_down.start_y()
     a_in[0].relay()
+    g_qkv.relay(1)
+    g_out.relay(1)
     a_in[1].relay()
-    g_qkv.relay()
-    g_out.relay()
-    g_up.start()
+    g_qkv.relay(2)
+    g_out.relay(2)
+    g_gate.start_z()
     a_in[0].finish()
+    a_in[1].finish()
+    a_cot[0].relay()
+    g_qkv.relay(3)
     g_qkv.finish()
     project(0)
-    a_in[1].finish()
+    g_out.relay(3)
+    g_out.finish()
+    g_gate.relay(1)
     project(1)
-    a_cot[0].relay()
     a_cot[1].relay()
     attention(0)
-    g_out.finish()
+    g_gate.relay(2)
+    g_up.start_z()
     out_project(0)
     sums[0].start()
     attention(1)
     sums[0].middle()
     out_project(1)
     sums[1].start()
-    g_gate.relay()
-    g_down.start()
+    g_gate.relay(3)
+    sums[1].middle()
     stored = [middle_norm(0)]
-    sums[1].middle()
+    g_up.relay(1)
+    stored.append(middle_norm(1))
     a_ffn[0].relay()
-    stored.append(middle_norm(1))
+    g_up.relay(2)
+    g_down.start_z()
     a_ffn[1].relay()
-    g_up.relay()
+    g_up.relay(3)
+    g_down.relay(1)
     a_cot[0].finish()
     a_cot[1].finish()
     a_ffn[0].finish()
     g_gate.finish()
     g_up.finish()
     gate_up(0)
+    g_down.relay(2)
     a_ffn[1].finish()
     gate_up(1)
-    g_down.relay()
+    g_down.relay(3)
+    g_down.keep_own()
+    down(0, True)
+    down(1, True)
     grad_down()
     g_down.finish()
+    down(0, False)
+    down(1, False)
     for copy in stored:
         copy.wait()
     copies.close()
 
 
-def forward(near, tokens, cot, low_qkv, low_out, low_gu, low_down, gains, cosines, sines, seg_col, parent_col, seg_row):
+def forward(tokens, cot, w_qkv, w_out, w_gu, w_down, gains, tables):
     low = jnp.bfloat16
+    wide = jnp.float32
     shape = jax.ShapeDtypeStruct
     all_tokens = MICRO * TREE
     outs = [
         shape((D, 768), low), shape((512, D), low), shape((2, D, WIDE), low), shape((WIDE, D), low),
         shape((all_tokens, D), low), shape((all_tokens, D), low), shape((all_tokens, D), low),
-        shape((all_tokens, 768), low), shape((all_tokens, 512), low), shape((MICRO, OWN, D), jnp.float32),
+        shape((all_tokens, 768), low), shape((all_tokens, 512), low), shape((2 * MICRO * 4 * TREE, 128), wide),
+        shape((MICRO, OWN, D), wide),
         shape((all_tokens, WIDE), low), shape((all_tokens, WIDE), low), shape((all_tokens, WIDE), low),
-        shape((WIDE, D), low),
+        shape((WIDE, D), low), shape((all_tokens, D), low),
     ]
     dma = pltpu.SemaphoreType.DMA
+    blocks = [(OWN, 768), (512, OWN), (2, OWN, WIDE), (WIDE, OWN)]
+    scratch = [
+        pltpu.VMEM((MICRO, NX * NC, OWN, D), low),
+        pltpu.VMEM((MICRO, NX, OWN, D), low),
+        pltpu.VMEM((MICRO, OWN, D), low),
+        pltpu.VMEM((MICRO, OWN, D), low),
+        pltpu.VMEM((MICRO, OWN, D), low),
+        pltpu.VMEM((MICRO, OWN, D), low),
+        pltpu.VMEM((MICRO, OWN, D), low),
+        pltpu.VMEM((2, D), wide),
+    ]
+    scratch += [pltpu.VMEM(block, wide) for block in blocks]
+    scratch += [pltpu.VMEM(block, low) for block in blocks]
+    scratch += [
+        dma((5, 3, NZ * NY)), dma((5, NZ * NY)), dma((5,)),
+        dma((6, 3)), dma((6, NX * NC)), dma((6,)),
+        dma((MICRO, 3)), dma((MICRO, 3)), dma((7,)),
+    ]
     return pl.pallas_call(
         forward_kernel,
         out_shape=outs,
-        in_specs=[HBM] * 13,
+        in_specs=[HBM] * 12,
         out_specs=[HBM] * len(outs),
-        scratch_shapes=[
-            pltpu.VMEM((MICRO, NX * NC, OWN, D), low),
-            pltpu.VMEM((MICRO, NX, OWN, D), low),
-            pltpu.VMEM((MICRO, OWN, D), low),
-            pltpu.VMEM((MICRO, OWN, D), jnp.float32),
-            pltpu.VMEM((MICRO, OWN, D), low),
-            pltpu.VMEM((OWN, D), low),
-            pltpu.VMEM((2, D), jnp.float32),
-            dma((5, 7)), dma((5, NZ * NY)), dma((5,)),
-            dma((6, 3)), dma((6, NX * NC)), dma((6,)),
-            dma((MICRO, 3)), dma((MICRO, 3)), dma((4,)),
-        ],
+        scratch_shapes=scratch,
         compiler_params=pltpu.CompilerParams(
-            collective_id=0, has_side_effects=True, vmem_limit_bytes=60 * 1024 * 1024
+            collective_id=0, has_side_effects=True, vmem_limit_bytes=63 * 1024 * 1024
         ),
         cost_estimate=pl.CostEstimate(flops=90 * 10**9, bytes_accessed=2 * 10**8, transcendentals=10**7),
         name="forward",
-    )(near, tokens, cot, low_qkv, low_out, low_gu, low_down, gains, cosines, sines, seg_col, parent_col, seg_row)
+    )(tokens, cot, w_qkv.reshape(OWN, 768), w_out, w_gu, w_down, gains, *tables)
 
 
 class GradSum:
     ORDER = (2, 1, 3)
 
-    def __init__(self, place, copies, full, view, from_y, summed, from_z, owned, squares, sems):
+    def __init__(self, place, copies, full, view, from_y, from_z, owned, squares, sems):
         self.place, self.copies, self.full, self.view = place, copies, full, view
-        self.from_y, self.summed, self.from_z, self.owned = from_y, summed, from_z, owned
+        self.from_y, self.from_z, self.owned = from_y, from_z, owned
         self.squares = squares
         self.y_send, self.y_recv, self.z_send, self.z_recv = sems
         rows, cols = owned.shape
@@ -970,10 +1110,10 @@
 
         mine = self.view(self.full, p.row_z[off])
         pltpu.emit_pipeline(body, grid=(self.grid,), in_specs=[self.spec] * 2, out_specs=[self.spec])(
-            mine, self.from_y.at[off], self.summed.at[off - 1]
+            mine, self.from_y.at[off], self.from_y.at[off]
         )
         self.copies.send(
-            self.summed.at[off - 1], self.from_z.at[off - 1], self.z_send.at[off - 1], self.z_recv.at[off - 1], p.at_z[off]
+            self.from_y.at[off], self.from_z.at[off - 1], self.z_send.at[off - 1], self.z_recv.at[off - 1], p.at_z[off]
         )
 
     def end(self):
@@ -997,13 +1137,14 @@
 
 
 def backward_kernel(
-    w_qkv, w_out, w_gu, w_down, attn_in, cot_full, ffn_in, qkv, heads, resid, gate, up, hidden, down_grad,
-    tokens, cot, gain, cosines, sines, seg_col, parent_col, seg_row,
-    mixed, d_tokens, own_qkv, own_out, own_gate, own_up, own_down, gain_out, square_out,
-    gate_grad, up_grad, out_back, heads_grad, proj_grad, gu_grad, out_grad, qkv_grad,
-    y_qkv, y_out, y_gate, y_up, y_down, s_qkv, s_out, s_gate, s_up, s_down, z_qkv, z_out, z_gate, z_up, z_down,
-    partial, from_core, from_x, mid, wide_buf, low_buf, near_buf, gain_buf, gain_sum, squares, key_sum, value_sum,
-    r_ysend, r_yrecv, r_zsend, r_zrecv, t_send, t_recv, t_keep, u_send, u_recv, l_sem,
+    w_qkv, w_out, w_gu, w_down, attn_in, cot_full, ffn_in, qkv, heads, log_sums, resid, gate, up, hidden, down_grad,
+    down_out, tokens, cot, gain, cosines, sines, seg_col, parent_col, seg_row,
+    mixed, d_tokens, own_qkv, own_out, own_gu, own_down, totals_out,
+    gate_grad, up_grad, out_back, proj_grad, gu_grad, out_grad, qkv_grad,
+    y_qkv, y_out, y_gate, y_up, y_down, z_qkv, z_out, z_gate, z_up, z_down,
+    partial, away, mine, from_core, from_x, mid, wide_buf, low_buf, near_buf, gain_buf, gain_sum, squares,
+    key_sum, value_sum, grad_buf, stage, came, z_came, totals,
+    r_ysend, r_yrecv, r_zsend, r_zrecv, t_send, t_recv, t_keep, u_send, u_recv, l_sem, n_send, n_recv,
 ):
     place = Place()
     copies = Copies()
@@ -1019,19 +1160,26 @@
         sems = (r_ysend.at[index], r_yrecv.at[index], r_zsend.at[index], r_zrecv.at[index])
         return GradSum(place, copies, full, view, *refs, squares, sems)
 
-    r_qkv = grad_sum(0, qkv_grad, row_block, y_qkv, s_qkv, z_qkv, own_qkv)
-    r_out = grad_sum(1, out_grad, col_block, y_out, s_out, z_out, own_out)
-    r_gate = grad_sum(2, gu_grad.at[0], row_block, y_gate, s_gate, z_gate, own_gate)
-    r_up = grad_sum(3, gu_grad.at[1], row_block, y_up, s_up, z_up, own_up)
-    r_down = grad_sum(4, down_grad, col_block, y_down, s_down, z_down, own_down)
+    r_qkv = grad_sum(0, qkv_grad, row_block, y_qkv, z_qkv, own_qkv)
+    r_out = grad_sum(1, out_grad, col_block, y_out, z_out, own_out)
+    r_gate = grad_sum(2, gu_grad.at[0], row_block, y_gate, z_gate, own_gu.at[0])
+    r_up = grad_sum(3, gu_grad.at[1], row_block, y_up, z_up, own_gu.at[1])
+    r_down = grad_sum(4, down_grad, col_block, y_down, z_down, own_down)
     a_back = [
         TokenGather(place, copies, out_back, m * TREE, t_send.at[m], t_recv.at[m]) for m in range(MICRO)
     ]
 
     def token_sum(turn, m):
+        if turn == 1:
+            blocks = lambda i: down_out.at[pl.ds(pl.multiple_of(m * TREE + i * OWN, OWN), OWN), :]
+            far, near = away.at[m], mine.at[m]
+        else:
+            blocks = lambda i: partial.at[m, i]
+            far, near = partial.at[m, place.col_x], partial.at[m, place.own]
         lands = 1 if turn == 1 else 0
         return TokenSum(
-            place, copies, partial.at[m], from_core.at[lands, m], from_x.at[lands, m], u_send.at[turn, m], u_recv.at[turn, m]
+            place, copies, blocks, far, near, from_core.at[lands, m], from_x.at[lands, m], u_send.at[turn, m],
+            u_recv.at[turn, m],
         )
 
     ffn_sum = [token_sum(0, m) for m in range(MICRO)]
@@ -1043,11 +1191,8 @@
             for part in range(TREE // OWN):
                 rows = slice(part * OWN, (part + 1) * OWN)
                 back = residual_mult * dot_nt(c_ref[rows, :], w_ref[...])
-                g = gate_ref[rows, :].astype(jnp.float32)
-                u = up_ref[rows, :].astype(jnp.float32)
-                act = jax.nn.sigmoid(g)
-                gate_out[rows, :] = (back * u * act * (1.0 + g * (1.0 - act))).astype(jnp.bfloat16)
-                up_out[rows, :] = (back * g * act).astype(jnp.bfloat16)
+                gate_out[rows, :] = (back * gate_ref[rows, :].astype(jnp.float32)).astype(jnp.bfloat16)
+                up_out[rows, :] = (back * up_ref[rows, :].astype(jnp.float32)).astype(jnp.bfloat16)
 
         cols = pl.BlockSpec((TREE, 256), lambda j: (m, j))
         pltpu.emit_pipeline(
@@ -1062,19 +1207,21 @@
             out_specs=[cols, cols],
         )(cot_full, w_down, gate, up, gate_grad, up_grad)
 
-    def grad_weight(near_all, far_all, out, near_cols, far_cols):
+    def grad_weight(near_all, far_all, out, near_cols, far_cols, side=None):
         def body(a_ref, b_ref, out_ref):
             out_ref[...] = dot_tn(a_ref[...], b_ref[...]).astype(jnp.bfloat16)
 
-        step = min(256, near_cols)
+        def block(j):
+            return j if side is None else j * NY + side
+
         pltpu.emit_pipeline(
             body,
-            grid=(near_cols // step,),
+            grid=(near_cols // OWN if side is None else NZ,),
             in_specs=[
-                pl.BlockSpec((MICRO * TREE, step), lambda i: (0, i)),
-                pl.BlockSpec((MICRO * TREE, far_cols), lambda i: (0, 0)),
+                pl.BlockSpec((MICRO * TREE, OWN), lambda j: (0, block(j))),
+                pl.BlockSpec((MICRO * TREE, far_cols), lambda j: (0, 0)),
             ],
-            out_specs=[pl.BlockSpec((step, far_cols), lambda i: (i, 0))],
+            out_specs=[pl.BlockSpec((OWN, far_cols), lambda j: (block(j), 0))],
         )(near_all, far_all, out)
 
     def back_ffn(m):
@@ -1098,48 +1245,18 @@
             _explicit_indices=True,
         )(gate_grad, up_grad, w_gu, w_gu)
 
-    def down(m):
-        def body(step, h_ref, w_ref):
-            for part in range(TREE // OWN):
-                rows = slice(part * OWN, (part + 1) * OWN)
-                value = dot_nn(h_ref[rows, :], w_ref[...])
-                partial[m, part, :, pl.ds(pl.multiple_of(step.index[0] * 256, 256), 256)] = value.astype(jnp.bfloat16)
-
-        pltpu.emit_pipeline(
-            body,
-            grid=(D // 256,),
-            in_specs=[
-                pl.BlockSpec((TREE, WIDE), lambda j: (m, 0)),
-                pl.BlockSpec((WIDE, 256), lambda j: (0, j)),
-            ],
-            out_specs=[],
-            _explicit_indices=True,
-        )(hidden, w_down)
-
-    def back_heads(m):
-        def body(a_ref, w_ref, out_ref):
-            out_ref[...] = dot_nt(a_ref[...], w_ref[...]).astype(jnp.bfloat16)
-
-        steps = TREE // OWN
-        pltpu.emit_pipeline(
-            body,
-            grid=(steps,),
-            in_specs=[
-                pl.BlockSpec((OWN, D), lambda i: (m * steps + i, 0)),
-                pl.BlockSpec((512, D), lambda i: (0, 0)),
-            ],
-            out_specs=[pl.BlockSpec((OWN, 512), lambda i: (m * steps + i, 0))],
-        )(out_back, w_out, heads_grad)
-
     def back_attention(m):
         tree = pl.BlockSpec((TREE, 128), lambda g: (m, 0))
         group = pl.BlockSpec((TREE, 384), lambda g: (m, g))
         pltpu.emit_pipeline(
-            functools.partial(attend_back, key_sum, value_sum),
+            functools.partial(attend_back, key_sum, value_sum, grad_buf),
             grid=(2,),
             in_specs=[
+                pl.BlockSpec((TREE, D), lambda g: (m, 0)),
+                pl.BlockSpec((256, D), lambda g: (g, 0)),
+                pl.BlockSpec((TREE, 256), lambda g: (m, g)),
+                pl.BlockSpec((4 * TREE, 128), lambda g: (m * 2 + g, 0)),
                 group,
-                pl.BlockSpec((TREE, 256), lambda g: (m, g)),
                 tree,
                 tree,
                 tree,
@@ -1147,7 +1264,7 @@
                 pl.BlockSpec((8, TREE), lambda g: (m, 0)),
             ],
             out_specs=[group],
-        )(qkv, heads_grad, cosines, sines, seg_col, parent_col, seg_row, proj_grad)
+        )(out_back, w_out, heads, log_sums, qkv, cosines, sines, seg_col, parent_col, seg_row, proj_grad)
 
     def back_project(m):
         def body(step, a_ref, w_ref):
@@ -1215,82 +1332,112 @@
         return copies.local(mid.at[m], d_tokens.at[m], l_sem.at[2 + m])
 
     def sent(part):
-        done = part.sent + [part.passed]
-        for copy in done:
-            copy.wait_send()
-        copies.open_sends = [copy for copy in copies.open_sends if not any(copy is gone for gone in done)]
+        copies.close(part.sent)
+
+    def sum_everywhere():
+        stage[0] = jnp.zeros_like(stage[0])
+        stage[0, 0:2, :] = gain_sum[0:2, :]
+        stage[0, 2:3, :] = squares[0:1, :]
+        for k, partner in enumerate((place.at_c, place.at_x, place.at_y)):
+            copies.send(stage.at[k], came.at[k], n_send.at[k], n_recv.at[k], partner)
+            copies.arrive(came.at[k], n_send.at[k], n_recv.at[k], partner)
+            stage[k + 1] = stage[k] + came[k]
+        last = stage.at[3]
+        for off in range(1, NZ):
+            copies.send(last, z_came.at[place.z], n_send.at[2 + off], n_recv.at[3 + place.z], place.at_z[off])
+        z_came[place.z] = stage[3]
+        for off in range(1, NZ):
+            there = lax.rem(place.z + off, NZ)
+            copies.arrive(z_came.at[there], n_send.at[2 + off], n_recv.at[3 + there], place.at_z[off])
+        total = z_came[0]
+        for there in range(1, NZ):
+            total = total + z_came[there]
+        gains_total = total[0:2]
+        norm = jnp.sqrt(
+            jnp.sum(total[2:3], axis=(0, 1), keepdims=True) + jnp.sum(gains_total * gains_total, axis=(0, 1), keepdims=True)
+        )
+        factor = jnp.minimum(1.0, clip_bound() / (norm + 1e-06))
+        totals[...] = jnp.zeros_like(totals)
+        totals[0:2, :] = gains_total
+        totals[2:3, :] = jnp.broadcast_to(factor, (1, D))
+        totals[3:4, :] = jnp.broadcast_to(norm, (1, D))
+
+    def load_partial(m):
+        return [
+            copies.local(mlp_sum[m].blocks(place.col_x), away.at[m], l_sem.at[2 + 2 * m]),
+            copies.local(mlp_sum[m].blocks(place.own), mine.at[m], l_sem.at[3 + 2 * m]),
+        ]
 
     r_down.start()
+    mlp_sum[0].start()
+    mlp_sum[1].start()
     load_gain = copies.local(gain, gain_buf, l_sem.at[0])
+    parts = load_partial(0) + load_partial(1)
     gain_sum[...] = jnp.zeros_like(gain_sum)
     squares[...] = jnp.zeros_like(squares)
     load_gain.wait()
+    for copy in parts:
+        copy.wait()
+    mlp_sum[0].middle()
+    mlp_sum[1].middle()
     grad_hidden(0)
     grad_hidden(1)
+    r_down.middle(2)
     back_ffn(0)
     ffn_sum[0].start()
-    r_down.middle(2)
+    r_down.middle(1)
     back_ffn(1)
     ffn_sum[1].start()
     ffn_sum[0].middle()
-    r_down.middle(1)
-    grad_weight(ffn_in, gate_grad, gu_grad.at[0], D, WIDE)
+    grad_weight(ffn_in, gate_grad, gu_grad.at[0], D, WIDE, 1 - place.y)
     r_gate.start()
     ffn_sum[1].middle()
     r_down.middle(3)
+    grad_weight(ffn_in, gate_grad, gu_grad.at[0], D, WIDE, place.y)
+    finish_mixed(0)
     middle_back(0)
+    grad_weight(ffn_in, up_grad, gu_grad.at[1], D, WIDE, 1 - place.y)
+    r_up.start()
     middle_back(1)
-    sent(ffn_sum[0])
-    down(0)
-    mlp_sum[0].start()
     r_gate.middle(2)
     a_back[0].relay()
+    grad_weight(ffn_in, up_grad, gu_grad.at[1], D, WIDE, place.y)
+    r_gate.middle(1)
+    finish_mixed(1)
     a_back[1].relay()
-    sent(ffn_sum[1])
-    down(1)
-    mlp_sum[1].start()
-    mlp_sum[0].middle()
-    r_gate.middle(1)
-    grad_weight(ffn_in, up_grad, gu_grad.at[1], D, WIDE)
-    r_up.start()
-    mlp_sum[1].middle()
+    a_back[0].finish()
+    back_attention(0)
     r_gate.middle(3)
-    a_back[0].finish()
-    back_heads(0)
-    back_attention(0)
-    finish_mixed(0)
-    sent(mlp_sum[0])
+    sent(ffn_sum[0])
     back_project(0)
     attn_sum[0].start()
+    a_back[1].finish()
+    grad_weight(heads, out_back, out_grad, 512, D)
+    r_out.start()
     r_up.middle(2)
-    a_back[1].finish()
-    back_heads(1)
     back_attention(1)
-    finish_mixed(1)
-    sent(mlp_sum[1])
-    back_project(1)
-    attn_sum[1].start()
+    sent(ffn_sum[1])
     attn_sum[0].middle()
     grad_weight(attn_in, proj_grad, qkv_grad, D, 768)
     r_qkv.start()
-    grad_weight(heads, out_back, out_grad, 512, D)
-    r_out.start()
     r_up.middle(1)
-    attn_sum[1].middle()
+    back_project(1)
+    attn_sum[1].start()
     r_up.middle(3)
     r_down.end()
+    attn_sum[1].middle()
+    for off in GradSum.ORDER:
+        r_out.middle(off)
     stores = [finish_tokens(0)]
     for off in GradSum.ORDER:
         r_qkv.middle(off)
+    r_gate.end()
     stores.append(finish_tokens(1))
-    for off in GradSum.ORDER:
-        r_out.middle(off)
-    stores.append(copies.local(gain_sum, gain_out, l_sem.at[0]))
-    r_gate.end()
     r_up.end()
+    r_out.end()
     r_qkv.end()
-    r_out.end()
-    stores.append(copies.local(squares, square_out, l_sem.at[1]))
+    sum_everywhere()
+    stores.append(copies.local(totals, totals_out, l_sem.at[1]))
     for copy in stores:
         copy.wait()
     copies.close()
@@ -1303,24 +1450,26 @@
     all_tokens = MICRO * TREE
     blocks = [(OWN, 768), (512, OWN), (OWN, WIDE), (OWN, WIDE), (WIDE, OWN)]
     outs = [shape((MICRO, OWN, D), low), shape((MICRO, OWN, D), wide)]
-    outs += [shape(block, wide) for block in blocks]
-    outs += [shape((8, D), wide), shape((8, D), wide)]
+    outs += [shape(block, wide) for block in ((OWN, 768), (512, OWN), (2, OWN, WIDE), (WIDE, OWN))]
+    outs += [shape((8, D), wide)]
     outs += [
         shape((all_tokens, WIDE), low), shape((all_tokens, WIDE), low), shape((all_tokens, D), low),
-        shape((all_tokens, 512), low), shape((all_tokens, 768), low),
+        shape((all_tokens, 768), low),
         shape((2, D, WIDE), low), shape((512, D), low), shape((D, 768), low),
     ]
     outs += [shape((NZ,) + block, low) for block in blocks]
     outs += [shape((NZ - 1,) + block, low) for block in blocks]
-    outs += [shape((NZ - 1,) + block, low) for block in blocks]
     dma = pltpu.SemaphoreType.DMA
+    args = (*saved, tokens, cot, gains, *tables)
     return pl.pallas_call(
         backward_kernel,
         out_shape=outs,
-        in_specs=[HBM] * 22,
+        in_specs=[HBM] * len(args),
         out_specs=[HBM] * len(outs),
         scratch_shapes=[
             pltpu.VMEM((MICRO, NX * NC, OWN, D), low),
+            pltpu.VMEM((MICRO, OWN, D), low),
+            pltpu.VMEM((MICRO, OWN, D), low),
             pltpu.VMEM((2, MICRO, NX, OWN, D), low),
             pltpu.VMEM((2, MICRO, OWN, D), low),
             pltpu.VMEM((MICRO, OWN, D), wide),
@@ -1332,16 +1481,82 @@
             pltpu.VMEM((8, D), wide),
             pltpu.VMEM((TREE, 128), wide),
             pltpu.VMEM((TREE, 128), wide),
+            pltpu.VMEM((TREE, 256), low),
+            pltpu.VMEM((4, 8, D), wide),
+            pltpu.VMEM((3, 8, D), wide),
+            pltpu.VMEM((NZ, 8, D), wide),
+            pltpu.VMEM((8, D), wide),
             dma((5, NZ)), dma((5, NZ)), dma((5, NZ)), dma((5, NZ)),
             dma((MICRO, 3)), dma((MICRO, NX * NC)), dma((MICRO,)),
-            dma((3, MICRO, 3)), dma((3, MICRO, 3)), dma((4,)),
+            dma((3, MICRO, 3)), dma((3, MICRO, 3)), dma((6,)), dma((6,)), dma((3 + NZ,)),
         ],
+        input_output_aliases={11: 7, 12: 8},
         compiler_params=pltpu.CompilerParams(
             collective_id=1, has_side_effects=True, vmem_limit_bytes=63 * 1024 * 1024
         ),
         cost_estimate=pl.CostEstimate(flops=140 * 10**9, bytes_accessed=5 * 10**8, transcendentals=10**7),
         name="backward",
-    )(*saved, tokens, cot, gains, *tables)
+    )(*args)
+
+
+def update_kernel(
+    g_qkv, g_out, g_gu, g_down, w_qkv, w_out, w_gu, w_down, mom_qkv, mom_out, mom_gu, mom_down, gains, mom_gains, totals,
+    new_qkv, new_out, new_gu, new_down, moments_qkv, moments_out, moments_gu, moments_down,
+    copy_qkv, copy_out, copy_gu, copy_down, new_gains, moments_gains,
+):
+    rates = step_rates()
+
+    def step_of(grad, master, first, second, rate):
+        clipped = totals[2:3, 0:1].reshape((1,) * grad.ndim) * grad
+        first = beta_one * first + (1.0 - beta_one) * clipped
+        second = beta_two * second + (1.0 - beta_two) * clipped * clipped
+        first_hat = first / (1.0 - beta_one**STEP)
+        second_hat = second / (1.0 - beta_two**STEP)
+        updated = master - rate * (first_hat / (jnp.sqrt(second_hat) + adam_eps) + weight_decay * master)
+        return updated, first, second
+
+    def weight(rate, rows, grad, master, moments, new, new_moments, new_copy):
+        def body(g_ref, w_ref, m_ref, new_ref, mom_ref, low_ref):
+            updated, first, second = step_of(g_ref[...], w_ref[...], m_ref[0], m_ref[1], rate)
+            new_ref[...] = updated
+            mom_ref[0] = first
+            mom_ref[1] = second
+            low_ref[...] = updated.astype(jnp.bfloat16)
+
+        rest = master.shape[1:]
+        zeros = (0,) * len(rest)
+        one = pl.BlockSpec((rows,) + rest, lambda i: (i,) + zeros)
+        two = pl.BlockSpec((2, rows) + rest, lambda i: (0, i) + zeros)
+        pltpu.emit_pipeline(
+            body, grid=(master.shape[0] // rows,), in_specs=[one, one, two], out_specs=[one, two, one]
+        )(grad, master, moments, new, new_moments, new_copy)
+
+    weight(rates[2], 64, g_gu, w_gu, mom_gu, new_gu, moments_gu, copy_gu)
+    weight(rates[3], 512, g_down, w_down, mom_down, new_down, moments_down, copy_down)
+    weight(rates[1], 256, g_out, w_out, mom_out, new_out, moments_out, copy_out)
+    weight(rates[0], 64, g_qkv, w_qkv, mom_qkv, new_qkv, moments_qkv, copy_qkv)
+    updated, first, second = step_of(totals[0:2, :], gains[...], mom_gains[0], mom_gains[1], rates[4])
+    new_gains[...] = updated
+    moments_gains[0] = first
+    moments_gains[1] = second
+
+
+def update(grads, masters, states, gains, mom_gains, totals):
+    shape = jax.ShapeDtypeStruct
+    outs = [shape(master.shape, jnp.float32) for master in masters]
+    outs += [shape(state.shape, jnp.float32) for state in states]
+    outs += [shape(master.shape, jnp.bfloat16) for master in masters]
+    outs += [shape(gains.shape, jnp.float32), shape(mom_gains.shape, jnp.float32)]
+    whole = pl.BlockSpec(memory_space=pltpu.VMEM)
+    return pl.pallas_call(
+        update_kernel,
+        out_shape=outs,
+        in_specs=[HBM] * 12 + [whole] * 3,
+        out_specs=[HBM] * 12 + [whole] * 2,
+        compiler_params=pltpu.CompilerParams(vmem_limit_bytes=63 * 1024 * 1024),
+        cost_estimate=pl.CostEstimate(flops=60 * 10**6, bytes_accessed=58 * 10**6, transcendentals=4 * 10**6),
+        name="update",
+    )(*grads, *masters, *states, gains, mom_gains, totals)
 
 
 def fast_local(
@@ -1360,53 +1575,27 @@
     gains,
     mom_gains,
 ):
-    low = jnp.bfloat16
     tables = [position_tables(segment_of[m], leaf_parent[m]) for m in range(MICRO)]
     tables = [jnp.concatenate([table[i] for table in tables], axis=0) for i in range(5)]
-    near, _ = normalize(tokens.astype(jnp.float32), gains[0])
-    saved = forward(
-        near.astype(low), tokens, cotangent,
-        w_qkv.astype(low).reshape(OWN, 768), w_out.astype(low), w_gu.astype(low), w_down.astype(low),
-        gains, *tables,
+    saved = forward(tokens, cotangent, w_qkv, w_out, w_gu, w_down, gains, tables)
+    mixed, d_tokens, g_qkv, g_out, g_gu, g_down, totals = backward(saved, tokens, cotangent, gains, tables)[:7]
+
+    def flat(value, lead):
+        return value.reshape(value.shape[:lead] + (-1, WIDE))
+
+    masters = (w_qkv, w_out, flat(w_gu, 0), w_down)
+    states = (mom_qkv, mom_out, flat(mom_gu, 1), mom_down)
+    done = update(
+        (g_qkv.reshape(w_qkv.shape), g_out, flat(g_gu, 0), g_down), masters, states, gains, mom_gains, totals
     )
-    mixed, d_tokens, g_qkv, g_out, g_gate, g_up, g_down, gain_rows, squares = backward(
-        saved, tokens, cotangent, gains, tables
-    )[:9]
-    owned = (g_qkv.reshape(w_qkv.shape), g_out, jnp.stack([g_gate, g_up]), g_down)
-    local_squares = jnp.sum(squares[0])
-    gain_partial = gain_rows[:2]
-    total_squares, gain_total = lax.psum((local_squares, gain_partial), ("row", "col"))
-    grad_norm = jnp.sqrt(total_squares + jnp.sum(gain_total * gain_total))
-    factor = jnp.minimum(1.0, clip_bound() / (grad_norm + 1e-06))
-    rates = step_rates()
-    masters = (w_qkv, w_out, w_gu, w_down)
-    states = (mom_qkv, mom_out, mom_gu, mom_down)
+    new, moments, copies = list(done[:4]), list(done[4:8]), list(done[8:12])
+    new[2] = new[2].reshape(w_gu.shape)
+    moments[2] = moments[2].reshape(mom_gu.shape)
+    copies[2] = copies[2].reshape(w_gu.shape)
     results = []
-    for index_w in range(4):
-        updated, moments = adamw(
-            masters[index_w], states[index_w], owned[index_w], factor, rates[index_w]
-        )
-        results.append((updated, moments, updated.astype(jnp.bfloat16)))
-    new_gains, moments_gains = adamw(gains, mom_gains, gain_total, factor, rates[4])
-    return (
-        mixed,
-        d_tokens,
-        grad_norm,
-        results[0][0],
-        results[0][1],
-        results[0][2],
-        results[1][0],
-        results[1][1],
-        results[1][2],
-        results[2][0],
-        results[2][1],
-        results[2][2],
-        results[3][0],
-        results[3][1],
-        results[3][2],
-        new_gains,
-        moments_gains,
-    )
+    for i in range(4):
+        results += [new[i], moments[i], copies[i]]
+    return (mixed, d_tokens, totals[3, 0], *results, done[12], done[13])
 
 
 def solution(mesh):

time: 1020 us -> 862 us (0.85)
  Pallas kernels: 897 us -> 831 us
  blocking collectives: 45 us -> 0 us
  other arithmetic: 51.1 us -> 10.8 us
    pallas_call x2 -> x3, Pallas kernels: 897 us -> 831 us  [the longest x1 410 us: backward(): pl.pallas_call(backward_kernel, out_shape=outs, in_specs=[HBM] * len(args...]
    psum x1 -> x0, blocking collectives: 45 us -> none  [fast_local(): lax.psum((local_squares, gain_partial), ('row', 'col'))]
    convert_element_type x7 -> x0, other arithmetic: 16.7 us -> none  [the longest x2 8.91 us: fast_local(): results.append((updated, moments, updated.astype(jnp.bfloat16)))]
    another operation x10 -> x2, other arithmetic: 15.5 us -> 0.38 us  [the longest x8 15.2 us: adamw(): return (updated, jnp.stack([first_moment, second_moment]))]
where the time goes in v3:
time: 862 us; the launch traced here: 858 us
  Pallas kernels  831 us (96%)
  local copies, waits for them, and re-layouts  14.7 us (2%)
  other arithmetic  10.8 us (1%)
    pallas_call x1, Pallas kernels, backward(): pl.pallas_call(backward_kernel, out_shape=outs, in_specs=[HBM] * len(args...  410 us
    pallas_call x1, Pallas kernels, forward(): pl.pallas_call(forward_kernel, out_shape=outs, in_specs=[HBM] * 12, out_s...  389 us
    pallas_call x1, Pallas kernels, update(): pl.pallas_call(update_kernel, out_shape=outs, in_specs=[HBM] * 12 + [whol...  32.5 us

profile of v3, /device:TPU:0, one launch (start us, length us, event | category | flops | bytes accessed | tf_op | source)
XLA Modules:
  0.0 857.9 jit_solution(315376328045932459)
XLA Ops:
  0.7 0.8 broadcast_add_fusion.1
  1.4 0.1 concatenate.56
  1.5 0.1 concatenate.57
  1.6 0.8 slice_bitcast_fusion.1
  2.3 0.8 slice_convert_fusion.1
  3.1 0.1 convert_reduce_fusion
  3.2 0.1 convert_reduce_fusion.1
  3.4 0.2 reduce-window.16
  3.6 0.1 slice.32
  3.7 0.1 select_reduce_fusion.5
  3.8 0.2 reduce-window.17
  4.0 0.1 slice.36
  4.1 0.1 select_reduce_fusion.4
  4.2 0.1 fusion.3
  4.3 0.1 select_reduce_fusion
  4.5 0.1 select_reduce_fusion.1
  4.6 0.6 pad_maximum_fusion.seg_row
  5.3 2.1 copy.35
  7.3 1.3 broadcast.50.parent_col
  8.6 1.3 broadcast.49.seg_col
  9.9 3.7 fusion
  13.7 1.9 maximum_maximum_fusion.1.sines
  15.5 1.8 maximum_maximum_fusion.cosines
  17.4 388.8 %forward.1 = (bf16[2048,768]{1,0:T(8,128)(2,1)}, bf16[512,2048]{1,0:T(8,128)(2,1)}, bf16[2,2048,2048]{2,1,0:T(8,128)(2,1)}, bf16[2048,2048]{1,0:T(8,128)(2,1)}, ...) custom-call(bf16[2,256,2048]{2,1,0:T(8,128)(2,1)} %tokens.3, ...), custom_call_target="tpu_custom_call" | custom-call | flops 89999998976 | bytes 200000000 | tf_op jit(solution)/shard_map/forward/pallas_call | solution.py:1067
  406.2 410.0 %backward.1 = (bf16[2,256,2048]{2,1,0:T(8,128)(2,1)}, f32[2,256,2048]{2,1,0:T(8,128)}, f32[256,768]{1,0:T(8,128)}, f32[512,256]{1,0:T(8,128)}, f32[2,256,2048]{2...) custom-call(bf16[2048,768]{1,0:T(8,128)(2,1)} %get-tuple-element.54., ...), custom_call_target="tpu_custom_call", output_to_operand_aliasing={{7}: (11, {}), {8}: (12, {})} | custom-call | flops 140000002048 | bytes 500000000 | tf_op jit(solution)/shard_map/backward/pallas_call | solution.py:1464
  816.3 1.2 slice.37
  817.4 2.4 reshape.204.g_qkv
  819.9 32.5 %update.1 = (f32[256,2,384]{2,1,0:T(2,128)}, f32[512,256]{1,0:T(8,128)}, f32[512,2048]{1,0:T(8,128)}, f32[2048,256]{1,0:T(8,128)}, f32[2,256,2,384]{3,2,1,0:T(2,...) custom-call(f32[256,2,384]{2,1,0:T(2,128)} %reshape.204.g_qkv, ...), custom_call_target="tpu_custom_call" | custom-call | flops 60000000 | bytes 58000000 | tf_op jit(solution)/shard_map/update/pallas_call | solution.py:1551
  852.4 0.0 copy-start
  852.4 3.3 copy.40
  855.7 0.0 copy-done
  855.7 2.0 copy.41
  (15 shorter events, 0.2 us)
Async XLA Ops:
  852.4 3.3 copy-start

commit v4 on v3

--- a/solution.py
+++ b/solution.py
@@ -1079,61 +1079,195 @@
 
 
 class GradSum:
-    ORDER = (2, 1, 3)
+    ENDS = (3, 2, 1)
+    MIDDLES = (3, 2, 0)
 
     def __init__(self, place, copies, full, view, from_y, from_z, owned, squares, sems):
         self.place, self.copies, self.full, self.view = place, copies, full, view
         self.from_y, self.from_z, self.owned = from_y, from_z, owned
         self.squares = squares
         self.y_send, self.y_recv, self.z_send, self.z_recv = sems
+        h, odd = place.z // 2, place.z % 2
+        self.h = h
+        self.inner = odd + h - 2 * odd * h
+        self.at_end, self.at_middle = self.inner == 0, self.inner == 1
+        inward = place.row + NY * (1 - 2 * h)
+        outward = place.row - NY * (1 - 2 * h)
+        size = NZ * NY
+        self.inward = (lax.rem(inward + size, size), place.col)
+        self.outward = (lax.rem(outward + size, size), place.col)
+        self.end_slot = (3 - 3 * h, 2 - h, 1 + 3 * h)
+        self.middle_slot = (3 - 3 * h, 2 + 2 * h, 4 - h)
+        self.middle_from = (3 - 3 * h, 2 - h, 3 * h)
         rows, cols = owned.shape
-        step = max(16, min(rows, (256 * 1024) // cols))
-        self.grid = rows // step
-        self.spec = pl.BlockSpec((step, cols), lambda i: (i, 0))
+        self.grid = 2
+        self.spec = pl.BlockSpec((rows // 2, cols), lambda i: (i, 0))
+
+    def z_of(self, base):
+        return base + self.h * (3 - 2 * base)
+
+    def add(self, out, *terms, wide=1):
+        def body(*refs):
+            total = refs[0][...].astype(jnp.float32)
+            for ref in refs[1:-1]:
+                total = total + ref[...].astype(jnp.float32)
+            refs[-1][...] = total.astype(jnp.bfloat16)
+
+        rows, cols = self.owned.shape
+        spec = pl.BlockSpec((rows // 2, wide * cols), lambda i: (i, 0))
+        pltpu.emit_pipeline(body, grid=(2,), in_specs=[spec] * len(terms), out_specs=[spec])(*terms, out)
+
+    def last_add(self, *terms):
+        def body(*refs):
+            total = refs[0][...].astype(jnp.float32)
+            for ref in refs[1:-1]:
+                total = total + ref[...].astype(jnp.float32)
+            refs[-1][...] = total
+            cols = total.shape[1]
+            self.squares[0:1, 0:cols] += jnp.sum(total * total, axis=0, keepdims=True)
+
+        pltpu.emit_pipeline(body, grid=(self.grid,), in_specs=[self.spec] * len(terms), out_specs=[self.spec])(
+            *terms, self.owned
+        )
+
+    def got_z(self, slot, side=0):
+        land = self.landing(slot, side)
+        self.copies.arrive(land, self.z_send.at[0, side], self.z_recv.at[slot, side], self.place.at_up)
+
+
+class FarGradSum(GradSum):
+    def landing(self, slot, side):
+        return self.from_z.at[slot]
+
+    def turn_z(self, turn):
+        base = (3, 2, 1 - self.inner, self.inner)[turn]
+        return base + self.h * (3 - 2 * base)
 
     def start(self):
         p = self.place
-        for off in self.ORDER + (0,):
+        for turn in range(NZ):
             self.copies.send(
-                self.view(self.full, p.row_yz[off]), self.from_y.at[off], self.y_send.at[off], self.y_recv.at[off], p.at_y
+                self.view(self.full, self.turn_z(turn) * NY + (1 - p.y)), self.from_y.at[turn],
+                self.y_send.at[turn], self.y_recv.at[turn], p.at_y,
             )
 
-    def got_y(self, off):
-        self.copies.arrive(self.from_y.at[off], self.y_send.at[off], self.y_recv.at[off], self.place.at_y)
-
-    def middle(self, off):
+    def got_y(self, turn):
+        self.copies.arrive(self.from_y.at[turn], self.y_send.at[turn], self.y_recv.at[turn], self.place.at_y)
+
+    def hook(self, step):
         p = self.place
-        self.got_y(off)
-
-        def body(a_ref, b_ref, out_ref):
-            out_ref[...] = (a_ref[...].astype(jnp.float32) + b_ref[...].astype(jnp.float32)).astype(jnp.bfloat16)
-
-        mine = self.view(self.full, p.row_z[off])
-        pltpu.emit_pipeline(body, grid=(self.grid,), in_specs=[self.spec] * 2, out_specs=[self.spec])(
-            mine, self.from_y.at[off], self.from_y.at[off]
-        )
-        self.copies.send(
-            self.from_y.at[off], self.from_z.at[off - 1], self.z_send.at[off - 1], self.z_recv.at[off - 1], p.at_z[off]
-        )
+        if step < 3:
+
+            @pl.when(self.at_end)
+            def _():
+                self.got_y(step)
+                mine = self.view(self.full, self.z_of(self.ENDS[step]) * NY + p.y)
+                self.add(self.from_y.at[step], mine, self.from_y.at[step])
+
+            slot = self.end_slot[step]
+            self.copies.send(
+                self.from_y.at[step], self.from_z.at[slot], self.z_send.at[step, 0], self.z_recv.at[slot, 0],
+                self.inward, self.at_end,
+            )
+        if step > 0:
+            turn = step - 1
+
+            @pl.when(self.at_middle)
+            def _():
+                self.got_y(turn)
+                self.got_z(self.middle_from[turn])
+                mine = self.view(self.full, self.z_of(self.MIDDLES[turn]) * NY + p.y)
+                self.add(self.from_y.at[turn], mine, self.from_y.at[turn], self.from_z.at[self.middle_from[turn]])
+
+            slot = self.middle_slot[turn]
+            self.copies.send(
+                self.from_y.at[turn], self.from_z.at[slot], self.z_send.at[turn, 1], self.z_recv.at[slot, 0],
+                self.inward if turn < 2 else self.outward, self.at_middle,
+            )
 
     def end(self):
         p = self.place
-        self.got_y(0)
-        for off in (1, 3, 2):
-            self.copies.arrive(self.from_z.at[off - 1], self.z_send.at[off - 1], self.z_recv.at[off - 1], p.at_z[off])
-
-        def body(a_ref, b_ref, c_ref, d_ref, e_ref, out_ref):
-            total = a_ref[...].astype(jnp.float32)
-            for ref in (b_ref, c_ref, d_ref, e_ref):
-                total = total + ref[...].astype(jnp.float32)
-            out_ref[...] = total
-            cols = total.shape[1]
-            self.squares[0:1, 0:cols] += jnp.sum(total * total, axis=0, keepdims=True)
-
+        self.got_y(3)
         mine = self.view(self.full, p.row)
-        pltpu.emit_pipeline(body, grid=(self.grid,), in_specs=[self.spec] * 5, out_specs=[self.spec])(
-            mine, self.from_y.at[0], self.from_z.at[0], self.from_z.at[1], self.from_z.at[2], self.owned
-        )
+
+        @pl.when(self.at_end)
+        def _():
+            self.got_z(4 - self.h)
+            self.last_add(mine, self.from_y.at[3], self.from_z.at[4 - self.h])
+
+        @pl.when(self.at_middle)
+        def _():
+            self.got_z(1 + self.h)
+            self.got_z(4)
+            self.last_add(mine, self.from_y.at[3], self.from_z.at[1 + self.h], self.from_z.at[4])
+
+
+class NearGradSum(GradSum):
+    def landing(self, slot, side):
+        return self.from_z.at[slot] if side is None else self.from_z.at[slot, :, rows_of(side, OWN)]
+
+    def pair(self, base):
+        return self.full.at[:, rows_of(self.z_of(base), NY * OWN)]
+
+    def got_pair(self, slot):
+        self.copies.arrive(self.from_z.at[slot], self.z_send.at[0, 0], self.z_recv.at[slot, 0], self.place.at_up)
+
+    def hook(self, step):
+        if step < 3:
+            slot = self.end_slot[step]
+            self.copies.send(
+                self.pair(self.ENDS[step]), self.from_z.at[slot], self.z_send.at[step, 0], self.z_recv.at[slot, 0],
+                self.inward, self.at_end,
+            )
+        if step > 0:
+            turn = step - 1
+            here, slot = self.middle_from[turn], self.middle_slot[turn]
+
+            @pl.when(self.at_middle)
+            def _():
+                self.got_pair(here)
+                self.add(self.from_z.at[here], self.pair(self.MIDDLES[turn]), self.from_z.at[here], wide=NY)
+
+            self.copies.send(
+                self.from_z.at[here], self.from_z.at[slot], self.z_send.at[turn, 1], self.z_recv.at[slot, 0],
+                self.inward if turn < 2 else self.outward, self.at_middle,
+            )
+
+    def cross(self):
+        p = self.place
+        side = 1 - p.y
+        mine = self.view(self.full, p.row_y)
+
+        @pl.when(self.at_end)
+        def _():
+            land = self.landing(4 - self.h, side)
+            self.got_pair(4 - self.h)
+            self.add(land, mine, land)
+
+        @pl.when(self.at_middle)
+        def _():
+            land = self.landing(4, side)
+            self.got_pair(1 + self.h)
+            self.got_pair(4)
+            self.add(land, mine, land, self.landing(1 + self.h, side))
+
+        for slot, when in ((4 - self.h, self.at_end), (4, self.at_middle)):
+            self.copies.send(
+                self.landing(slot, side), self.from_y.at[0], self.y_send.at[0], self.y_recv.at[0], p.at_y, when
+            )
+
+    def end(self):
+        p = self.place
+        self.copies.arrive(self.from_y.at[0], self.y_send.at[0], self.y_recv.at[0], p.at_y)
+        mine = self.view(self.full, p.row)
+
+        @pl.when(self.at_end)
+        def _():
+            self.last_add(mine, self.from_y.at[0], self.landing(4 - self.h, p.y))
+
+        @pl.when(self.at_middle)
+        def _():
+            self.last_add(mine, self.from_y.at[0], self.landing(1 + self.h, p.y), self.landing(4, p.y))
 
 
 def backward_kernel(
@@ -1141,7 +1275,7 @@
     down_out, tokens, cot, gain, cosines, sines, seg_col, parent_col, seg_row,
     mixed, d_tokens, own_qkv, own_out, own_gu, own_down, totals_out,
     gate_grad, up_grad, out_back, proj_grad, gu_grad, out_grad, qkv_grad,
-    y_qkv, y_out, y_gate, y_up, y_down, z_qkv, z_out, z_gate, z_up, z_down,
+    y_qkv, y_out, y_gate, y_up, y_far, y_near, z_qkv, z_out, z_gate, z_up, z_far, z_near,
     partial, away, mine, from_core, from_x, mid, wide_buf, low_buf, near_buf, gain_buf, gain_sum, squares,
     key_sum, value_sum, grad_buf, stage, came, z_came, totals,
     r_ysend, r_yrecv, r_zsend, r_zrecv, t_send, t_recv, t_keep, u_send, u_recv, l_sem, n_send, n_recv,
@@ -1156,15 +1290,18 @@
     def col_block(full, r):
         return full.at[:, rows_of(r, OWN)]
 
-    def grad_sum(index, full, view, *refs):
+    def grad_sum(kind, index, full, view, *refs):
         sems = (r_ysend.at[index], r_yrecv.at[index], r_zsend.at[index], r_zrecv.at[index])
-        return GradSum(place, copies, full, view, *refs, squares, sems)
-
-    r_qkv = grad_sum(0, qkv_grad, row_block, y_qkv, z_qkv, own_qkv)
-    r_out = grad_sum(1, out_grad, col_block, y_out, z_out, own_out)
-    r_gate = grad_sum(2, gu_grad.at[0], row_block, y_gate, z_gate, own_gu.at[0])
-    r_up = grad_sum(3, gu_grad.at[1], row_block, y_up, z_up, own_gu.at[1])
-    r_down = grad_sum(4, down_grad, col_block, y_down, z_down, own_down)
+        return kind(place, copies, full, view, *refs, squares, sems)
+
+    half = WIDE // 2
+    low_half, high_half = pl.ds(0, half), pl.ds(half, half)
+    r_qkv = grad_sum(FarGradSum, 0, qkv_grad, row_block, y_qkv, z_qkv, own_qkv)
+    r_out = grad_sum(FarGradSum, 1, out_grad, col_block, y_out, z_out, own_out)
+    r_gate = grad_sum(FarGradSum, 2, gu_grad.at[0], row_block, y_gate, z_gate, own_gu.at[0])
+    r_up = grad_sum(FarGradSum, 3, gu_grad.at[1], row_block, y_up, z_up, own_gu.at[1])
+    r_far = grad_sum(FarGradSum, 4, down_grad.at[low_half, :], col_block, y_far, z_far, own_down.at[low_half, :])
+    r_near = grad_sum(NearGradSum, 5, down_grad.at[high_half, :], col_block, y_near, z_near, own_down.at[high_half, :])
     a_back = [
         TokenGather(place, copies, out_back, m * TREE, t_send.at[m], t_recv.at[m]) for m in range(MICRO)
     ]
@@ -1186,25 +1323,20 @@
     mlp_sum = [token_sum(1, m) for m in range(MICRO)]
     attn_sum = [token_sum(2, m) for m in range(MICRO)]
 
-    def grad_hidden(m):
+    def grad_hidden():
         def body(c_ref, w_ref, gate_ref, up_ref, gate_out, up_out):
-            for part in range(TREE // OWN):
-                rows = slice(part * OWN, (part + 1) * OWN)
-                back = residual_mult * dot_nt(c_ref[rows, :], w_ref[...])
-                gate_out[rows, :] = (back * gate_ref[rows, :].astype(jnp.float32)).astype(jnp.bfloat16)
-                up_out[rows, :] = (back * up_ref[rows, :].astype(jnp.float32)).astype(jnp.bfloat16)
-
-        cols = pl.BlockSpec((TREE, 256), lambda j: (m, j))
+            for part in range(WIDE // 512):
+                cols = slice(part * 512, (part + 1) * 512)
+                back = residual_mult * dot_nt(c_ref[...], w_ref[cols, :])
+                gate_out[:, cols] = (back * gate_ref[:, cols].astype(jnp.float32)).astype(jnp.bfloat16)
+                up_out[:, cols] = (back * up_ref[:, cols].astype(jnp.float32)).astype(jnp.bfloat16)
+
+        rows = pl.BlockSpec((OWN, WIDE), lambda i: (i, 0))
         pltpu.emit_pipeline(
             body,
-            grid=(WIDE // 256,),
-            in_specs=[
-                pl.BlockSpec((TREE, D), lambda j: (m, 0)),
-                pl.BlockSpec((256, D), lambda j: (j, 0)),
-                cols,
-                cols,
-            ],
-            out_specs=[cols, cols],
+            grid=(MICRO * TREE // OWN,),
+            in_specs=[rows, pl.BlockSpec((WIDE, D), lambda i: (0, 0)), rows, rows],
+            out_specs=[rows, rows],
         )(cot_full, w_down, gate, up, gate_grad, up_grad)
 
     def grad_weight(near_all, far_all, out, near_cols, far_cols, side=None):
@@ -1368,7 +1500,8 @@
             copies.local(mlp_sum[m].blocks(place.own), mine.at[m], l_sem.at[3 + 2 * m]),
         ]
 
-    r_down.start()
+    r_far.start()
+    r_near.hook(0)
     mlp_sum[0].start()
     mlp_sum[1].start()
     load_gain = copies.local(gain, gain_buf, l_sem.at[0])
@@ -1380,59 +1513,68 @@
         copy.wait()
     mlp_sum[0].middle()
     mlp_sum[1].middle()
-    grad_hidden(0)
-    grad_hidden(1)
-    r_down.middle(2)
+    r_near.hook(1)
+    r_far.hook(0)
+    grad_hidden()
+    grad_weight(ffn_in, gate_grad, gu_grad.at[0], D, WIDE)
+    r_gate.start()
+    r_far.hook(1)
+    r_near.hook(2)
+    r_far.hook(2)
     back_ffn(0)
     ffn_sum[0].start()
-    r_down.middle(1)
+    r_near.hook(3)
+    r_far.hook(3)
     back_ffn(1)
     ffn_sum[1].start()
     ffn_sum[0].middle()
-    grad_weight(ffn_in, gate_grad, gu_grad.at[0], D, WIDE, 1 - place.y)
-    r_gate.start()
+    r_near.cross()
+    r_gate.hook(0)
+    grad_weight(ffn_in, up_grad, gu_grad.at[1], D, WIDE)
+    r_up.start()
     ffn_sum[1].middle()
-    r_down.middle(3)
-    grad_weight(ffn_in, gate_grad, gu_grad.at[0], D, WIDE, place.y)
+    r_gate.hook(1)
+    middle_back(0)
+    r_gate.hook(2)
+    middle_back(1)
     finish_mixed(0)
-    middle_back(0)
-    grad_weight(ffn_in, up_grad, gu_grad.at[1], D, WIDE, 1 - place.y)
-    r_up.start()
-    middle_back(1)
-    r_gate.middle(2)
+    finish_mixed(1)
     a_back[0].relay()
-    grad_weight(ffn_in, up_grad, gu_grad.at[1], D, WIDE, place.y)
-    r_gate.middle(1)
-    finish_mixed(1)
-    a_back[1].relay()
+    r_gate.hook(3)
     a_back[0].finish()
     back_attention(0)
-    r_gate.middle(3)
+    a_back[1].relay()
+    r_up.hook(0)
     sent(ffn_sum[0])
     back_project(0)
     attn_sum[0].start()
     a_back[1].finish()
     grad_weight(heads, out_back, out_grad, 512, D)
     r_out.start()
-    r_up.middle(2)
+    r_up.hook(1)
     back_attention(1)
-    sent(ffn_sum[1])
     attn_sum[0].middle()
+    r_up.hook(2)
     grad_weight(attn_in, proj_grad, qkv_grad, D, 768)
     r_qkv.start()
-    r_up.middle(1)
+    r_up.hook(3)
+    sent(ffn_sum[1])
     back_project(1)
     attn_sum[1].start()
-    r_up.middle(3)
-    r_down.end()
+    r_far.end()
+    r_near.end()
+    r_gate.end()
     attn_sum[1].middle()
-    for off in GradSum.ORDER:
-        r_out.middle(off)
+    r_out.hook(0)
+    r_out.hook(1)
+    r_out.hook(2)
+    r_out.hook(3)
     stores = [finish_tokens(0)]
-    for off in GradSum.ORDER:
-        r_qkv.middle(off)
-    r_gate.end()
+    r_qkv.hook(0)
+    r_qkv.hook(1)
     stores.append(finish_tokens(1))
+    r_qkv.hook(2)
+    r_qkv.hook(3)
     r_up.end()
     r_out.end()
     r_qkv.end()
@@ -1448,7 +1590,8 @@
     wide = jnp.float32
     shape = jax.ShapeDtypeStruct
     all_tokens = MICRO * TREE
-    blocks = [(OWN, 768), (512, OWN), (OWN, WIDE), (OWN, WIDE), (WIDE, OWN)]
+    half = (WIDE // 2, OWN)
+    blocks = [(OWN, 768), (512, OWN), (OWN, WIDE), (OWN, WIDE), half, half]
     outs = [shape((MICRO, OWN, D), low), shape((MICRO, OWN, D), wide)]
     outs += [shape(block, wide) for block in ((OWN, 768), (512, OWN), (2, OWN, WIDE), (WIDE, OWN))]
     outs += [shape((8, D), wide)]
@@ -1457,8 +1600,10 @@
         shape((all_tokens, 768), low),
         shape((2, D, WIDE), low), shape((512, D), low), shape((D, 768), low),
     ]
-    outs += [shape((NZ,) + block, low) for block in blocks]
-    outs += [shape((NZ - 1,) + block, low) for block in blocks]
+    outs += [shape((NZ,) + block, low) for block in blocks[:5]]
+    outs += [shape((1,) + blocks[5], low)]
+    outs += [shape((NZ + 1,) + block, low) for block in blocks[:5]]
+    outs += [shape((NZ + 1, WIDE // 2, NY * OWN), low)]
     dma = pltpu.SemaphoreType.DMA
     args = (*saved, tokens, cot, gains, *tables)
     return pl.pallas_call(
@@ -1486,7 +1631,7 @@
             pltpu.VMEM((3, 8, D), wide),
             pltpu.VMEM((NZ, 8, D), wide),
             pltpu.VMEM((8, D), wide),
-            dma((5, NZ)), dma((5, NZ)), dma((5, NZ)), dma((5, NZ)),
+            dma((6, NZ)), dma((6, NZ)), dma((6, 3, 2)), dma((6, NZ + 1, 2)),
             dma((MICRO, 3)), dma((MICRO, NX * NC)), dma((MICRO,)),
             dma((3, MICRO, 3)), dma((3, MICRO, 3)), dma((6,)), dma((6,)), dma((3 + NZ,)),
         ],

time: 862 us -> 836 us (0.970)
  Pallas kernels: 831 us -> 806 us
    pallas_call x1, Pallas kernels: 410 us -> 385 us  [backward(): pl.pallas_call(backward_kernel, out_shape=outs, in_specs=[HBM] * len(args...]
where the time goes in v4:
time: 836 us; the launch traced here: 833 us
  Pallas kernels  806 us (96%)
  local copies, waits for them, and re-layouts  14.8 us (2%)
  other arithmetic  10.8 us (1%)
    pallas_call x1, Pallas kernels, forward(): pl.pallas_call(forward_kernel, out_shape=outs, in_specs=[HBM] * 12, out_s...  388 us
    pallas_call x1, Pallas kernels, backward(): pl.pallas_call(backward_kernel, out_shape=outs, in_specs=[HBM] * len(args...  385 us
    pallas_call x1, Pallas kernels, update(): pl.pallas_call(update_kernel, out_shape=outs, in_specs=[HBM] * 12 + [whol...  32.5 us

profile of v4, /device:TPU:0, one launch (start us, length us, event | category | flops | bytes accessed | tf_op | source)
XLA Modules:
  0.0 832.7 jit_solution(8012298848192818365)
XLA Ops:
  0.7 0.8 broadcast_add_fusion.1
  1.4 0.1 concatenate.56
  1.5 0.1 concatenate.57
  1.6 0.8 slice_bitcast_fusion.1
  2.3 0.8 slice_convert_fusion.1
  3.1 0.1 convert_reduce_fusion
  3.2 0.1 convert_reduce_fusion.1
  3.4 0.2 reduce-window.16
  3.6 0.1 slice.32
  3.7 0.1 select_reduce_fusion.5
  3.8 0.2 reduce-window.17
  4.0 0.1 slice.36
  4.1 0.1 select_reduce_fusion.4
  4.2 0.1 fusion.3
  4.3 0.1 select_reduce_fusion
  4.5 0.1 select_reduce_fusion.1
  4.6 0.6 pad_maximum_fusion.seg_row
  5.3 2.1 copy.35
  7.3 1.3 broadcast.50.parent_col
  8.6 1.3 broadcast.49.seg_col
  9.9 3.7 fusion
  13.7 1.9 maximum_maximum_fusion.1.sines
  15.5 1.8 maximum_maximum_fusion.cosines
  17.4 388.4 %forward.1 = (bf16[2048,768]{1,0:T(8,128)(2,1)}, bf16[512,2048]{1,0:T(8,128)(2,1)}, bf16[2,2048,2048]{2,1,0:T(8,128)(2,1)}, bf16[2048,2048]{1,0:T(8,128)(2,1)}, ...) custom-call(bf16[2,256,2048]{2,1,0:T(8,128)(2,1)} %tokens.3, ...), custom_call_target="tpu_custom_call" | custom-call | flops 89999998976 | bytes 200000000 | tf_op jit(solution)/shard_map/forward/pallas_call | solution.py:1067
  405.8 385.2 %backward.1 = (bf16[2,256,2048]{2,1,0:T(8,128)(2,1)}, f32[2,256,2048]{2,1,0:T(8,128)}, f32[256,768]{1,0:T(8,128)}, f32[512,256]{1,0:T(8,128)}, f32[2,256,2048]{2...) custom-call(bf16[2048,768]{1,0:T(8,128)(2,1)} %get-tuple-element.54., ...), custom_call_target="tpu_custom_call", output_to_operand_aliasing={{7}: (11, {}), {8}: (12, {})} | custom-call | flops 140000002048 | bytes 500000000 | tf_op jit(solution)/shard_map/backward/pallas_call | solution.py:1609
  791.0 1.2 slice.37
  792.2 2.4 reshape.204.g_qkv
  794.7 32.5 %update.1 = (f32[256,2,384]{2,1,0:T(2,128)}, f32[512,256]{1,0:T(8,128)}, f32[512,2048]{1,0:T(8,128)}, f32[2048,256]{1,0:T(8,128)}, f32[2,256,2,384]{3,2,1,0:T(2,...) custom-call(f32[256,2,384]{2,1,0:T(2,128)} %reshape.204.g_qkv, ...), custom_call_target="tpu_custom_call" | custom-call | flops 60000000 | bytes 58000000 | tf_op jit(solution)/shard_map/update/pallas_call | solution.py:1696
  827.2 0.0 copy-start
  827.2 3.3 copy.40
  830.5 0.0 copy-done
  830.5 2.0 copy.41
  (15 shorter events, 0.2 us)
Async XLA Ops:
  827.2 3.3 copy-start

commit v5 on v4

--- a/solution.py
+++ b/solution.py
@@ -890,13 +890,28 @@
         a_ffn[m].start(normed_buf.at[m], t_keep.at[4 + m])
         return copies.local(resid_buf.at[m], resid.at[m], l_sem.at[m])
 
-    def gate_up(m):
-        def body(a_ref, g_ref, u_ref, gate_ref, up_ref, hidden_ref):
+    def project_gate(m):
+        def body(a_ref, g_ref, gate_ref):
             for part in range(TREE // OWN):
                 rows = slice(part * OWN, (part + 1) * OWN)
-                value = a_ref[rows, :]
-                g = dot_nn(value, g_ref[0])
-                u = dot_nn(value, u_ref[0])
+                gate_ref[rows, :] = dot_nn(a_ref[rows, :], g_ref[0]).astype(jnp.bfloat16)
+
+        pltpu.emit_pipeline(
+            body,
+            grid=(WIDE // 256,),
+            in_specs=[
+                pl.BlockSpec((TREE, D), lambda j: (m, 0)),
+                pl.BlockSpec((1, D, 256), lambda j: (0, 0, j)),
+            ],
+            out_specs=[pl.BlockSpec((TREE, 256), lambda j: (m, j))],
+        )(ffn_in, w_gu, gate)
+
+    def project_up(m):
+        def body(a_ref, u_ref, g_ref, gate_ref, up_ref, hidden_ref):
+            for part in range(TREE // OWN):
+                rows = slice(part * OWN, (part + 1) * OWN)
+                u = dot_nn(a_ref[rows, :], u_ref[0])
+                g = g_ref[rows, :].astype(jnp.float32)
                 act = jax.nn.sigmoid(g)
                 silu = g * act
                 gate_ref[rows, :] = (u * act * (1.0 + g * (1.0 - act))).astype(jnp.bfloat16)
@@ -909,11 +924,11 @@
             grid=(WIDE // 256,),
             in_specs=[
                 pl.BlockSpec((TREE, D), lambda j: (m, 0)),
-                pl.BlockSpec((1, D, 256), lambda j: (0, 0, j)),
                 pl.BlockSpec((1, D, 256), lambda j: (1, 0, j)),
+                cols,
             ],
             out_specs=[cols, cols, cols],
-        )(ffn_in, w_gu, w_gu, gate, up, hidden)
+        )(ffn_in, w_gu, gate, gate, up, hidden)
 
     def grad_down():
         def body(h_ref, c_ref, out_ref):
@@ -1007,18 +1022,20 @@
     a_ffn[0].relay()
     g_up.relay(2)
     g_down.start_z()
+    g_gate.finish()
+    a_ffn[0].finish()
+    project_gate(0)
     a_ffn[1].relay()
     g_up.relay(3)
     g_down.relay(1)
+    a_ffn[1].finish()
+    project_gate(1)
     a_cot[0].finish()
     a_cot[1].finish()
-    a_ffn[0].finish()
-    g_gate.finish()
     g_up.finish()
-    gate_up(0)
+    project_up(0)
     g_down.relay(2)
-    a_ffn[1].finish()
-    gate_up(1)
+    project_up(1)
     g_down.relay(3)
     g_down.keep_own()
     down(0, True)

time: 836 us -> 824 us (0.986)
  Pallas kernels: 806 us -> 793 us
    pallas_call x1, Pallas kernels: 388 us -> 376 us  [forward(): pl.pallas_call(forward_kernel, out_shape=outs, in_specs=[HBM] * 12, out_s...]
where the time goes in v5:
time: 824 us; the launch traced here: 820 us
  Pallas kernels  793 us (96%)
  local copies, waits for them, and re-layouts  14.8 us (2%)
  other arithmetic  10.8 us (1%)
    pallas_call x1, Pallas kernels, backward(): pl.pallas_call(backward_kernel, out_shape=outs, in_specs=[HBM] * len(args...  385 us
    pallas_call x1, Pallas kernels, forward(): pl.pallas_call(forward_kernel, out_shape=outs, in_specs=[HBM] * 12, out_s...  376 us
    pallas_call x1, Pallas kernels, update(): pl.pallas_call(update_kernel, out_shape=outs, in_specs=[HBM] * 12 + [whol...  32.5 us

profile of v5, /device:TPU:0, one launch (start us, length us, event | category | flops | bytes accessed | tf_op | source)
XLA Modules:
  0.0 819.8 jit_solution(296772425445021152)
XLA Ops:
  0.7 0.8 broadcast_add_fusion.1
  1.4 0.1 concatenate.56
  1.5 0.1 concatenate.57
  1.6 0.8 slice_bitcast_fusion.1
  2.3 0.8 slice_convert_fusion.1
  3.1 0.1 convert_reduce_fusion
  3.2 0.1 convert_reduce_fusion.1
  3.4 0.2 reduce-window.16
  3.6 0.1 slice.32
  3.7 0.1 select_reduce_fusion.5
  3.8 0.2 reduce-window.17
  4.0 0.1 slice.36
  4.1 0.1 select_reduce_fusion.4
  4.2 0.1 fusion.3
  4.3 0.1 select_reduce_fusion
  4.5 0.1 select_reduce_fusion.1
  4.6 0.6 pad_maximum_fusion.seg_row
  5.3 2.1 copy.35
  7.3 1.3 broadcast.50.parent_col
  8.6 1.3 broadcast.49.seg_col
  9.9 3.7 fusion
  13.7 1.9 maximum_maximum_fusion.1.sines
  15.5 1.8 maximum_maximum_fusion.cosines
  17.4 375.6 %forward.1 = (bf16[2048,768]{1,0:T(8,128)(2,1)}, bf16[512,2048]{1,0:T(8,128)(2,1)}, bf16[2,2048,2048]{2,1,0:T(8,128)(2,1)}, bf16[2048,2048]{1,0:T(8,128)(2,1)}, ...) custom-call(bf16[2,256,2048]{2,1,0:T(8,128)(2,1)} %tokens.3, ...), custom_call_target="tpu_custom_call" | custom-call | flops 89999998976 | bytes 200000000 | tf_op jit(solution)/shard_map/forward/pallas_call | solution.py:1084
  393.0 385.2 %backward.1 = (bf16[2,256,2048]{2,1,0:T(8,128)(2,1)}, f32[2,256,2048]{2,1,0:T(8,128)}, f32[256,768]{1,0:T(8,128)}, f32[512,256]{1,0:T(8,128)}, f32[2,256,2048]{2...) custom-call(bf16[2048,768]{1,0:T(8,128)(2,1)} %get-tuple-element.54., ...), custom_call_target="tpu_custom_call", output_to_operand_aliasing={{7}: (11, {}), {8}: (12, {})} | custom-call | flops 140000002048 | bytes 500000000 | tf_op jit(solution)/shard_map/backward/pallas_call | solution.py:1626
  778.1 1.2 slice.37
  779.3 2.4 reshape.204.g_qkv
  781.7 32.5 %update.1 = (f32[256,2,384]{2,1,0:T(2,128)}, f32[512,256]{1,0:T(8,128)}, f32[512,2048]{1,0:T(8,128)}, f32[2048,256]{1,0:T(8,128)}, f32[2,256,2,384]{3,2,1,0:T(2,...) custom-call(f32[256,2,384]{2,1,0:T(2,128)} %reshape.204.g_qkv, ...), custom_call_target="tpu_custom_call" | custom-call | flops 60000000 | bytes 58000000 | tf_op jit(solution)/shard_map/update/pallas_call | solution.py:1713
  814.2 0.0 copy-start
  814.2 3.3 copy.40
  817.6 0.0 copy-done
  817.6 2.0 copy.41
  (15 shorter events, 0.2 us)
Async XLA Ops:
  814.2 3.3 copy-start
